TPU v7x, 128 devices: a whole 4x4x4 slice. The times are simulated.
128 devices in a mesh: blk: 32 (over x, z, core), head: 4 (over y).
Axes of the slice: x: 4, y: 4, z: 4, core: 2. Of those that a mesh axis runs over, the one named last changes fastest.
Arguments:
- tokens_in: bfloat16 [2, 16384, 1024], P(None, ('blk', 'head')), may hold values from -6 to 6
- grad_out: bfloat16 [2, 16384, 1024], P(None, ('blk', 'head')), may hold values from -6 to 6
- flags: int32 [2, 32], P(None, 'blk'), may hold values from 0 to 1, as said below
- attn_gain: float32 [1024], replicated, may hold values from 0.1 to 1.9
- mlp_gain: float32 [1024], replicated, may hold values from 0.1 to 1.9
- w_qkv: bfloat16 [1024, 3, 1024], P(None, None, 'head'), may hold values from -0.1875 to 0.1875
- w_out: bfloat16 [1024, 1024], P('head'), may hold values from -0.75 to 0.75
- rel_bias: float32 [32, 8], P(None, 'head'), may hold values from -4 to 4
- state_query: bfloat16 [512, 1024], P(None, 'head'), may hold values from -5 to 5
- state_proj: bfloat16 [8, 128, 256], P('head'), may hold values from -0.5 to 0.5
- forget_bias: float32 [1024], P('head'), may hold values from -2 to 5
- forget_scale: float32 [1024], P('head'), may hold values from -6 to 6
- w_up: bfloat16 [1024, 4096], P(None, 'head'), may hold values from -0.1875 to 0.1875
- w_down: bfloat16 [4096, 1024], P('head'), may hold values from -0.09375 to 0.09375
Outputs:
- out_tokens: float32 [2, 16384, 1024], P(None, ('blk', 'head'))
- grad_tokens: float32 [2, 16384, 1024], P(None, ('blk', 'head'))
- block_states: float32 [2, 32, 512, 1024], P(None, 'blk', None, 'head')
- grad_attn_gain: float32 [1024], replicated
- grad_mlp_gain: float32 [1024], replicated
- grad_qkv: float32 [1024, 3, 1024], P(None, None, 'head')
- grad_out_proj: float32 [1024, 1024], P('head')
- grad_rel_bias: float32 [32, 8], P(None, 'head')
- grad_state_query: float32 [512, 1024], P(None, 'head')
- grad_state_proj: float32 [8, 128, 256], P('head')
- grad_forget_bias: float32 [1024], P('head')
- grad_forget_scale: float32 [1024], P('head')
- grad_up: float32 [1024, 4096], P(None, 'head')
- grad_down: float32 [4096, 1024], P('head')
Inputs may be any that keep to these rules, and one draw needn't show every extreme that they name: flags[m, 0] is 1 for every micro-batch; in one micro-batch drawn from the seed every other entry is 0.
All inputs are finite; a program needn't handle non-finite values.
Results may differ from a plain program's by a relative error of at most 0.025.
Values may be sent and summed in bfloat16 or wider, within the bound.
A program may use at most 256 MiB of HBM per device.

v0:
```python
import math

import jax
import jax.numpy as jnp
from jax import lax
from jax.sharding import PartitionSpec as P

BUCKETS = 32
MAXDIST = 128


EPSILON = 1e-06
MASKED = -1e30


def shifted(block, axis, distance):
    devices = range(lax.axis_size(axis))
    route = [(i - distance, i) for i in devices if i - distance in devices]
    return lax.ppermute(block, axis, route)


def carried_in(shard, axis, combine, identity):
    size, place = (lax.axis_size(axis), lax.axis_index(axis))
    everything = jax.tree.map(lambda part: lax.all_gather(part, axis), shard)
    start = jax.tree.map(
        lambda part, zero: jnp.broadcast_to(jnp.asarray(zero, part.dtype), part.shape),
        shard,
        identity,
    )

    def turn(k, before):
        reached = k < place
        new = combine(before, jax.tree.map(lambda part: part[k], everything))
        return jax.tree.map(lambda a, b: jnp.where(reached, a, b), new, before)

    return lax.fori_loop(0, size, turn, start)


def entering(shard, axis, join, neutral):
    count = lax.axis_size(axis)
    place = lax.axis_index(axis)
    ahead = count - 1 - place
    gathered = jax.tree.map(
        lambda a, kind: lax.all_gather(a.astype(kind), axis), shard, (jnp.bfloat16, jnp.bfloat16)
    )
    state = jax.tree.map(lambda a, e: jnp.zeros_like(a) + jnp.asarray(e, a.dtype), shard, neutral)

    def one(turn, state):
        source = count - 1 - turn
        return join(
            state,
            jax.tree.map(
                lambda a, own: lax.dynamic_index_in_dim(a, source, 0, False).astype(own.dtype),
                gathered,
                shard,
            ),
        )

    return lax.fori_loop(0, ahead, one, state)


def bucket_index(distance):
    exact_part = BUCKETS // 2
    result = jnp.minimum(distance, exact_part)
    for level in range(1, BUCKETS - exact_part):
        boundary = int(
            math.ceil(exact_part * (MAXDIST / exact_part) ** (level / (BUCKETS - exact_part)))
        )
        result = result + (distance >= boundary).astype(jnp.int32)
    return result


def window_layout(length):
    query_pos = lax.broadcasted_iota(jnp.int32, (length, 2 * length), 0)
    key_pos = lax.broadcasted_iota(jnp.int32, (length, 2 * length), 1)
    distance = query_pos + length - key_pos
    inside = (distance >= 0) & (distance < length)
    earlier = key_pos < length
    return (bucket_index(jnp.maximum(distance, 0)), inside, earlier)


def rms_norm(values, gain):
    return values * lax.rsqrt(jnp.mean(values * values, axis=-1, keepdims=True) + EPSILON) * gain


def chain_combine(earlier, later):
    return (earlier[0] * later[0], later[0] * earlier[1] + later[1])


def gather_rows(values):
    return lax.all_gather(values, "head", axis=0, tiled=True)


def reduce_rows(term, rows):
    return lax.psum_scatter(
        term(jnp.int32(0), rows * lax.axis_size("head")), "head", scatter_dimension=0, tiled=True
    )


def gather_grads(values):
    return lax.all_gather(values, "head", axis=0, tiled=True)


def reduce_grads(term, rows):
    return lax.psum_scatter(
        term(jnp.int32(0), lax.axis_size("head") * rows).astype(jnp.bfloat16),
        "head",
        scatter_dimension=0,
        tiled=True,
    ).astype(jnp.float32)


def row_product(left, right):

    def term(start, count):
        return jnp.dot(left, right, preferred_element_type=jnp.float32)

    return term


def row_product_back(left, right):

    def term(start, count):
        return jnp.einsum("ie,de->id", left, right, preferred_element_type=jnp.float32)

    return term


def body(
    tokens_in,
    grad_out,
    flags,
    attn_gain,
    mlp_gain,
    w_qkv,
    w_out,
    rel_bias,
    state_query,
    state_proj,
    forget_bias,
    forget_scale,
    w_up,
    w_down,
):
    rows = tokens_in.shape[1]
    width = tokens_in.shape[2]
    block = rows * lax.axis_size("head")
    local_width = w_qkv.shape[2]
    heads = rel_bias.shape[1]
    head_size = local_width // heads
    states_count = state_query.shape[0]
    buckets = rel_bias.shape[0]
    scale = head_size ** (-0.5)
    qkv_flat = w_qkv.reshape(width, 3 * local_width)
    query_heads = state_query.reshape(states_count, heads, head_size)
    bucket, inside, earlier = window_layout(block)
    bias_table = jnp.zeros((heads, block, 2 * block), jnp.float32)
    for level in range(buckets):
        bias_table = bias_table + jnp.where(
            (bucket == level)[None], rel_bias[level][:, None, None], 0.0
        )

    def scores_of(queries, all_keys, state_keys, flag):
        usable = inside & (jnp.logical_not(earlier) | (flag[0] == 0))
        token_scores = (
            jnp.einsum("ihd,jhd->hij", queries, all_keys, preferred_element_type=jnp.float32)
            * scale
            + bias_table
        )
        token_scores = jnp.where(usable[None], token_scores, MASKED)
        state_scores = (
            jnp.einsum("ihd,shd->his", queries, state_keys, preferred_element_type=jnp.float32)
            * scale
        )
        return (token_scores, state_scores)

    def forward(x_low, flag):
        rows_full = x_low.astype(jnp.float32)
        keep = (1 - flag[0]).astype(jnp.float32)
        normed = rms_norm(rows_full, attn_gain).astype(jnp.bfloat16)
        whole = gather_rows(normed)
        mixed = (
            jnp.dot(whole, qkv_flat, preferred_element_type=jnp.float32)
            .astype(jnp.bfloat16)
            .reshape(block, 3, heads, head_size)
        )
        queries = mixed[:, 0]
        keys = mixed[:, 1]
        values = mixed[:, 2]
        earlier_kv = shifted(mixed[:, 1:], "blk", 1)
        update_scores = (
            jnp.einsum("shd,jhd->hsj", query_heads, keys, preferred_element_type=jnp.float32)
            * scale
        )
        update_top = jnp.max(update_scores, axis=-1, keepdims=True)
        update_exp = jnp.exp(update_scores - update_top)
        update_total = jnp.sum(update_exp, axis=-1, keepdims=True)
        update_lse = update_top + jnp.log(update_total)
        update_weights = (update_exp / update_total).astype(jnp.bfloat16)
        update = jnp.einsum(
            "hsj,jhd->shd", update_weights, values, preferred_element_type=jnp.float32
        )
        unit = (
            update * lax.rsqrt(jnp.mean(update * update, axis=-1, keepdims=True) + EPSILON)
        ).reshape(states_count, local_width)
        forget = jax.nn.sigmoid(forget_bias + forget_scale * unit)
        factor = keep * forget
        addend = (1.0 - forget) * unit
        ignored, state_before = carried_in(
            (factor, addend), "blk", chain_combine, (jnp.ones_like(factor), jnp.zeros_like(addend))
        )
        prior = keep * state_before
        state_after = forget * prior + addend
        state_low = prior.astype(jnp.bfloat16).reshape(states_count, heads, head_size)
        state_kv = jnp.einsum(
            "shd,hde->she", state_low, state_proj, preferred_element_type=jnp.float32
        ).astype(jnp.bfloat16)
        all_keys = jnp.concatenate([earlier_kv[:, 0], keys], 0)
        all_values = jnp.concatenate([earlier_kv[:, 1], values], 0)
        token_scores, state_scores = scores_of(queries, all_keys, state_kv[..., :head_size], flag)
        highest = jnp.maximum(
            jnp.max(token_scores, axis=-1, keepdims=True),
            jnp.max(state_scores, axis=-1, keepdims=True),
        )
        token_exp = jnp.exp(token_scores - highest)
        state_exp = jnp.exp(state_scores - highest)
        total = jnp.sum(token_exp, axis=-1, keepdims=True) + jnp.sum(
            state_exp, axis=-1, keepdims=True
        )
        lse = highest + jnp.log(total)
        attended = jnp.einsum(
            "hij,jhd->ihd",
            (token_exp / total).astype(jnp.bfloat16),
            all_values,
            preferred_element_type=jnp.float32,
        )
        attended = attended + jnp.einsum(
            "his,shd->ihd",
            (state_exp / total).astype(jnp.bfloat16),
            state_kv[..., head_size:],
            preferred_element_type=jnp.float32,
        )
        attended = attended.astype(jnp.bfloat16).reshape(block, local_width)
        branch = reduce_rows(row_product(attended, w_out), rows)
        middle = rows_full + branch
        normed_mlp = rms_norm(middle, mlp_gain).astype(jnp.bfloat16)
        whole_mlp = gather_rows(normed_mlp)
        hidden = jnp.dot(whole_mlp, w_up, preferred_element_type=jnp.float32)
        active = jax.nn.gelu(hidden).astype(jnp.bfloat16)
        branch_mlp = reduce_rows(row_product(active, w_down), rows)
        output = middle + branch_mlp
        saved = (
            whole,
            mixed,
            earlier_kv,
            update_lse,
            update,
            forget,
            prior,
            state_kv,
            lse,
            attended,
            middle,
            whole_mlp,
            hidden,
            active,
        )
        return (output, state_after, saved)

    def forward_micro(carry, inputs):
        x_low, flag = inputs
        output, state_after, saved = forward(x_low, flag)
        return (carry, (output, state_after, saved))

    ignored, (outputs, states, kept) = lax.scan(
        forward_micro, jnp.zeros((), jnp.float32), (tokens_in, flags)
    )

    def mlp_back(carry, inputs):
        g_up, g_down, g_mlp_gain = carry
        cotangent, saved = inputs
        middle, whole_mlp, hidden, active = (saved[10], saved[11], saved[12], saved[13])
        grad_whole = gather_grads(cotangent)
        g_down = g_down + jnp.einsum(
            "if,id->fd", active, grad_whole, preferred_element_type=jnp.float32
        )
        grad_active = jnp.einsum(
            "id,fd->if", grad_whole, w_down, preferred_element_type=jnp.float32
        )
        unused, gelu_pull = jax.vjp(jax.nn.gelu, hidden)
        grad_hidden = gelu_pull(grad_active)[0].astype(jnp.bfloat16)
        g_up = g_up + jnp.einsum(
            "id,if->df", whole_mlp, grad_hidden, preferred_element_type=jnp.float32
        )
        grad_normed = reduce_grads(row_product_back(grad_hidden, w_up), rows)
        unused, norm_pull = jax.vjp(rms_norm, middle, mlp_gain)
        grad_middle_part, grad_gain = norm_pull(grad_normed)
        grad_middle = cotangent.astype(jnp.float32) + grad_middle_part
        return ((g_up, g_down, g_mlp_gain + grad_gain), grad_middle)

    mlp_start = (
        jnp.zeros(w_up.shape, jnp.float32),
        jnp.zeros(w_down.shape, jnp.float32),
        jnp.zeros(mlp_gain.shape, jnp.float32),
    )
    (g_up, g_down, g_mlp_gain), grad_middles = lax.scan(mlp_back, mlp_start, (grad_out, kept))

    def attn_back(carry, inputs):
        g_qkv, g_out, bias_acc, g_query, g_proj, g_bias, g_scale, g_attn_gain = carry
        grad_middle, saved, flag, x_low = inputs
        whole, mixed, earlier_kv, update_lse, update, forget, prior, state_kv, lse, attended = (
            saved[:10]
        )
        keep = (1 - flag[0]).astype(jnp.float32)
        queries = mixed[:, 0]
        keys = mixed[:, 1]
        values = mixed[:, 2]
        all_keys = jnp.concatenate([earlier_kv[:, 0], keys], 0)
        all_values = jnp.concatenate([earlier_kv[:, 1], values], 0)
        state_keys = state_kv[..., :head_size]
        state_values = state_kv[..., head_size:]
        grad_whole = gather_grads(grad_middle.astype(jnp.bfloat16))
        g_out = g_out + jnp.einsum(
            "ie,id->ed", attended, grad_whole, preferred_element_type=jnp.float32
        )
        grad_att = (
            jnp.einsum("id,ed->ie", grad_whole, w_out, preferred_element_type=jnp.float32)
            .astype(jnp.bfloat16)
            .reshape(block, heads, head_size)
        )
        token_scores, state_scores = scores_of(queries, all_keys, state_keys, flag)
        token_probs = jnp.exp(token_scores - lse)
        state_probs = jnp.exp(state_scores - lse)
        grad_token_probs = jnp.einsum(
            "ihd,jhd->hij", grad_att, all_values, preferred_element_type=jnp.float32
        )
        grad_state_probs = jnp.einsum(
            "ihd,shd->his", grad_att, state_values, preferred_element_type=jnp.float32
        )
        delta = jnp.sum(token_probs * grad_token_probs, axis=-1, keepdims=True) + jnp.sum(
            state_probs * grad_state_probs, axis=-1, keepdims=True
        )
        grad_token_scores = token_probs * (grad_token_probs - delta)
        grad_state_scores = state_probs * (grad_state_probs - delta)
        bias_acc = bias_acc + grad_token_scores
        token_low = grad_token_scores.astype(jnp.bfloat16)
        state_grad_low = grad_state_scores.astype(jnp.bfloat16)
        grad_values_all = jnp.einsum(
            "hij,ihd->jhd",
            token_probs.astype(jnp.bfloat16),
            grad_att,
            preferred_element_type=jnp.float32,
        )
        grad_state_values = jnp.einsum(
            "his,ihd->shd",
            state_probs.astype(jnp.bfloat16),
            grad_att,
            preferred_element_type=jnp.float32,
        )
        grad_queries = scale * (
            jnp.einsum("hij,jhd->ihd", token_low, all_keys, preferred_element_type=jnp.float32)
            + jnp.einsum(
                "his,shd->ihd", state_grad_low, state_keys, preferred_element_type=jnp.float32
            )
        )
        grad_keys_all = scale * jnp.einsum(
            "hij,ihd->jhd", token_low, queries, preferred_element_type=jnp.float32
        )
        grad_state_keys = scale * jnp.einsum(
            "his,ihd->shd", state_grad_low, queries, preferred_element_type=jnp.float32
        )
        earlier_grads = jnp.stack([grad_keys_all[:block], grad_values_all[:block]], 1)
        later_grads = shifted(earlier_grads.astype(jnp.bfloat16), "blk", -1).astype(
            earlier_grads.dtype
        )
        grad_state_kv = jnp.concatenate([grad_state_keys, grad_state_values], -1).astype(
            jnp.bfloat16
        )
        state_low = prior.astype(jnp.bfloat16).reshape(states_count, heads, head_size)
        g_proj = g_proj + jnp.einsum(
            "shd,she->hde", state_low, grad_state_kv, preferred_element_type=jnp.float32
        )
        grad_prior = jnp.einsum(
            "she,hde->shd", grad_state_kv, state_proj, preferred_element_type=jnp.float32
        ).reshape(states_count, local_width)
        ignored_part, grad_after = entering(
            (keep * forget, keep * grad_prior),
            "blk",
            chain_combine,
            (jnp.ones_like(forget), jnp.zeros_like(grad_prior)),
        )

        def state_rule(update_values, bias_values, scale_values):
            unit_values = update_values * lax.rsqrt(
                jnp.mean(update_values * update_values, axis=-1, keepdims=True) + EPSILON
            )
            unit_values = unit_values.reshape(states_count, local_width)
            gate = jax.nn.sigmoid(bias_values + scale_values * unit_values)
            return gate * prior + (1.0 - gate) * unit_values

        unused, state_pull = jax.vjp(state_rule, update, forget_bias, forget_scale)
        grad_update, grad_bias, grad_scale = state_pull(grad_after)
        grad_update_low = grad_update.astype(jnp.bfloat16)
        update_scores = (
            jnp.einsum("shd,jhd->hsj", query_heads, keys, preferred_element_type=jnp.float32)
            * scale
        )
        update_probs = jnp.exp(update_scores - update_lse)
        grad_update_probs = jnp.einsum(
            "shd,jhd->hsj", grad_update_low, values, preferred_element_type=jnp.float32
        )
        update_delta = jnp.sum(update_probs * grad_update_probs, axis=-1, keepdims=True)
        grad_update_scores = (update_probs * (grad_update_probs - update_delta)).astype(
            jnp.bfloat16
        )
        grad_values_update = jnp.einsum(
            "hsj,shd->jhd",
            update_probs.astype(jnp.bfloat16),
            grad_update_low,
            preferred_element_type=jnp.float32,
        )
        g_query = g_query + scale * jnp.einsum(
            "hsj,jhd->shd", grad_update_scores, keys, preferred_element_type=jnp.float32
        ).reshape(states_count, local_width)
        grad_keys_update = scale * jnp.einsum(
            "hsj,shd->jhd", grad_update_scores, query_heads, preferred_element_type=jnp.float32
        )
        grad_keys = grad_keys_all[block:] + later_grads[:, 0] + grad_keys_update
        grad_values = grad_values_all[block:] + later_grads[:, 1] + grad_values_update
        grad_mixed = (
            jnp.stack([grad_queries, grad_keys, grad_values], 1)
            .astype(jnp.bfloat16)
            .reshape(block, 3 * local_width)
        )
        g_qkv = g_qkv + jnp.einsum(
            "id,ie->de", whole, grad_mixed, preferred_element_type=jnp.float32
        ).reshape(width, 3, local_width)
        grad_normed = reduce_grads(row_product_back(grad_mixed, qkv_flat), rows)
        unused_norm, norm_pull = jax.vjp(rms_norm, x_low.astype(jnp.float32), attn_gain)
        grad_x_part, grad_gain = norm_pull(grad_normed)
        grad_x = grad_middle + grad_x_part
        carry = (
            g_qkv,
            g_out,
            bias_acc,
            g_query,
            g_proj,
            g_bias + grad_bias,
            g_scale + grad_scale,
            g_attn_gain + grad_gain,
        )
        return (carry, grad_x)

    attn_start = (
        jnp.zeros(w_qkv.shape, jnp.float32),
        jnp.zeros(w_out.shape, jnp.float32),
        jnp.zeros((heads, block, 2 * block), jnp.float32),
        jnp.zeros(state_query.shape, jnp.float32),
        jnp.zeros(state_proj.shape, jnp.float32),
        jnp.zeros(forget_bias.shape, jnp.float32),
        jnp.zeros(forget_scale.shape, jnp.float32),
        jnp.zeros(attn_gain.shape, jnp.float32),
    )
    (g_qkv, g_out, bias_acc, g_query, g_proj, g_bias, g_scale, g_attn_gain), grad_rows = lax.scan(
        attn_back, attn_start, (grad_middles, kept, flags, tokens_in)
    )
    g_rel = jnp.stack(
        [
            jnp.sum(jnp.where((bucket == level)[None], bias_acc, 0.0), axis=(1, 2))
            for level in range(buckets)
        ],
        0,
    )
    g_attn_gain, g_mlp_gain = lax.psum((g_attn_gain, g_mlp_gain), ("blk", "head"))
    g_qkv, g_out, g_rel, g_query, g_proj, g_bias, g_scale, g_up, g_down = (
        lax.psum(g_qkv.astype(jnp.bfloat16), "blk").astype(jnp.float32),
        lax.psum(g_out.astype(jnp.bfloat16), "blk").astype(jnp.float32),
        lax.psum(g_rel.astype(jnp.bfloat16), "blk").astype(jnp.float32),
        lax.psum(g_query.astype(jnp.bfloat16), "blk").astype(jnp.float32),
        lax.psum(g_proj.astype(jnp.bfloat16), "blk").astype(jnp.float32),
        lax.psum(g_bias.astype(jnp.bfloat16), "blk").astype(jnp.float32),
        lax.psum(g_scale.astype(jnp.bfloat16), "blk").astype(jnp.float32),
        lax.psum(g_up.astype(jnp.bfloat16), "blk").astype(jnp.float32),
        lax.psum(g_down.astype(jnp.bfloat16), "blk").astype(jnp.float32),
    )
    return (
        outputs,
        grad_rows,
        states[:, None],
        g_attn_gain,
        g_mlp_gain,
        g_qkv,
        g_out,
        g_rel,
        g_query,
        g_proj,
        g_bias,
        g_scale,
        g_up,
        g_down,
    )


def solution(mesh):
    return jax.shard_map(
        body,
        mesh=mesh,
        in_specs=(
            P(None, ("blk", "head"), None),
            P(None, ("blk", "head"), None),
            P(None, "blk"),
            P(),
            P(),
            P(None, None, "head"),
            P("head", None),
            P(None, "head"),
            P(None, "head"),
            P("head", None, None),
            P("head"),
            P("head"),
            P(None, "head"),
            P("head", None),
        ),
        out_specs=(
            P(None, ("blk", "head"), None),
            P(None, ("blk", "head"), None),
            P(None, "blk", None, "head"),
            P(),
            P(),
            P(None, None, "head"),
            P("head", None),
            P(None, "head"),
            P(None, "head"),
            P("head", None, None),
            P("head"),
            P("head"),
            P(None, "head"),
            P("head", None),
        ),
        check_vma=False,
    )
```

profile of v0, /device:TPU:1, one launch (start us, length us, event | category | flops | bytes accessed | tf_op | source)
XLA Modules:
  0.0 1505.2 jit_solution(13966172280272282951)
XLA Ops:
  15.5 16.0 %broadcast_compare_fusion.31 = (pred[512,1024]{1,0:T(8,128)(4,1)}, pred[512,1024]{1,0:T(8,128)(4,1)}, pred[512,1024]{1,0:T(8,128)(4,1)}, pred[512,1024]{1,0:T(8,...) fusion(s32[512]{0:T(512)S(1)} %iota_add_fusion), kind=kLoop, calls=%fused_computation.368 | loop fusion | flops 41943040 | bytes 16779264 | tf_op jit(solution)/shard_map/eq | solution.py:160
  33.7 17.8 %select_add_fusion.8 = f32[2,512,1024]{2,1,0:T(8,128)} fusion(f32[2]{0:T(128)S(1)} %get-tuple-element.1864, f32[2]{0:T(128)S(1)} %get-tuple-element.1865, f32[2]{0:T(128)S(1)} %get-tuple-element.1835, f32[2]{0:T(128)S(1)} %get-tuple-element.1836, f32[2]{0:T(128)S(1)} %get-tuple-element.1837, f32[2]{0:T(128)S(1)} %get-tuple-element.1838, ...), kind=kLoop, calls=%fused_computation.318 | loop fusion | flops 66060288 | bytes 20971776 | tf_op jit(solution)/shard_map/add | solution.py:159
  56.4 689.6 %while.133 = (s32[]{:T(128)}, f32[2,128,1024]{2,1,0:T(8,128)}, f32[2,512,256]{2,1,0:T(8,128)}, bf16[2,512,1024]{2,1,0:T(8,128)(2,1)}, bf16[2,512,3,2,128]{4,3,2,...) while((s32[]{:T(128)}, f32[2,128,1024]{2,1,0:T(8,128)}, ...), condition=%wide.region_14.15_spmd.clone, body=%wide.region_0.14_spmd.clone.sunk | while | flops 4402053120 | bytes 332517280 | solution.py:275
  59.0 26.5 %all-gather.13.cloned.1.call-done = bf16[512,1024]{1,0:T(8,128)(2,1)} async-done(((bf16[128,1024]{1,0:T(8,128)(2,1)}), bf16[512,1024]{1,0:T(8,128)(2,1)}) %all-gather.13.cloned.1.call-update) | async-done | bytes 1048592 | tf_op jit(solution)/shard_map/while/body/eval_jaxpr/all_gather | solution.py:91
  116.1 52.8 %all-gather.15.cloned.1.call-done = f32[32,512,256]{2,1,0:T(8,128)} async-done(((f32[1,512,256]{2,1,0:T(8,128)}), f32[32,512,256]{2,1,0:T(8,128)}) %all-gather.15.cloned.1.call-update) | async-done | bytes 16777232 | tf_op jit(solution)/shard_map/while/body/eval_jaxpr/all_gather | solution.py:24
  168.9 74.3 %all-gather.17.cloned.1.call-done = f32[32,512,256]{2,1,0:T(8,128)} async-done(((f32[1,512,256]{2,1,0:T(8,128)}), f32[32,512,256]{2,1,0:T(8,128)}) %all-gather.17.cloned.1.call-update) | async-done | bytes 16777232 | tf_op jit(solution)/shard_map/while/body/eval_jaxpr/all_gather | solution.py:24
  243.2 53.7 %while.137 = (s32[]{:T(128)}, f32[512,256]{1,0:T(8,128)S(1)}, s32[]{:T(128)}, f32[32,512,256]{2,1,0:T(8,128)}, f32[32,512,256]{2,1,0:T(8,128)}, /*index=5*/s32[]{:T(128)}, s32[]{:T(128)}) while((s32[]{:T(128)}, f32[512,256]{1,0:T(8,128)S(1)}, s32[]{:T(128)}, f32[32,512,256]{2,1,0:T(8,128)}, f32[32,512,256]{2,1,0:T(8,128)}, ...), condition=%wide.region_7.7_spmd.clone, body=%wide.region_6.6_spmd.clone.sunk | while | flops 524292 | bytes 2097261 | solution.py:36
  305.7 28.8 %reduce-scatter.5.cloned.1.call-done = f32[128,1024]{1,0:T(8,128)} async-done(((f32[512,1024]{1,0:T(8,128)}), f32[128,1024]{1,0:T(8,128)}) %reduce-scatter.5.cloned.1.call-update) | async-done | bytes 524304 | tf_op jit(solution)/shard_map/while/body/eval_jaxpr/reduce_scatter | solution.py:95
  337.6 22.8 %all-gather.19.cloned.1.call-done = bf16[512,1024]{1,0:T(8,128)(2,1)} async-done(((bf16[128,1024]{1,0:T(8,128)(2,1)}), bf16[512,1024]{1,0:T(8,128)(2,1)}) %all-gather.19.cloned.1.call-update) | async-done | bytes 1048592 | tf_op jit(solution)/shard_map/while/body/eval_jaxpr/all_gather | solution.py:91
  379.4 21.0 %reduce-scatter.7.cloned.1.call-done = f32[128,1024]{1,0:T(8,128)} async-done(((f32[512,1024]{1,0:T(8,128)}), f32[128,1024]{1,0:T(8,128)}) %reduce-scatter.7.cloned.1.call-update) | async-done | bytes 524304 | tf_op jit(solution)/shard_map/while/body/eval_jaxpr/reduce_scatter | solution.py:95
  405.2 23.0 %all-gather.13.cloned.1.call-done = bf16[512,1024]{1,0:T(8,128)(2,1)} async-done(((bf16[128,1024]{1,0:T(8,128)(2,1)}), bf16[512,1024]{1,0:T(8,128)(2,1)}) %all-gather.13.cloned.1.call-update) | async-done | bytes 1048592 | tf_op jit(solution)/shard_map/while/body/eval_jaxpr/all_gather | solution.py:91
  458.8 52.8 %all-gather.15.cloned.1.call-done = f32[32,512,256]{2,1,0:T(8,128)} async-done(((f32[1,512,256]{2,1,0:T(8,128)}), f32[32,512,256]{2,1,0:T(8,128)}) %all-gather.15.cloned.1.call-update) | async-done | bytes 16777232 | tf_op jit(solution)/shard_map/while/body/eval_jaxpr/all_gather | solution.py:24
  511.6 74.3 %all-gather.17.cloned.1.call-done = f32[32,512,256]{2,1,0:T(8,128)} async-done(((f32[1,512,256]{2,1,0:T(8,128)}), f32[32,512,256]{2,1,0:T(8,128)}) %all-gather.17.cloned.1.call-update) | async-done | bytes 16777232 | tf_op jit(solution)/shard_map/while/body/eval_jaxpr/all_gather | solution.py:24
  585.9 53.7 %while.137 = (s32[]{:T(128)}, f32[512,256]{1,0:T(8,128)S(1)}, s32[]{:T(128)}, f32[32,512,256]{2,1,0:T(8,128)}, f32[32,512,256]{2,1,0:T(8,128)}, /*index=5*/s32[]{:T(128)}, s32[]{:T(128)}) while((s32[]{:T(128)}, f32[512,256]{1,0:T(8,128)S(1)}, s32[]{:T(128)}, f32[32,512,256]{2,1,0:T(8,128)}, f32[32,512,256]{2,1,0:T(8,128)}, ...), condition=%wide.region_7.7_spmd.clone, body=%wide.region_6.6_spmd.clone.sunk | while | flops 524292 | bytes 2097261 | solution.py:36
  648.4 28.8 %reduce-scatter.5.cloned.1.call-done = f32[128,1024]{1,0:T(8,128)} async-done(((f32[512,1024]{1,0:T(8,128)}), f32[128,1024]{1,0:T(8,128)}) %reduce-scatter.5.cloned.1.call-update) | async-done | bytes 524304 | tf_op jit(solution)/shard_map/while/body/eval_jaxpr/reduce_scatter | solution.py:95
  680.4 22.8 %all-gather.19.cloned.1.call-done = bf16[512,1024]{1,0:T(8,128)(2,1)} async-done(((bf16[128,1024]{1,0:T(8,128)(2,1)}), bf16[512,1024]{1,0:T(8,128)(2,1)}) %all-gather.19.cloned.1.call-update) | async-done | bytes 1048592 | tf_op jit(solution)/shard_map/while/body/eval_jaxpr/all_gather | solution.py:91
  722.0 21.1 %reduce-scatter.7.cloned.1.call-done = f32[128,1024]{1,0:T(8,128)} async-done(((f32[512,1024]{1,0:T(8,128)}), f32[128,1024]{1,0:T(8,128)}) %reduce-scatter.7.cloned.1.call-update) | async-done | bytes 524304 | tf_op jit(solution)/shard_map/while/body/eval_jaxpr/reduce_scatter | solution.py:95
  747.1 121.2 %while.134 = (s32[]{:T(128)}, f32[1024,1024]{1,0:T(8,128)}, f32[1024,1024]{1,0:T(8,128)}, f32[1024]{0:T(1024)}, f32[2,128,1024]{2,1,0:T(8,128)}, /*index=5*/bf16...) while((s32[]{:T(128)}, f32[1024,1024]{1,0:T(8,128)}, ...), condition=%wide.region_20.21_spmd.clone, body=%wide.region_15.20_spmd.clone.sunk | while | flops 4312401920 | bytes 70055400 | solution.py:306
  748.8 24.1 %all-gather.21.cloned.1.call-done = bf16[1,512,1024]{2,1,0:T(8,128)(2,1)} async-done(((bf16[1,128,1024]{2,1,0:T(8,128)(2,1)}), bf16[1,512,1024]{2,1,0:T(8,128)(2,1)}) %all-gather.21.cloned.1.call-update) | async-done | bytes 1048592 | tf_op jit(solution)/shard_map/while/body/eval_jaxpr/all_gather | solution.py:101
  789.6 14.3 reduce-scatter.9.cloned.1.call-done
  808.9 25.2 %all-gather.21.cloned.1.call-done = bf16[1,512,1024]{2,1,0:T(8,128)(2,1)} async-done(((bf16[1,128,1024]{2,1,0:T(8,128)(2,1)}), bf16[1,512,1024]{2,1,0:T(8,128)(2,1)}) %all-gather.21.cloned.1.call-update) | async-done | bytes 1048592 | tf_op jit(solution)/shard_map/while/body/eval_jaxpr/all_gather | solution.py:101
  869.3 442.4 %while.136 = (s32[]{:T(128)}, f32[1024,3,256]{2,0,1:T(8,128)}, f32[256,1024]{1,0:T(8,128)}, f32[2,512,1024]{2,1,0:T(8,128)}, f32[512,256]{0,1:T(8,128)}, /*index...) while((s32[]{:T(128)}, f32[1024,3,256]{2,0,1:T(8,128)}, ...), condition=%wide.region_35.36_spmd.clone, body=%wide.region_21.35_spmd.clone.sunk | while | flops 5009186816 | bytes 400735008 | solution.py:464
  879.3 17.3 %all-gather.23.cloned.1.call-done = bf16[512,1024]{1,0:T(8,128)(2,1)} async-done(((bf16[128,1024]{1,0:T(8,128)(2,1)}), bf16[512,1024]{1,0:T(8,128)(2,1)}) %all-gather.23.cloned.1.call-update) | async-done | bytes 1048592 | tf_op jit(solution)/shard_map/while/body/eval_jaxpr/all_gather | solution.py:101
  934.7 19.0 %all-gather.25.cloned.1.call-done = bf16[32,512,256]{2,1,0:T(8,128)(2,1)} async-done(((bf16[1,512,256]{2,1,0:T(8,128)(2,1)}), bf16[32,512,256]{2,1,0:T(8,128)(2,1)}) %all-gather.25.cloned.1.call-update) | async-done | bytes 8388624 | tf_op jit(solution)/shard_map/while/body/eval_jaxpr/all_gather | solution.py:44
  953.7 55.6 %all-gather.27.cloned.1.call-done = bf16[32,512,256]{2,1,0:T(8,128)(2,1)} async-done(((bf16[1,512,256]{2,1,0:T(8,128)(2,1)}), bf16[32,512,256]{2,1,0:T(8,128)(2,1)}) %all-gather.27.cloned.1.call-update) | async-done | bytes 8388624 | tf_op jit(solution)/shard_map/while/body/eval_jaxpr/all_gather | solution.py:44
  1009.4 40.2 %while.138 = (s32[]{:T(128)}, f32[512,256]{1,0:T(8,128)S(1)}, s32[]{:T(128)}, bf16[32,512,256]{2,1,0:T(8,128)(2,1)}, bf16[32,512,256]{2,1,0:T(8,128)(2,1)}, /*index=5*/s32[]{:T(128)}, s32[]{:T(128)}, s32[]{:T(128)}, s32[]{:T(128)}) while((s32[]{:T(128)}, f32[512,256]{1,0:T(8,128)S(1)}, s32[]{:T(128)}, bf16[32,512,256]{2,1,0:T(8,128)(2,1)}, ...), condition=%wide.region_26.26_spmd, body=%wide.region_25.25_spmd.sunk | while | flops 524294 | bytes 1573015 | solution.py:59
  1099.2 17.6 %all-gather.23.cloned.1.call-done = bf16[512,1024]{1,0:T(8,128)(2,1)} async-done(((bf16[128,1024]{1,0:T(8,128)(2,1)}), bf16[512,1024]{1,0:T(8,128)(2,1)}) %all-gather.23.cloned.1.call-update) | async-done | bytes 1048592 | tf_op jit(solution)/shard_map/while/body/eval_jaxpr/all_gather | solution.py:101
  1159.9 15.2 %all-gather.25.cloned.1.call-done = bf16[32,512,256]{2,1,0:T(8,128)(2,1)} async-done(((bf16[1,512,256]{2,1,0:T(8,128)(2,1)}), bf16[32,512,256]{2,1,0:T(8,128)(2,1)}) %all-gather.25.cloned.1.call-update) | async-done | bytes 8388624 | tf_op jit(solution)/shard_map/while/body/eval_jaxpr/all_gather | solution.py:44
  1175.2 56.2 %all-gather.27.cloned.1.call-done = bf16[32,512,256]{2,1,0:T(8,128)(2,1)} async-done(((bf16[1,512,256]{2,1,0:T(8,128)(2,1)}), bf16[32,512,256]{2,1,0:T(8,128)(2,1)}) %all-gather.27.cloned.1.call-update) | async-done | bytes 8388624 | tf_op jit(solution)/shard_map/while/body/eval_jaxpr/all_gather | solution.py:44
  1231.4 40.2 %while.138 = (s32[]{:T(128)}, f32[512,256]{1,0:T(8,128)S(1)}, s32[]{:T(128)}, bf16[32,512,256]{2,1,0:T(8,128)(2,1)}, bf16[32,512,256]{2,1,0:T(8,128)(2,1)}, /*index=5*/s32[]{:T(128)}, s32[]{:T(128)}, s32[]{:T(128)}, s32[]{:T(128)}) while((s32[]{:T(128)}, f32[512,256]{1,0:T(8,128)S(1)}, s32[]{:T(128)}, bf16[32,512,256]{2,1,0:T(8,128)(2,1)}, ...), condition=%wide.region_26.26_spmd, body=%wide.region_25.25_spmd.sunk | while | flops 524294 | bytes 1573015 | solution.py:59
  1354.6 64.2 %all-reduce.1 = (bf16[32,2]{0,1:T(2,128)(2,1)S(1)}, bf16[256]{0:T(256)(128)(2,1)S(1)}, bf16[256]{0:T(256)(128)(2,1)S(1)}) all-reduce(bf16[32,2]{0,1:T(2,128)(2,1)S(1)} %stack.213, bf16[256]{0:T(256)(128)(2,1)S(1)} %convert_element_type.3724, bf16[256]{0:T(256)(128)(2,1)S(1)} %convert_element_type.3726), channel_id=1, replica_groups=mesh['blk'=32,'head'=4] {'blk'}, use_global_device_ids=true, to_apply=%region_72.73 | all-reduce | flops 576 | bytes 2304 | tf_op jit(solution)/shard_map/psum | solution.py:478
  1420.5 66.0 %all-reduce = (f32[1024]{0:T(1024)}, f32[1024]{0:T(1024)}) all-reduce(f32[1024]{0:T(1024)S(1)} %copy-done.109, f32[1024]{0:T(1024)S(1)} %copy-done.112), channel_id=1, replica_groups=mesh['blk'=32,'head'=4] {'blk','head'}, use_global_device_ids=true, to_apply=%region_36.37 | all-reduce | flops 2048 | bytes 16384 | tf_op jit(solution)/shard_map/psum | solution.py:474
  (1007 shorter events, 619.8 us)
Async XLA Ops:
  56.6 28.8 %all-gather.13.cloned.1.call-start = ((), (), s32[]{:S(2)}) async-start(), calls=%async_computation.5 | async-start | bytes 1310720 | tf_op jit(solution)/shard_map/while/body/eval_jaxpr/all_gather | solution.py:91
  57.7 111.3 %all-gather.15.cloned.1.call-start = ((), (), s32[]{:S(2)}) async-start(), calls=%async_computation.6 | async-start | bytes 17301504 | tf_op jit(solution)/shard_map/while/body/eval_jaxpr/all_gather | solution.py:24
  94.5 148.7 %all-gather.17.cloned.1.call-start = ((), (), s32[]{:S(2)}) async-start(), calls=%async_computation.7 | async-start | bytes 17301504 | tf_op jit(solution)/shard_map/while/body/eval_jaxpr/all_gather | solution.py:24
  95.3 239.2 %reduce-scatter.5.cloned.1.call-start = ((), (), s32[]{:S(2)}) async-start(), calls=%async_computation.8 | async-start | bytes 2621440 | tf_op jit(solution)/shard_map/while/body/eval_jaxpr/reduce_scatter | solution.py:95
  96.6 11.9 collective-permute-start.1
  305.6 54.9 %all-gather.19.cloned.1.call-start = ((), (), s32[]{:S(2)}) async-start(), calls=%async_computation.9 | async-start | bytes 1310720 | tf_op jit(solution)/shard_map/while/body/eval_jaxpr/all_gather | solution.py:91
  337.6 62.7 %reduce-scatter.7.cloned.1.call-start = ((), (), s32[]{:S(2)}) async-start(), calls=%async_computation.10 | async-start | bytes 2621440 | tf_op jit(solution)/shard_map/while/body/eval_jaxpr/reduce_scatter | solution.py:95
  402.8 25.3 %all-gather.13.cloned.1.call-start = ((), (), s32[]{:S(2)}) async-start(), calls=%async_computation.5 | async-start | bytes 1310720 | tf_op jit(solution)/shard_map/while/body/eval_jaxpr/all_gather | solution.py:91
  403.8 107.8 %all-gather.15.cloned.1.call-start = ((), (), s32[]{:S(2)}) async-start(), calls=%async_computation.6 | async-start | bytes 17301504 | tf_op jit(solution)/shard_map/while/body/eval_jaxpr/all_gather | solution.py:24
  437.3 148.7 %all-gather.17.cloned.1.call-start = ((), (), s32[]{:S(2)}) async-start(), calls=%async_computation.7 | async-start | bytes 17301504 | tf_op jit(solution)/shard_map/while/body/eval_jaxpr/all_gather | solution.py:24
  438.0 239.2 %reduce-scatter.5.cloned.1.call-start = ((), (), s32[]{:S(2)}) async-start(), calls=%async_computation.8 | async-start | bytes 2621440 | tf_op jit(solution)/shard_map/while/body/eval_jaxpr/reduce_scatter | solution.py:95
  439.3 11.9 collective-permute-start.1
  648.3 54.9 %all-gather.19.cloned.1.call-start = ((), (), s32[]{:S(2)}) async-start(), calls=%async_computation.9 | async-start | bytes 1310720 | tf_op jit(solution)/shard_map/while/body/eval_jaxpr/all_gather | solution.py:91
  680.3 62.8 %reduce-scatter.7.cloned.1.call-start = ((), (), s32[]{:S(2)}) async-start(), calls=%async_computation.10 | async-start | bytes 2621440 | tf_op jit(solution)/shard_map/while/body/eval_jaxpr/reduce_scatter | solution.py:95
  747.1 25.8 %all-gather.21.cloned.1.call-start = ((), (), s32[]{:S(2)}) async-start(), calls=%async_computation.11 | async-start | bytes 1310720 | tf_op jit(solution)/shard_map/while/body/eval_jaxpr/all_gather | solution.py:101
  748.8 55.0 %reduce-scatter.9.cloned.1.call-start = ((), (), s32[]{:S(2)}) async-start(), calls=%async_computation.12 | async-start | bytes 1310720 | tf_op jit(solution)/shard_map/while/body/eval_jaxpr/reduce_scatter | solution.py:105
  807.1 26.9 %all-gather.21.cloned.1.call-start = ((), (), s32[]{:S(2)}) async-start(), calls=%async_computation.11 | async-start | bytes 1310720 | tf_op jit(solution)/shard_map/while/body/eval_jaxpr/all_gather | solution.py:101
  808.8 56.1 %reduce-scatter.9.cloned.1.call-start = ((), (), s32[]{:S(2)}) async-start(), calls=%async_computation.12 | async-start | bytes 1310720 | tf_op jit(solution)/shard_map/while/body/eval_jaxpr/reduce_scatter | solution.py:105
  869.5 27.1 %all-gather.23.cloned.1.call-start = ((), (), s32[]{:S(2)}) async-start(), calls=%async_computation.13 | async-start | bytes 1310720 | tf_op jit(solution)/shard_map/while/body/eval_jaxpr/all_gather | solution.py:101
  871.6 82.1 %all-gather.25.cloned.1.call-start = ((), (), s32[]{:S(2)}) async-start(), calls=%async_computation.14 | async-start | bytes 8650752 | tf_op jit(solution)/shard_map/while/body/eval_jaxpr/all_gather | solution.py:44
  875.4 133.9 %all-gather.27.cloned.1.call-start = ((), (), s32[]{:S(2)}) async-start(), calls=%async_computation.15 | async-start | bytes 8650752 | tf_op jit(solution)/shard_map/while/body/eval_jaxpr/all_gather | solution.py:44
  910.1 176.2 %reduce-scatter.11.cloned.1.call-start = ((), (), s32[]{:S(2)}) async-start(), calls=%async_computation.16 | async-start | bytes 1310720 | tf_op jit(solution)/shard_map/while/body/eval_jaxpr/reduce_scatter | solution.py:105
  920.7 11.8 collective-permute-start
  1009.4 41.3 %copy-start.99 = (f32[256]{0:T(256)S(1)}, f32[256]{0:T(256)}, u32[]{:S(2)}) copy-start(f32[256]{0:T(256)} %copy-done.98) | copy-start | bytes 3076 | tf_op jit(solution)/shard_map/while
  1089.5 27.4 %all-gather.23.cloned.1.call-start = ((), (), s32[]{:S(2)}) async-start(), calls=%async_computation.13 | async-start | bytes 1310720 | tf_op jit(solution)/shard_map/while/body/eval_jaxpr/all_gather | solution.py:101
  1091.6 83.6 %all-gather.25.cloned.1.call-start = ((), (), s32[]{:S(2)}) async-start(), calls=%async_computation.14 | async-start | bytes 8650752 | tf_op jit(solution)/shard_map/while/body/eval_jaxpr/all_gather | solution.py:44
  1095.4 136.0 %all-gather.27.cloned.1.call-start = ((), (), s32[]{:S(2)}) async-start(), calls=%async_computation.15 | async-start | bytes 8650752 | tf_op jit(solution)/shard_map/while/body/eval_jaxpr/all_gather | solution.py:44
  1130.3 178.0 %reduce-scatter.11.cloned.1.call-start = ((), (), s32[]{:S(2)}) async-start(), calls=%async_computation.16 | async-start | bytes 1310720 | tf_op jit(solution)/shard_map/while/body/eval_jaxpr/reduce_scatter | solution.py:105
  1143.2 14.6 collective-permute-start
  1311.7 174.8 %all-reduce.5.cloned.1.call-start = ((), (), s32[]{:S(2)}) async-start(), calls=%async_computation.4 | async-start | bytes 13369344 | tf_op jit(solution)/shard_map/psum | solution.py:476
  1338.4 82.1 %copy-start.109 = (f32[1024]{0:T(1024)S(1)}, f32[1024]{0:T(1024)}, u32[]{:S(2)}) copy-start(f32[1024]{0:T(1024)} %get-tuple-element.1174) | copy-start | bytes 12292
  1338.4 82.1 %copy-start.112 = (f32[1024]{0:T(1024)S(1)}, f32[1024]{0:T(1024)}, u32[]{:S(2)}) copy-start(f32[1024]{0:T(1024)} %get-tuple-element.1175) | copy-start | bytes 12292
  (237 other events, 1343.7 us)
Sparse Core Ops, SparseCore 0:
  59.1 26.2 all-gather.12
  94.7 74.2 all-gather.14
  171.2 71.9 all-gather.16
  305.7 28.7 reduce-scatter.4
  337.7 22.7 all-gather.18
  369.4 30.9 reduce-scatter.6
  405.3 22.7 all-gather.12
  437.4 74.2 all-gather.14
  513.9 71.9 all-gather.16
  648.4 28.7 reduce-scatter.4
  680.4 22.7 all-gather.18
  712.1 30.9 reduce-scatter.6
  750.1 22.7 all-gather.20
  780.4 23.3 reduce-scatter.8
  809.9 24.1 all-gather.20
  841.5 23.3 reduce-scatter.8
  872.4 24.1 all-gather.22
  899.0 54.6 all-gather.24
  956.8 52.5 all-gather.26
  1066.9 19.3 reduce-scatter.10
  1092.7 24.1 all-gather.22
  1119.4 55.7 all-gather.24
  1178.3 53.0 all-gather.26
  1288.9 19.3 reduce-scatter.10
Sparse Core Ops, SparseCore 1:
  1325.3 118.9 all-reduce.4
where the time goes:
time: 1520 us; the launch traced here: 1510 us
  waiting for transfers between devices  732 us (48%)
  other arithmetic  357 us (23%)
  matrix products  139 us (9%)
  blocking collectives  130 us (9%)
  local copies, waits for them, and re-layouts  102 us (7%)
  starting transfers between devices  17.2 us (1%)
  between operations  16.2 us (1%)
    all_gather x4, waiting for transfers between devices, carried_in(): everything = jax.tree.map(lambda part: lax.all_gather(part, axis), shard)  254 us
    all_gather x4, waiting for transfers between devices, entering(): lax.all_gather(a.astype(kind), axis)  146 us
    select_n x64, other arithmetic, turn(): return jax.tree.map(lambda a, b: jnp.where(reached, a, b), new, before)  106 us
    reduce_scatter x4, waiting for transfers between devices, reduce_rows(): lax.psum_scatter(term(jnp.int32(0), rows * lax.axis_size('head')), 'head'...  99.7 us
    all_gather x4, waiting for transfers between devices, gather_rows(): return lax.all_gather(values, 'head', axis=0, tiled=True)  95.1 us
    all_gather x4, waiting for transfers between devices, gather_grads(): return lax.all_gather(values, 'head', axis=0, tiled=True)  84.3 us
    add x60, other arithmetic, chain_combine(): return (earlier[0] * later[0], later[0] * earlier[1] + later[1])  79.2 us
    psum x1, blocking collectives, body(): lax.psum((g_attn_gain, g_mlp_gain), ('blk', 'head'))  66 us
  transfers between devices with their start and end apart: 29, of which 27 were waited for; matrix products, arithmetic and copies ran while one was open for 12% of the time, Pallas kernels for 0%

commit v1 on v0

v1 whole, which is shorter than its diff:
```python
import functools
import math

import jax
import jax.numpy as jnp
from jax import lax
from jax.experimental import pallas as pl
from jax.experimental.pallas import tpu as pltpu
from jax.sharding import PartitionSpec as P

BUCKETS = 32
MAXDIST = 128
EPSILON = 1e-06
MASKED = -1e30
TILE = 128
MESH = pl.DeviceIdType.MESH
BF = jnp.bfloat16
F32 = jnp.float32


def bucket_index(distance):
    exact_part = BUCKETS // 2
    result = jnp.minimum(distance, exact_part)
    for level in range(1, BUCKETS - exact_part):
        boundary = int(
            math.ceil(exact_part * (MAXDIST / exact_part) ** (level / (BUCKETS - exact_part)))
        )
        result = result + (distance >= boundary).astype(jnp.int32)
    return result


def rms_norm(values, gain):
    return values * lax.rsqrt(jnp.mean(values * values, axis=-1, keepdims=True) + EPSILON) * gain


def rms_back(values, gain, grad):
    inverse = lax.rsqrt(jnp.mean(values * values, axis=-1, keepdims=True) + EPSILON)
    unit = values * inverse
    scaled = grad * gain
    inner = jnp.mean(scaled * unit, axis=-1, keepdims=True)
    return inverse * (scaled - unit * inner), jnp.sum(grad * unit, axis=0)


def ring(step):
    return [(i, (i + step) % 4) for i in range(4)]


def to_right(values):
    return lax.ppermute(values, "head", ring(1))


def to_left(values):
    return lax.ppermute(values, "head", ring(3))


def gather_ring(values):
    half = values.shape[0] // 2
    left = to_right(values)
    right = to_left(values)
    first = to_right(left[:half])
    second = to_left(right[half:])
    return jnp.concatenate([values, right, first, second, left], 0)


def reduce_ring(partial):
    rows = partial.shape[0] // 4
    half = rows // 2
    low = partial.astype(BF)
    own, right, opposite, left = (low[k * rows : (k + 1) * rows] for k in range(4))
    a = to_right(opposite[:half])
    b = to_left(opposite[half:])
    a = jnp.concatenate([(a.astype(F32) + right[:half].astype(F32)).astype(BF), right[half:]], 0)
    b = jnp.concatenate([left[:half], (b.astype(F32) + left[half:].astype(F32)).astype(BF)], 0)
    a = to_right(a)
    b = to_left(b)
    return partial[:rows] + a.astype(F32) + b.astype(F32)


def rolled(values, start):
    return lax.dynamic_slice_in_dim(
        jnp.concatenate([values, values], 0), start, values.shape[0], 0
    )


def shifted(block, distance):
    devices = range(lax.axis_size("blk"))
    route = [(i - distance, i) for i in devices if i - distance in devices]
    return lax.ppermute(block, "blk", route)


def enter_all(count, place):
    barrier = pltpu.get_barrier_semaphore()

    def greet(j, c):
        pl.semaphore_signal(
            barrier, inc=1, device_id={"blk": lax.rem(place + j, count)}, device_id_type=MESH
        )
        return c

    lax.fori_loop(1, count, greet, 0)
    pl.semaphore_wait(barrier, count - 1)


def exchange(count, place, source, target, send_sem, recv_sem, local_sem):
    def part(j):
        peer = lax.rem(place + j, count)
        return pltpu.make_async_remote_copy(
            src_ref=source.at[:, peer],
            dst_ref=target.at[:, place],
            send_sem=send_sem.at[j],
            recv_sem=recv_sem.at[j],
            device_id={"blk": peer},
            device_id_type=MESH,
        )

    def start(j, c):
        part(j).start()
        return c

    def finish(j, c):
        part(j).wait()
        return c

    lax.fori_loop(1, count, start, 0)
    own = pltpu.make_async_copy(source.at[:, place], target.at[:, place], local_sem)
    own.start()
    own.wait()
    lax.fori_loop(1, count, finish, 0)


def scan_kernel(
    count, own_keep, unit, bias, slope, prior, across, keep, held, s0, r0, s1, r1, s2, r2, local
):
    place = lax.axis_index("blk")
    enter_all(count, place)

    def tell(j):
        return pltpu.make_async_remote_copy(
            src_ref=own_keep,
            dst_ref=keep.at[place],
            send_sem=s0.at[j],
            recv_sem=r0.at[j],
            device_id={"blk": lax.rem(place + j, count)},
            device_id_type=MESH,
        )

    def tell_start(j, c):
        tell(j).start()
        return c

    def tell_wait(j, c):
        tell(j).wait()
        return c

    lax.fori_loop(1, count, tell_start, 0)
    own = pltpu.make_async_copy(own_keep, keep.at[place], local.at[2])
    own.start()
    own.wait()
    exchange(count, place, unit, across, s1, r1, local.at[0])
    lax.fori_loop(1, count, tell_wait, 0)
    for m in range(unit.shape[0]):
        def step(b, state, m=m):
            u = across[m, b].astype(F32)
            forget = jax.nn.sigmoid(bias[...] + slope[...] * u)
            before = keep[b, m : m + 1] * state
            held[m, b] = before.astype(BF)
            return forget * before + (1.0 - forget) * u

        lax.fori_loop(0, count, step, jnp.zeros(unit.shape[2:], F32))
    exchange(count, place, held, prior, s2, r2, local.at[1])


def scan_back_kernel(count, keep, grads, across, bias, slope, out, moved, held, s1, r1, s2, r2, local):
    place = lax.axis_index("blk")
    enter_all(count, place)
    exchange(count, place, grads, moved, s1, r1, local.at[0])
    for m in range(grads.shape[0]):
        def step(t, grad, m=m):
            b = count - 1 - t
            held[m, b] = grad.astype(BF)
            u = across[m, b].astype(F32)
            forget = jax.nn.sigmoid(bias[...] + slope[...] * u)
            return keep[b, m : m + 1] * (moved[m, b].astype(F32) + forget * grad)

        lax.fori_loop(0, count, step, jnp.zeros(grads.shape[2:], F32))
    exchange(count, place, held, out, s2, r2, local.at[1])


def semaphores(count):
    return [pltpu.SemaphoreType.DMA((count,))] * 4 + [pltpu.SemaphoreType.DMA((3,))]


VMEM = pl.BlockSpec(memory_space=pltpu.VMEM)
SMEM = pl.BlockSpec(memory_space=pltpu.SMEM)


def state_scan(keep, unit, bias, slope):
    count = lax.axis_size("blk")
    shape = jax.ShapeDtypeStruct(unit.shape, BF)
    return pl.pallas_call(
        functools.partial(scan_kernel, count),
        out_shape=(shape, shape, jax.ShapeDtypeStruct((count,) + keep.shape, F32)),
        in_specs=[VMEM, VMEM, VMEM, VMEM],
        out_specs=(VMEM, VMEM, VMEM),
        scratch_shapes=[pltpu.VMEM(unit.shape, BF)]
        + [pltpu.SemaphoreType.DMA((count,))] * 2
        + semaphores(count),
        compiler_params=pltpu.CompilerParams(collective_id=1, has_side_effects=True),
        name="state_scan",
    )(keep, unit, bias, slope)


def state_scan_back(keep, grads, across, bias, slope):
    count = lax.axis_size("blk")
    shape = jax.ShapeDtypeStruct(grads.shape, BF)
    return pl.pallas_call(
        functools.partial(scan_back_kernel, count),
        out_shape=shape,
        in_specs=[VMEM, VMEM, VMEM, VMEM, VMEM],
        out_specs=VMEM,
        scratch_shapes=[pltpu.VMEM(grads.shape, BF)] * 2 + semaphores(count),
        compiler_params=pltpu.CompilerParams(collective_id=2, has_side_effects=True),
        name="state_scan_back",
    )(keep, grads, across, bias, slope)


def dot(a, b, dims):
    return lax.dot_general(a, b, (dims, ((), ())), preferred_element_type=F32)


def body(
    tokens_in,
    grad_out,
    flags,
    attn_gain,
    mlp_gain,
    w_qkv,
    w_out,
    rel_bias,
    state_query,
    state_proj,
    forget_bias,
    forget_scale,
    w_up,
    w_down,
):
    micros, rows, width = tokens_in.shape
    place = lax.axis_index("head")
    block = rows * 4
    local_width = w_qkv.shape[2]
    heads = rel_bias.shape[1]
    head_size = local_width // heads
    states = state_query.shape[0]
    buckets = rel_bias.shape[0]
    scale = head_size ** (-0.5)
    tiles = block // TILE
    qkv_flat = w_qkv.reshape(width, 3 * local_width)
    query_heads = state_query.reshape(states, heads, head_size)
    to_absolute = lax.rem(4 - place, 4) * rows
    to_relative = place * rows

    keep_own = (1 - flags[:, 0]).astype(F32)
    keep_rows = jnp.zeros((8, local_width), F32).at[:micros].set(keep_own[:, None])

    near = (
        lax.broadcasted_iota(jnp.int32, (TILE, 2 * TILE), 0)
        + TILE
        - lax.broadcasted_iota(jnp.int32, (TILE, 2 * TILE), 1)
    )
    near_bucket = bucket_index(jnp.maximum(near, 0))
    near_bias = jnp.zeros((heads, TILE, 2 * TILE), F32)
    for level in range(buckets):
        near_bias = near_bias + jnp.where(
            (near_bucket == level)[None], rel_bias[level][:, None, None], 0.0
        )
    far = jnp.broadcast_to(rel_bias[buckets - 1][:, None, None], (heads, TILE, TILE))
    off = jnp.full((heads, TILE, TILE), MASKED, F32)
    iota0 = lax.broadcasted_iota(jnp.int32, (TILE, TILE), 0)
    iota1 = lax.broadcasted_iota(jnp.int32, (TILE, TILE), 1)
    diagonal = jnp.where((iota0 >= iota1)[None], near_bias[..., TILE:], MASKED)
    last = jnp.where((iota0 < iota1)[None], far, MASKED)
    by_offset = {0: last, tiles: diagonal, tiles - 1: near_bias[..., :TILE]}
    bias_table = jnp.concatenate(
        [
            jnp.concatenate(
                [
                    off if k < q or k > q + tiles else by_offset.get(k - q, far)
                    for k in range(2 * tiles)
                ],
                -1,
            )
            for q in range(tiles)
        ],
        1,
    )

    x = [tokens_in[m].astype(F32) for m in range(micros)]
    both = range(micros)
    whole = [gather_ring(rms_norm(x[m], attn_gain).astype(BF)) for m in both]

    queries, keys, values, earlier_kv = [], [], [], []
    update, unit, update_lse = [], [], []
    for m in both:
        mixed = rolled(dot(whole[m], qkv_flat, ((1,), (0,))).astype(BF), to_absolute).reshape(
            block, 3, heads, head_size
        )
        queries.append(mixed[:, 0])
        keys.append(mixed[:, 1])
        values.append(mixed[:, 2])
        earlier_kv.append(shifted(mixed[:, 1:], 1))
        scores = (
            jnp.einsum("shd,jhd->hsj", query_heads, keys[m], preferred_element_type=F32) * scale
        )
        top = jnp.max(scores, axis=-1, keepdims=True)
        raised = jnp.exp(scores - top)
        total = jnp.sum(raised, axis=-1, keepdims=True)
        update_lse.append(top + jnp.log(total))
        weights = (raised / total).astype(BF)
        update.append(
            jnp.einsum("hsj,jhd->shd", weights, values[m], preferred_element_type=F32)
        )
        unit.append(
            (
                update[m]
                * lax.rsqrt(jnp.mean(update[m] * update[m], axis=-1, keepdims=True) + EPSILON)
            ).reshape(states, local_width)
        )

    count = lax.axis_size("blk")
    split = (micros, count, states // count, local_width)
    bias_row, scale_row = forget_bias[None], forget_scale[None]
    prior_low, across, keeps = state_scan(
        keep_rows, jnp.stack(unit).astype(BF).reshape(split), bias_row, scale_row
    )
    prior_low = prior_low.reshape(micros, states, local_width)
    whole_grad = [gather_ring(grad_out[m]) for m in both]

    forget, state_after, state_kv = [], [], []
    all_keys, all_values, lse, attended, middle, whole_mlp = [], [], [], [], [], []
    for m in both:
        forget.append(jax.nn.sigmoid(forget_bias + forget_scale * unit[m]))
        state_after.append(
            forget[m] * prior_low[m].astype(F32) + (1.0 - forget[m]) * unit[m]
        )
        state_kv.append(
            jnp.einsum(
                "shd,hde->she",
                prior_low[m].reshape(states, heads, head_size),
                state_proj,
                preferred_element_type=F32,
            ).astype(BF)
        )
        all_keys.append(jnp.concatenate([earlier_kv[m][:, 0], keys[m]], 0))
        all_values.append(jnp.concatenate([earlier_kv[m][:, 1], values[m]], 0))

    def scores_of(m):
        closed = jnp.where(flags[m, 0] == 0, 0.0, MASKED)
        closed = jnp.concatenate(
            [jnp.broadcast_to(closed, (block,)), jnp.zeros((block,), F32)]
        )
        token_scores = (
            jnp.einsum("ihd,jhd->hij", queries[m], all_keys[m], preferred_element_type=F32)
            * scale
            + bias_table
            + closed[None, None]
        )
        state_scores = (
            jnp.einsum(
                "ihd,shd->his",
                queries[m],
                state_kv[m][..., :head_size],
                preferred_element_type=F32,
            )
            * scale
        )
        return token_scores, state_scores

    for m in both:
        token_scores, state_scores = scores_of(m)
        highest = jnp.maximum(
            jnp.max(token_scores, axis=-1, keepdims=True),
            jnp.max(state_scores, axis=-1, keepdims=True),
        )
        token_exp = jnp.exp(token_scores - highest)
        state_exp = jnp.exp(state_scores - highest)
        total = jnp.sum(token_exp, axis=-1, keepdims=True) + jnp.sum(
            state_exp, axis=-1, keepdims=True
        )
        lse.append(highest + jnp.log(total))
        att = jnp.einsum(
            "hij,jhd->ihd",
            (token_exp / total).astype(BF),
            all_values[m],
            preferred_element_type=F32,
        ) + jnp.einsum(
            "his,shd->ihd",
            (state_exp / total).astype(BF),
            state_kv[m][..., head_size:],
            preferred_element_type=F32,
        )
        attended.append(rolled(att.astype(BF).reshape(block, local_width), to_relative))
        branch = reduce_ring(dot(attended[m], w_out, ((1,), (0,))))
        middle.append(x[m] + branch)
        whole_mlp.append(gather_ring(rms_norm(middle[m], mlp_gain).astype(BF)))

    out, grad_middle, whole_gm = [], [], []
    active, grad_hidden = [], []
    g_mlp_gain = jnp.zeros(mlp_gain.shape, F32)
    root = math.sqrt(2.0 / math.pi)
    for m in both:
        hidden = dot(whole_mlp[m], w_up, ((1,), (0,)))
        square = hidden * hidden
        bent = jnp.tanh(root * hidden * (1.0 + 0.044715 * square))
        active.append((0.5 * hidden * (1.0 + bent)).astype(BF))
        slope = 0.5 * (1.0 + bent) + 0.5 * hidden * (1.0 - bent * bent) * root * (
            1.0 + 3.0 * 0.044715 * square
        )
        grad_active = dot(whole_grad[m], w_down, ((1,), (1,)))
        grad_hidden.append((grad_active * slope).astype(BF))
        grad_normed = reduce_ring(dot(grad_hidden[m], w_up, ((1,), (1,))))
        part, gain = rms_back(middle[m], mlp_gain, grad_normed)
        g_mlp_gain = g_mlp_gain + gain
        grad_middle.append(grad_out[m].astype(F32) + part)
        whole_gm.append(gather_ring(grad_middle[m].astype(BF)))
        out.append(middle[m] + reduce_ring(dot(active[m], w_down, ((1,), (0,)))))

    def joined(parts):
        return jnp.concatenate(parts, 0)

    g_up = dot(joined(whole_mlp), joined(grad_hidden), ((0,), (0,)))
    g_down = dot(joined(active), joined(whole_grad), ((0,), (0,)))

    def summed(values):
        return lax.psum(values.astype(BF), "blk").astype(F32)

    g_up, g_down = summed((g_up)), summed((g_down))

    near_acc = jnp.zeros((heads, TILE, 2 * TILE), F32)
    all_acc = jnp.zeros((heads,), F32)
    g_proj = jnp.zeros(state_proj.shape, F32)
    grad_queries, grad_keys, grad_values, earlier_grads, grad_prior = [], [], [], [], []
    for m in both:
        grad_att = rolled(dot(whole_gm[m], w_out, ((1,), (1,))).astype(BF), to_absolute).reshape(
            block, heads, head_size
        )
        state_keys = state_kv[m][..., :head_size]
        state_values = state_kv[m][..., head_size:]
        token_scores, state_scores = scores_of(m)
        token_probs = jnp.exp(token_scores - lse[m])
        state_probs = jnp.exp(state_scores - lse[m])
        grad_token_probs = jnp.einsum(
            "ihd,jhd->hij", grad_att, all_values[m], preferred_element_type=F32
        )
        grad_state_probs = jnp.einsum(
            "ihd,shd->his", grad_att, state_values, preferred_element_type=F32
        )
        delta = jnp.sum(token_probs * grad_token_probs, axis=-1, keepdims=True) + jnp.sum(
            state_probs * grad_state_probs, axis=-1, keepdims=True
        )
        grad_token_scores = token_probs * (grad_token_probs - delta)
        grad_state_scores = state_probs * (grad_state_probs - delta)
        for q in range(tiles):
            near_acc = near_acc + grad_token_scores[
                :, q * TILE : (q + 1) * TILE, (q + tiles - 1) * TILE : (q + tiles + 1) * TILE
            ]
        all_acc = all_acc + jnp.sum(grad_token_scores, axis=(1, 2))
        token_low = grad_token_scores.astype(BF)
        state_low = grad_state_scores.astype(BF)
        grad_values_all = jnp.einsum(
            "hij,ihd->jhd", token_probs.astype(BF), grad_att, preferred_element_type=F32
        )
        grad_state_values = jnp.einsum(
            "his,ihd->shd", state_probs.astype(BF), grad_att, preferred_element_type=F32
        )
        grad_queries.append(
            scale
            * (
                jnp.einsum("hij,jhd->ihd", token_low, all_keys[m], preferred_element_type=F32)
                + jnp.einsum("his,shd->ihd", state_low, state_keys, preferred_element_type=F32)
            )
        )
        grad_keys_all = scale * jnp.einsum(
            "hij,ihd->jhd", token_low, queries[m], preferred_element_type=F32
        )
        grad_state_keys = scale * jnp.einsum(
            "his,ihd->shd", state_low, queries[m], preferred_element_type=F32
        )
        earlier_grads.append(
            shifted(
                jnp.stack([grad_keys_all[:block], grad_values_all[:block]], 1).astype(BF), -1
            )
        )
        grad_keys.append(grad_keys_all[block:])
        grad_values.append(grad_values_all[block:])
        grad_state_kv = jnp.concatenate([grad_state_keys, grad_state_values], -1).astype(BF)
        g_proj = g_proj + jnp.einsum(
            "shd,she->hde",
            prior_low[m].reshape(states, heads, head_size),
            grad_state_kv,
            preferred_element_type=F32,
        )
        grad_prior.append(
            jnp.einsum(
                "she,hde->shd", grad_state_kv, state_proj, preferred_element_type=F32
            ).reshape(states, local_width)
        )
    g_out = summed(dot(joined(attended), joined(whole_gm), ((0,), (0,))))

    grad_after_all = state_scan_back(
        keeps, jnp.stack(grad_prior).astype(BF).reshape(split), across, bias_row, scale_row
    ).reshape(micros, states, local_width)

    g_query = jnp.zeros((states, local_width), F32)
    g_bias = jnp.zeros(forget_bias.shape, F32)
    g_scale = jnp.zeros(forget_scale.shape, F32)
    grad_mixed = []
    for m in both:
        grad_after = grad_after_all[m].astype(F32)
        prior = prior_low[m].astype(F32)
        grad_gate = grad_after * (prior - unit[m]) * forget[m] * (1.0 - forget[m])
        g_bias = g_bias + jnp.sum(grad_gate, 0)
        g_scale = g_scale + jnp.sum(grad_gate * unit[m], 0)
        grad_unit = (
            (grad_after * (1.0 - forget[m]) + grad_gate * forget_scale)
        ).reshape(states, heads, head_size)
        inverse = lax.rsqrt(jnp.mean(update[m] * update[m], axis=-1, keepdims=True) + EPSILON)
        unit_heads = unit[m].reshape(states, heads, head_size)
        grad_update_low = (
            inverse
            * (grad_unit - unit_heads * jnp.mean(grad_unit * unit_heads, axis=-1, keepdims=True))
        ).astype(BF)
        scores = (
            jnp.einsum("shd,jhd->hsj", query_heads, keys[m], preferred_element_type=F32) * scale
        )
        probs = jnp.exp(scores - update_lse[m])
        grad_probs = jnp.einsum(
            "shd,jhd->hsj", grad_update_low, values[m], preferred_element_type=F32
        )
        delta = jnp.sum(probs * grad_probs, axis=-1, keepdims=True)
        grad_scores = (probs * (grad_probs - delta)).astype(BF)
        grad_values_update = jnp.einsum(
            "hsj,shd->jhd", probs.astype(BF), grad_update_low, preferred_element_type=F32
        )
        g_query = g_query + scale * jnp.einsum(
            "hsj,jhd->shd", grad_scores, keys[m], preferred_element_type=F32
        ).reshape(states, local_width)
        grad_keys_update = scale * jnp.einsum(
            "hsj,shd->jhd", grad_scores, query_heads, preferred_element_type=F32
        )
        later = earlier_grads[m].astype(F32)
        gk = grad_keys[m] + later[:, 0] + grad_keys_update
        gv = grad_values[m] + later[:, 1] + grad_values_update
        grad_mixed.append(
            rolled(
                jnp.stack([grad_queries[m], gk, gv], 1)
                .astype(BF)
                .reshape(block, 3 * local_width),
                to_relative,
            )
        )

    g_qkv = dot(joined(whole), joined(grad_mixed), ((0,), (0,))).reshape(width, 3, local_width)
    g_rel = jnp.stack(
        [
            jnp.sum(
                jnp.where(((near_bucket == level) & (near >= 0))[None], near_acc, 0.0),
                axis=(1, 2),
            )
            for level in range(buckets - 1)
        ],
        0,
    )
    g_rel = jnp.concatenate([g_rel, (all_acc - jnp.sum(g_rel, 0))[None]], 0)
    grad_x = []
    g_attn_gain = jnp.zeros(attn_gain.shape, F32)
    for m in both:
        grad_normed = reduce_ring(dot(grad_mixed[m], qkv_flat, ((1,), (1,))))
        part, gain = rms_back(x[m], attn_gain, grad_normed)
        g_attn_gain = g_attn_gain + gain
        grad_x.append(grad_middle[m] + part)
    def over_head(values):
        for step in (1, 2):
            values = values + lax.ppermute(values, "head", [(i, i ^ step) for i in range(4)])
        return values

    gains = over_head(jnp.stack([g_attn_gain, g_mlp_gain]).reshape(8, local_width))
    small = jnp.concatenate(
        [g_rel.reshape(1, buckets * heads), jnp.zeros((1, local_width - buckets * heads), F32)], 1
    )
    packed = jnp.concatenate(
        [g_query, gains, g_bias[None], g_scale[None], small, jnp.zeros((5, local_width), F32)], 0
    )
    g_qkv, packed, g_proj = (summed(part) for part in (g_qkv, packed, g_proj))
    g_query = packed[:states]
    gains = packed[states : states + 8].reshape(2, width)
    g_attn_gain, g_mlp_gain = gains[0], gains[1]
    g_bias, g_scale = packed[states + 8], packed[states + 9]
    g_rel = packed[states + 10, : buckets * heads].reshape(buckets, heads)
    return (
        jnp.stack(out),
        jnp.stack(grad_x),
        jnp.stack(state_after)[:, None],
        g_attn_gain,
        g_mlp_gain,
        g_qkv,
        g_out,
        g_rel,
        g_query,
        g_proj,
        g_bias,
        g_scale,
        g_up,
        g_down,
    )


def solution(mesh):
    return jax.shard_map(
        body,
        mesh=mesh,
        in_specs=(
            P(None, ("blk", "head"), None),
            P(None, ("blk", "head"), None),
            P(None, "blk"),
            P(),
            P(),
            P(None, None, "head"),
            P("head", None),
            P(None, "head"),
            P(None, "head"),
            P("head", None, None),
            P("head"),
            P("head"),
            P(None, "head"),
            P("head", None),
        ),
        out_specs=(
            P(None, ("blk", "head"), None),
            P(None, ("blk", "head"), None),
            P(None, "blk", None, "head"),
            P(),
            P(),
            P(None, None, "head"),
            P("head", None),
            P(None, "head"),
            P(None, "head"),
            P("head", None, None),
            P("head"),
            P("head"),
            P(None, "head"),
            P("head", None),
        ),
        check_vma=False,
    )
```

time: 1520 us -> 682 us (0.45)
  waiting for transfers between devices: 732 us -> 151 us
  other arithmetic: 357 us -> 98 us
  blocking collectives: 130 us -> 0 us
  starting transfers between devices: 17.2 us -> 106 us
  Pallas kernels: 0 us -> 71.6 us
  matrix products: 139 us -> 101 us
  local copies, waits for them, and re-layouts: 102 us -> 123 us
    all_gather x16 -> x0, waiting for transfers between devices: 580 us -> none  [the longest x4 254 us: carried_in(): everything = jax.tree.map(lambda part: lax.all_gather(part, axis), shard)]
    reduce_scatter x8 -> x0, waiting for transfers between devices: 145 us -> none  [the longest x4 99.7 us: reduce_rows(): lax.psum_scatter(term(jnp.int32(0), rows * lax.axis_size('head')), 'head'...]
    psum x2 -> x0, blocking collectives: 130 us -> none  [the longest x1 66 us: body(): lax.psum((g_attn_gain, g_mlp_gain), ('blk', 'head'))]
    psum x1, waiting for transfers between devices: 0.01 us -> 110 us  [summed(): return lax.psum(values.astype(BF), 'blk').astype(F32)]
    select_n x64 -> x0, other arithmetic: 106 us -> none  [turn(): return jax.tree.map(lambda a, b: jnp.where(reached, a, b), new, before)]
    add x76 -> x12, other arithmetic: 105 us -> 3.3 us  [the longest x2 1.21 us: body(): update_lse.append(top + jnp.log(total))]
    ppermute x4 -> x70, starting transfers between devices: 16.2 us -> 106 us  [the longest x32 83.5 us: to_left(): return lax.ppermute(values, 'head', ring(3))]
    pallas_call x0 -> x2, Pallas kernels: none -> 71.6 us  [the longest x1 40.1 us: state_scan_back(): pl.pallas_call(functools.partial(scan_back_kernel, count), out_shape=shap...]
  transfers between devices with their start and end apart: 29 -> 71, of which waited for: 27 -> 18; matrix products, arithmetic and copies ran while one was open for 12% -> 34% of each run, Pallas kernels for 0% -> 5%
where the time goes in v1:
time: 682 us; the launch traced here: 670 us
  waiting for transfers between devices  151 us (22%)
  local copies, waits for them, and re-layouts  123 us (18%)
  starting transfers between devices  106 us (16%)
  matrix products  101 us (15%)
  other arithmetic  98 us (14%)
  Pallas kernels  71.6 us (10%)
  between operations  19.7 us (3%)
    psum x1, waiting for transfers between devices, summed(): return lax.psum(values.astype(BF), 'blk').astype(F32)  110 us
    ppermute x32, starting transfers between devices, to_left(): return lax.ppermute(values, 'head', ring(3))  83.5 us
    unnamed x536, local copies, waits for them, and re-layouts  52.2 us
    ppermute x32, waiting for transfers between devices, to_right(): return lax.ppermute(values, 'head', ring(1))  41 us
    pallas_call x1, Pallas kernels, state_scan_back(): pl.pallas_call(functools.partial(scan_back_kernel, count), out_shape=shap...  40.1 us
    dot_general x20, matrix products, dot(): return lax.dot_general(a, b, (dims, ((), ())), preferred_element_type=F32)  38.9 us
    pallas_call x1, Pallas kernels, state_scan(): pl.pallas_call(functools.partial(scan_kernel, count), out_shape=(shape, s...  31.5 us
    another operation x36, other arithmetic  19.7 us
  transfers between devices with their start and end apart: 71, of which 18 were waited for; matrix products, arithmetic and copies ran while one was open for 34% of the time, Pallas kernels for 5%

profile of v1, /device:TPU:1, one launch (start us, length us, event | category | flops | bytes accessed | tf_op | source)
XLA Modules:
  0.0 670.1 jit_solution(95334735270436923)
XLA Ops:
  10.5 3.6 collective-permute-start
  68.7 6.6 collective-permute-start.4
  80.0 3.0 collective-permute-start.8
  96.5 2.9 bitcast_reduce_fusion
  101.4 3.0 collective-permute-start.21
  117.6 31.5 %state_scan.1 = (bf16[2,32,16,256]{3,2,1,0:T(8,128)(2,1)}, bf16[2,32,16,256]{3,2,1,0:T(8,128)(2,1)}, f32[32,8,256]{2,1,0:T(8,128)}) custom-call(f32[8,256]{1,0:T(8,128)} %scatter.8.own_keep, bf16[2,32,16,256]{3,2,1,0:T(8,128)(2,1)} %pad_maximum_fusion.7.unit, f32[1,256]{1,0:T(1,128)} %bitcast.584, f32[1,256]{1,0:T(1,128)} %bitcast.588), custom_call_target="tpu_custom_call" | custom-call | tf_op jit(solution)/shard_map/state_scan/pallas_call | solution.py:200
  156.6 3.3 multiply_reduce_fusion.6
  175.0 3.4 collective-permute-start.11
  188.0 3.6 fusion.299
  204.9 3.5 collective-permute-done.48
  215.7 4.1 collective-permute-done.23
  225.3 5.8 collective-permute-done.14
  231.3 2.9 collective-permute-start.16
  239.4 3.0 collective-permute-start.19
  252.1 3.1 collective-permute-start.41
  257.3 3.9 collective-permute-done.39
  289.7 4.2 multiply_reduce_fusion.1
  304.4 2.8 collective-permute-start.32
  316.4 3.8 fusion.27
  347.8 3.8 fusion.24
  351.6 4.8 collective-permute-done.56
  357.2 3.1 collective-permute-start.58
  369.8 4.2 multiply_reduce_fusion
  381.6 40.1 %state_scan_back.1 = bf16[2,32,16,256]{3,2,1,0:T(8,128)(2,1)} custom-call(f32[32,8,256]{2,1,0:T(8,128)} %get-tuple-element.30.keep, bf16[2,32,16,256]{3,2,1,0:T(8,128)(2,1)} %pad_maximum_fusion.13.grads, bf16[2,32,16,256]{3,2,1,0:T(8,128)(2,1)} %get-tuple-element.31.across, f32[1,256]{1,0:T(1,128)} %bitcast.585, f32[1,256]{1,0:T(1,128)} %bitcast.589), custom_call_target="tpu_custom_call" | custom-call | tf_op jit(solution)/shard_map/state_scan_back/pallas_call | solution.py:216
  427.6 7.4 %fusion.282 = (f32[2]{0:T(128)S(1)}, f32[2,512,1024]{2,1,0:T(8,128)S(1)}, f32[2]{0:T(128)S(1)}, f32[2,512,1024]{2,1,0:T(8,128)}) fusion(f32[2,512,1024]{2,1,0:T(8,128)} %get-tuple-element.458, f32[2,512]{1,0:T(2,128)S(1)} %copy-done.185, f32[2,512,1024]{2,1,0:T(8,128)} %copy-done.5, f32[2,512]{1,0:T(2,128)S(1)} %get-tuple-element.196, ...), kind=kLoop, calls=%fused_computation.743 | loop fusion | flops 8388604 | bytes 25182224 | tf_op jit(solution)/shard_map/reduce_sum | solution.py:466
  488.8 3.5 collective-permute-start.66
  500.1 3.0 collective-permute-start.62
  506.0 5.6 collective-permute-done.60
  517.2 3.7 collective-permute-start.69
  520.9 4.5 convolution_convert_fusion
  536.9 109.6 %all-reduce.7.cloned.1.call-done = (bf16[528,256]{1,0:T(8,128)(2,1)}, bf16[1024,3,256]{2,0,1:T(8,128)(2,1)}, bf16[256,1024]{1,0:T(8,128)(2,1)}, bf16[2,128,256]{...) async-done(((bf16[528,256]{1,0:T(8,128)(2,1)}, bf16[1024,3,256]{2,0,1:T(8,128)(2,1)}, bf16[256,1024]{1,0:T(8,128)(2,1)}, ...) | async-done | bytes 6692880 | tf_op jit(solution)/shard_map/psum | solution.py:434
  650.6 4.2 convert_element_type.5407
  (952 shorter events, 354.6 us)
Async XLA Ops:
  7.2 639.2 %all-reduce.7.cloned.1.call-start = ((), (), s32[]{:S(2)}) async-start(), calls=%async_computation | async-start | bytes 13385728 | tf_op jit(solution)/shard_map/psum | solution.py:434
  10.5 23.6 %collective-permute-start = (bf16[128,1024]{1,0:T(8,128)(2,1)}, bf16[128,1024]{1,0:T(8,128)(2,1)}, u32[]{:S(2)}, u32[]{:S(2)}) collective-permute-start(bf16[128,1024]{1,0:T(8,128)(2,1)} %get-tuple-element.190), channel_id=1, source_target_pairs={{0,3},{1,0},{2,1},{3,2},{4,7},{5,4},{6,5},{7,6},{8,11},{9,8},{10,9... | collective-permute-start | bytes 786440 | tf_op jit(solution)/shard_map/ppermute | solution.py:53
  14.1 12.1 %collective-permute-start.1 = (bf16[128,1024]{1,0:T(8,128)(2,1)}, bf16[128,1024]{1,0:T(8,128)(2,1)S(1)}, u32[]{:S(2)}, u32[]{:S(2)}) collective-permute-start(bf16[128,1024]{1,0:T(8,128)(2,1)} %get-tuple-element.190), channel_id=1, source_target_pairs={{0,1},{1,2},{2,3},{3,0},{4,5},{5,6},{6,7},{7,4},{8,9},{9,10},{10,1... | collective-permute-start | bytes 786440 | tf_op jit(solution)/shard_map/ppermute | solution.py:49
  16.0 186.2 %collective-permute-start.35 = (bf16[128,1024]{1,0:T(8,128)(2,1)}, bf16[128,1024]{1,0:T(8,128)(2,1)}, u32[]{:S(2)}, u32[]{:S(2)}) collective-permute-start(bf16[128,1024]{1,0:T(8,128)(2,1)} %get-tuple-element.272), channel_id=1, source_target_pairs={{0,1},{1,2},{2,3},{3,0},{4,5},{5,6},{6,7},{7,4},{8,9},{9,10},{10,1... | collective-permute-start | bytes 786440 | tf_op jit(solution)/shard_map/ppermute | solution.py:49
  16.0 188.9 %collective-permute-start.34 = (bf16[128,1024]{1,0:T(8,128)(2,1)}, bf16[128,1024]{1,0:T(8,128)(2,1)}, u32[]{:S(2)}, u32[]{:S(2)}) collective-permute-start(bf16[128,1024]{1,0:T(8,128)(2,1)} %get-tuple-element.272), channel_id=1, source_target_pairs={{0,3},{1,0},{2,1},{3,2},{4,7},{5,4},{6,5},{7,6},{8,11},{9,8},{10,9... | collective-permute-start | bytes 786440 | tf_op jit(solution)/shard_map/ppermute | solution.py:53
  27.4 12.2 %collective-permute-start.2 = (bf16[64,1024]{1,0:T(8,128)(2,1)S(1)}, bf16[64,1024]{1,0:T(8,128)(2,1)S(1)}, u32[]{:S(2)}, u32[]{:S(2)}) collective-permute-start(bf16[64,1024]{1,0:T(8,128)(2,1)S(1)} %slice.750), channel_id=1, source_target_pairs={{0,1},{1,2},{2,3},{3,0},{4,5},{5,6},{6,7},{7,4},{8,9},{9,10},{10,1... | collective-permute-start | bytes 393224 | tf_op jit(solution)/shard_map/ppermute | solution.py:49
  42.9 36.1 %collective-permute-start.5 = (bf16[128,1024]{1,0:T(8,128)(2,1)}, bf16[128,1024]{1,0:T(8,128)(2,1)}, u32[]{:S(2)}, u32[]{:S(2)}) collective-permute-start(bf16[128,1024]{1,0:T(8,128)(2,1)} %get-tuple-element.188), channel_id=1, source_target_pairs={{0,3},{1,0},{2,1},{3,2},{4,7},{5,4},{6,5},{7,6},{8,11},{9,8},{10,9... | collective-permute-start | bytes 786440 | tf_op jit(solution)/shard_map/ppermute | solution.py:53
  45.4 10.9 %collective-permute-start.6 = (bf16[128,1024]{1,0:T(8,128)(2,1)}, bf16[128,1024]{1,0:T(8,128)(2,1)}, u32[]{:S(2)}, u32[]{:S(2)}) collective-permute-start(bf16[128,1024]{1,0:T(8,128)(2,1)} %get-tuple-element.188), channel_id=1, source_target_pairs={{0,1},{1,2},{2,3},{3,0},{4,5},{5,6},{6,7},{7,4},{8,9},{9,10},{10,1... | collective-permute-start | bytes 786440 | tf_op jit(solution)/shard_map/ppermute | solution.py:49
  57.8 27.0 %collective-permute-start.7 = (bf16[64,1024]{1,0:T(8,128)(2,1)}, bf16[64,1024]{1,0:T(8,128)(2,1)S(1)}, u32[]{:S(2)}, u32[]{:S(2)}) collective-permute-start(bf16[64,1024]{1,0:T(8,128)(2,1)} %slice.760), channel_id=1, source_target_pairs={{0,1},{1,2},{2,3},{3,0},{4,5},{5,6},{6,7},{7,4},{8,9},{9,10},{10,1... | collective-permute-start | bytes 393224 | tf_op jit(solution)/shard_map/ppermute | solution.py:49
  68.7 96.8 %collective-permute-start.4 = (bf16[512,2,2,128]{3,0,2,1:T(8,128)(2,1)}, bf16[512,2,2,128]{3,0,2,1:T(8,128)(2,1)}, u32[]{:S(2)}, u32[]{:S(2)}) collective-permute-start(bf16[512,2,2,128]{3,0,2,1:T(8,128)(2,1)} %copy.398), channel_id=1, source_target_pairs={{0,4},{4,8},{8,12},{12,16},{16,20},{20,24},{24,28},{28,32},{32,36}... | collective-permute-start | bytes 1572872 | tf_op jit(solution)/shard_map/ppermute | solution.py:88
  101.4 85.4 %collective-permute-start.21 = (bf16[512,2,2,128]{3,0,2,1:T(8,128)(2,1)}, bf16[512,2,2,128]{3,0,2,1:T(8,128)(2,1)}, u32[]{:S(2)}, u32[]{:S(2)}) collective-permute-start(bf16[512,2,2,128]{3,0,2,1:T(8,128)(2,1)} %copy.404), channel_id=1, source_target_pairs={{0,4},{4,8},{8,12},{12,16},{16,20},{20,24},{24,28},{28,32},{32,36}... | collective-permute-start | bytes 1572872 | tf_op jit(solution)/shard_map/ppermute | solution.py:88
  182.8 28.5 %collective-permute-start.47 = (bf16[128,1024]{1,0:T(8,128)(2,1)}, bf16[128,1024]{1,0:T(8,128)(2,1)S(1)}, u32[]{:S(2)}, u32[]{:S(2)}) collective-permute-start(bf16[128,1024]{1,0:T(8,128)(2,1)} %get-tuple-element.271), channel_id=1, source_target_pairs={{0,3},{1,0},{2,1},{3,2},{4,7},{5,4},{6,5},{7,6},{8,11},{9,8},{10,9... | collective-permute-start | bytes 786440 | tf_op jit(solution)/shard_map/ppermute | solution.py:53
  202.0 12.3 %collective-permute-start.10 = (bf16[128,1024]{1,0:T(8,128)(2,1)S(1)}, bf16[128,1024]{1,0:T(8,128)(2,1)S(1)}, u32[]{:S(2)}, u32[]{:S(2)}) collective-permute-start(bf16[128,1024]{1,0:T(8,128)(2,1)S(1)} %pad_maximum_fusion.27), channel_id=1, source_target_pairs={{0,1},{1,2},{2,3},{3,0},{4,5},{5,6},{6,7},{7,4},{8,9},{9,10},{10,1... | collective-permute-start | bytes 786440 | tf_op jit(solution)/shard_map/ppermute | solution.py:49
  202.2 12.6 %collective-permute-start.12 = (bf16[128,1024]{1,0:T(8,128)(2,1)S(1)}, bf16[128,1024]{1,0:T(8,128)(2,1)S(1)}, u32[]{:S(2)}, u32[]{:S(2)}) collective-permute-start(bf16[128,1024]{1,0:T(8,128)(2,1)S(1)} %pad_maximum_fusion.28), channel_id=1, source_target_pairs={{0,3},{1,0},{2,1},{3,2},{4,7},{5,4},{6,5},{7,6},{8,11},{9,8},{10,9... | collective-permute-start | bytes 786440 | tf_op jit(solution)/shard_map/ppermute | solution.py:53
  204.9 15.0 %collective-permute-start.23 = (bf16[128,1024]{1,0:T(8,128)(2,1)S(1)}, bf16[128,1024]{1,0:T(8,128)(2,1)S(1)}, u32[]{:S(2)}, u32[]{:S(2)}) collective-permute-start(bf16[128,1024]{1,0:T(8,128)(2,1)S(1)} %pad_maximum_fusion.31), channel_id=1, source_target_pairs={{0,1},{1,2},{2,3},{3,0},{4,5},{5,6},{6,7},{7,4},{8,9},{9,10},{10,1... | collective-permute-start | bytes 786440 | tf_op jit(solution)/shard_map/ppermute | solution.py:49
  208.4 11.5 %collective-permute-start.25 = (bf16[128,1024]{1,0:T(8,128)(2,1)S(1)}, bf16[128,1024]{1,0:T(8,128)(2,1)S(1)}, u32[]{:S(2)}, u32[]{:S(2)}) collective-permute-start(bf16[128,1024]{1,0:T(8,128)(2,1)S(1)} %pad_maximum_fusion.32), channel_id=1, source_target_pairs={{0,3},{1,0},{2,1},{3,2},{4,7},{5,4},{6,5},{7,6},{8,11},{9,8},{10,9... | collective-permute-start | bytes 786440 | tf_op jit(solution)/shard_map/ppermute | solution.py:53
  211.3 11.3 %collective-permute-start.36 = (bf16[64,1024]{1,0:T(8,128)(2,1)S(1)}, bf16[64,1024]{1,0:T(8,128)(2,1)S(1)}, u32[]{:S(2)}, u32[]{:S(2)}) collective-permute-start(bf16[64,1024]{1,0:T(8,128)(2,1)S(1)} %slice.804), channel_id=1, source_target_pairs={{0,1},{1,2},{2,3},{3,0},{4,5},{5,6},{6,7},{7,4},{8,9},{9,10},{10,1... | collective-permute-start | bytes 393224 | tf_op jit(solution)/shard_map/ppermute | solution.py:49
  214.7 55.8 %collective-permute-start.49 = (bf16[64,1024]{1,0:T(8,128)(2,1)S(1)}, bf16[64,1024]{1,0:T(8,128)(2,1)S(1)}, u32[]{:S(2)}, u32[]{:S(2)}) collective-permute-start(bf16[64,1024]{1,0:T(8,128)(2,1)S(1)} %slice.819), channel_id=1, source_target_pairs={{0,1},{1,2},{2,3},{3,0},{4,5},{5,6},{6,7},{7,4},{8,9},{9,10},{10,1... | collective-permute-start | bytes 393224 | tf_op jit(solution)/shard_map/ppermute | solution.py:49
  255.8 14.8 %collective-permute-start.50 = (bf16[64,1024]{1,0:T(8,128)(2,1)S(1)}, bf16[64,1024]{1,0:T(8,128)(2,1)S(1)}, u32[]{:S(2)}, u32[]{:S(2)}) collective-permute-start(bf16[64,1024]{1,0:T(8,128)(2,1)S(1)} %slice.820), channel_id=1, source_target_pairs={{0,3},{1,0},{2,1},{3,2},{4,7},{5,4},{6,5},{7,6},{8,11},{9,8},{10,9... | collective-permute-start | bytes 393224 | tf_op jit(solution)/shard_map/ppermute | solution.py:53
  266.8 11.0 %collective-permute-start.26 = (bf16[128,1024]{1,0:T(8,128)(2,1)S(1)}, bf16[128,1024]{1,0:T(8,128)(2,1)S(1)}, u32[]{:S(2)}, u32[]{:S(2)}) collective-permute-start(bf16[128,1024]{1,0:T(8,128)(2,1)S(1)} %get-tuple-element.345), channel_id=1, source_target_pairs={{0,3},{1,0},{2,1},{3,2},{4,7},{5,4},{6,5},{7,6},{8,11},{9,8},{10,9... | collective-permute-start | bytes 786440 | tf_op jit(solution)/shard_map/ppermute | solution.py:53
  277.7 18.8 %collective-permute-start.28 = (bf16[64,1024]{1,0:T(8,128)(2,1)}, bf16[64,1024]{1,0:T(8,128)(2,1)}, u32[]{:S(2)}, u32[]{:S(2)}) collective-permute-start(bf16[64,1024]{1,0:T(8,128)(2,1)} %slice.795), channel_id=1, source_target_pairs={{0,1},{1,2},{2,3},{3,0},{4,5},{5,6},{6,7},{7,4},{8,9},{9,10},{10,1... | collective-permute-start | bytes 393224 | tf_op jit(solution)/shard_map/ppermute | solution.py:49
  278.4 19.8 %collective-permute-start.29 = (bf16[64,1024]{1,0:T(8,128)(2,1)}, bf16[64,1024]{1,0:T(8,128)(2,1)}, u32[]{:S(2)}, u32[]{:S(2)}) collective-permute-start(bf16[64,1024]{1,0:T(8,128)(2,1)} %slice.796), channel_id=1, source_target_pairs={{0,3},{1,0},{2,1},{3,2},{4,7},{5,4},{6,5},{7,6},{8,11},{9,8},{10,9... | collective-permute-start | bytes 393224 | tf_op jit(solution)/shard_map/ppermute | solution.py:53
  304.4 23.3 %collective-permute-start.30 = (bf16[64,1024]{1,0:T(8,128)(2,1)}, bf16[64,1024]{1,0:T(8,128)(2,1)}, u32[]{:S(2)}, u32[]{:S(2)}) collective-permute-start(bf16[64,1024]{1,0:T(8,128)(2,1)} %get-tuple-element.236), channel_id=1, source_target_pairs={{0,1},{1,2},{2,3},{3,0},{4,5},{5,6},{6,7},{7,4},{8,9},{9,10},{10,1... | collective-permute-start | bytes 393224 | tf_op jit(solution)/shard_map/ppermute | solution.py:49
  304.4 23.3 %collective-permute-start.32 = (bf16[64,1024]{1,0:T(8,128)(2,1)}, bf16[64,1024]{1,0:T(8,128)(2,1)}, u32[]{:S(2)}, u32[]{:S(2)}) collective-permute-start(bf16[64,1024]{1,0:T(8,128)(2,1)} %get-tuple-element.237), channel_id=1, source_target_pairs={{0,3},{1,0},{2,1},{3,2},{4,7},{5,4},{6,5},{7,6},{8,11},{9,8},{10,9... | collective-permute-start | bytes 393224 | tf_op jit(solution)/shard_map/ppermute | solution.py:53
  313.8 20.0 %collective-permute-start.51 = (bf16[64,1024]{1,0:T(8,128)(2,1)}, bf16[64,1024]{1,0:T(8,128)(2,1)}, u32[]{:S(2)}, u32[]{:S(2)}) collective-permute-start(bf16[64,1024]{1,0:T(8,128)(2,1)} %get-tuple-element.218), channel_id=1, source_target_pairs={{0,1},{1,2},{2,3},{3,0},{4,5},{5,6},{6,7},{7,4},{8,9},{9,10},{10,1... | collective-permute-start | bytes 393224 | tf_op jit(solution)/shard_map/ppermute | solution.py:49
  313.8 20.0 %collective-permute-start.53 = (bf16[64,1024]{1,0:T(8,128)(2,1)}, bf16[64,1024]{1,0:T(8,128)(2,1)}, u32[]{:S(2)}, u32[]{:S(2)}) collective-permute-start(bf16[64,1024]{1,0:T(8,128)(2,1)} %get-tuple-element.219), channel_id=1, source_target_pairs={{0,3},{1,0},{2,1},{3,2},{4,7},{5,4},{6,5},{7,6},{8,11},{9,8},{10,9... | collective-permute-start | bytes 393224 | tf_op jit(solution)/shard_map/ppermute | solution.py:53
  344.9 12.3 %collective-permute-start.55 = (bf16[128,1024]{1,0:T(8,128)(2,1)S(1)}, bf16[128,1024]{1,0:T(8,128)(2,1)S(1)}, u32[]{:S(2)}, u32[]{:S(2)}) collective-permute-start(bf16[128,1024]{1,0:T(8,128)(2,1)S(1)} %get-tuple-element.182), channel_id=1, source_target_pairs={{0,3},{1,0},{2,1},{3,2},{4,7},{5,4},{6,5},{7,6},{8,11},{9,8},{10,9... | collective-permute-start | bytes 786440 | tf_op jit(solution)/shard_map/ppermute | solution.py:53
  443.3 40.0 %collective-permute-start.63 = (bf16[512,2,2,128]{0,3,2,1:T(8,128)(2,1)S(1)}, bf16[512,2,2,128]{0,3,2,1:T(8,128)(2,1)S(1)}, u32[]{:S(2)}, u32[]{:S(2)}) collective-permute-start(bf16[512,2,2,128]{0,3,2,1:T(8,128)(2,1)S(1)} %pad_maximum_fusion.14), channel_id=1, source_target_pairs={{4,0},{8,4},{12,8},{16,12},{20,16},{24,20},{28,24},{32,28},{36,32}... | collective-permute-start | bytes 1572872 | tf_op jit(solution)/shard_map/ppermute | solution.py:88
  448.8 32.7 %collective-permute-start.46 = (bf16[512,2,2,128]{0,3,2,1:T(8,128)(2,1)S(1)}, bf16[512,2,2,128]{0,3,2,1:T(8,128)(2,1)S(1)}, u32[]{:S(2)}, u32[]{:S(2)}) collective-permute-start(bf16[512,2,2,128]{0,3,2,1:T(8,128)(2,1)S(1)} %pad_maximum_fusion.10), channel_id=1, source_target_pairs={{4,0},{8,4},{12,8},{16,12},{20,16},{24,20},{28,24},{32,28},{36,32}... | collective-permute-start | bytes 1572872 | tf_op jit(solution)/shard_map/ppermute | solution.py:88
  499.6 11.9 %collective-permute-start.60 = (bf16[128,1024]{1,0:T(8,128)(2,1)S(1)}, bf16[128,1024]{1,0:T(8,128)(2,1)S(1)}, u32[]{:S(2)}, u32[]{:S(2)}) collective-permute-start(bf16[128,1024]{1,0:T(8,128)(2,1)S(1)} %pad_maximum_fusion.39), channel_id=1, source_target_pairs={{0,1},{1,2},{2,3},{3,0},{4,5},{5,6},{6,7},{7,4},{8,9},{9,10},{10,1... | collective-permute-start | bytes 786440 | tf_op jit(solution)/shard_map/ppermute | solution.py:49
  500.1 11.5 %collective-permute-start.62 = (bf16[128,1024]{1,0:T(8,128)(2,1)S(1)}, bf16[128,1024]{1,0:T(8,128)(2,1)S(1)}, u32[]{:S(2)}, u32[]{:S(2)}) collective-permute-start(bf16[128,1024]{1,0:T(8,128)(2,1)S(1)} %pad_maximum_fusion.40), channel_id=1, source_target_pairs={{0,3},{1,0},{2,1},{3,2},{4,7},{5,4},{6,5},{7,6},{8,11},{9,8},{10,9... | collective-permute-start | bytes 786440 | tf_op jit(solution)/shard_map/ppermute | solution.py:53
  517.2 10.8 %collective-permute-start.69 = (f32[8,256]{1,0:T(8,128)S(1)}, f32[8,256]{1,0:T(8,128)S(1)}, u32[]{:S(2)}, u32[]{:S(2)}) collective-permute-start(f32[8,256]{1,0:T(8,128)S(1)} %add.5757), channel_id=1, source_target_pairs={{0,2},{1,3},{2,0},{3,1},{4,6},{5,7},{6,4},{7,5},{8,10},{9,11},{10,... | collective-permute-start | bytes 24584 | tf_op jit(solution)/shard_map/ppermute | solution.py:583
  (279 other events, 2482.1 us)
Sparse Core Ops, SparseCore 0:
  530.2 116.2 all-reduce.6

commit v2 on v0

v2 whole, which is shorter than its diff:
```python
import functools
import math

import jax
import jax.numpy as jnp
from jax import lax
from jax.experimental import pallas as pl
from jax.experimental.pallas import tpu as pltpu
from jax.sharding import PartitionSpec as P

BUCKETS = 32
MAXDIST = 128
EPSILON = 1e-06
MASKED = -1e30
TILE = 128
MESH = pl.DeviceIdType.MESH
BF = jnp.bfloat16
F32 = jnp.float32
VMEM = pl.BlockSpec(memory_space=pltpu.VMEM)
SMEM = pl.BlockSpec(memory_space=pltpu.SMEM)
LIMIT = 56 * 2**20
ROOT = math.sqrt(2.0 / math.pi)
CUBIC = 0.044715


def bucket_starts():
    exact = BUCKETS // 2
    levels = [
        int(math.ceil(exact * (MAXDIST / exact) ** (t / (BUCKETS - exact))))
        for t in range(1, BUCKETS - exact)
    ]
    return list(range(exact + 1)) + levels


STARTS = bucket_starts()


def nn(a, b):
    return lax.dot_general(a, b, (((1,), (0,)), ((), ())), preferred_element_type=F32)


def nt(a, b):
    return lax.dot_general(a, b, (((1,), (1,)), ((), ())), preferred_element_type=F32)


def tn(a, b):
    return lax.dot_general(a, b, (((0,), (0,)), ((), ())), preferred_element_type=F32)


def inverse_rms(values):
    return lax.rsqrt(jnp.mean(values * values, axis=-1, keepdims=True) + EPSILON)


def tile_of(index, size=TILE):
    return pl.ds(pl.multiple_of(index * size, size), size)


def loop(count, step):
    def run(i, c):
        step(i)
        return c

    lax.fori_loop(0, count, run, 0)


def remote(src, dst, send_sem, recv_sem, device):
    return pltpu.make_async_remote_copy(
        src_ref=src,
        dst_ref=dst,
        send_sem=send_sem,
        recv_sem=recv_sem,
        device_id=device,
        device_id_type=MESH,
    )


class Ring:
    def __init__(self, send, recv):
        self.me = lax.axis_index("head")
        self.right = lax.rem(self.me + 1, 4)
        self.left = lax.rem(self.me + 3, 4)
        self.send, self.recv, self.used = send, recv, 0

    def greet(self):
        barrier = pltpu.get_barrier_semaphore()
        for peer in (self.right, self.left):
            pl.semaphore_signal(barrier, inc=1, device_id={"head": peer}, device_id_type=MESH)
        return 2

    def go(self, src, dst, peer):
        copy = remote(
            src, dst, self.send.at[self.used], self.recv.at[self.used], {"head": peer}
        )
        self.used += 1
        copy.start()
        return copy

    def row_chunk(self, k):
        return tile_of(lax.rem(self.me + k, 4))


class Gather:
    def __init__(self, ring, buf):
        self.ring, self.buf = ring, buf
        self.half = buf.shape[1] // 2

    def start(self):
        r, b, h = self.ring, self.buf, self.half
        self.a0 = r.go(b.at[0, :h], b.at[3, :h], r.right)
        self.b0 = r.go(b.at[0, h:], b.at[1, h:], r.left)
        self.a1 = r.go(b.at[0, h:], b.at[3, h:], r.right)
        self.b1 = r.go(b.at[0, :h], b.at[1, :h], r.left)

    def relay(self):
        r, b, h = self.ring, self.buf, self.half
        self.a0.wait_recv()
        self.a2 = r.go(b.at[3, :h], b.at[2, :h], r.right)
        self.b0.wait_recv()
        self.b2 = r.go(b.at[1, h:], b.at[2, h:], r.left)

    def finish(self):
        for copy in (self.a1, self.b1, self.a2, self.b2):
            copy.wait_recv()

    def close(self):
        for copy in (self.a0, self.b0, self.a1, self.b1, self.a2, self.b2):
            copy.wait_send()


class Reduce:
    def __init__(self, ring, terms, mid, into):
        self.ring, self.terms, self.mid, self.into = ring, terms, mid, into
        self.half = terms.shape[1] // 2

    def start(self):
        r, t, h = self.ring, self.terms, self.half
        self.a0 = r.go(t.at[2, :h], self.mid.at[0], r.right)
        self.b0 = r.go(t.at[2, h:], self.mid.at[1], r.left)
        self.a1 = r.go(t.at[1, h:], self.into.at[0, h:], r.right)
        self.b1 = r.go(t.at[3, :h], self.into.at[1, :h], r.left)

    def relay(self):
        r, t, h, mid = self.ring, self.terms, self.half, self.mid
        self.a0.wait_recv()
        mid[2] = (mid[0].astype(F32) + t[1, :h].astype(F32)).astype(BF)
        self.a2 = r.go(mid.at[2], self.into.at[0, :h], r.right)
        self.b0.wait_recv()
        mid[3] = (mid[1].astype(F32) + t[3, h:].astype(F32)).astype(BF)
        self.b2 = r.go(mid.at[3], self.into.at[1, h:], r.left)

    def finish(self):
        for copy in (self.a1, self.b1, self.a2, self.b2):
            copy.wait_recv()
        return (
            self.terms[0].astype(F32) + self.into[0].astype(F32) + self.into[1].astype(F32)
        )

    def close(self):
        for copy in (self.a0, self.b0, self.a1, self.b1, self.a2, self.b2):
            copy.wait_send()


class Exchange:
    def __init__(self, source, target, send, recv, local):
        self.count = lax.axis_size("blk")
        self.place = lax.axis_index("blk")
        self.size = source.shape[0] // self.count
        self.source, self.target = source, target
        self.send, self.recv, self.local = send, recv, local

    def part(self, j):
        peer = lax.rem(self.place + j, self.count)
        return remote(
            self.source.at[tile_of(peer, self.size)],
            self.target.at[tile_of(self.place, self.size)],
            self.send.at[j],
            self.recv.at[j],
            {"blk": peer},
        )

    def own(self):
        rows = tile_of(self.place, self.size)
        return pltpu.make_async_copy(self.source.at[rows], self.target.at[rows], self.local)

    def start(self):
        loop(self.count - 1, lambda j: self.part(j + 1).start())
        self.own().start()

    def finish(self):
        self.own().wait()
        loop(self.count - 1, lambda j: self.part(j + 1).wait_recv())

    def close(self):
        loop(self.count - 1, lambda j: self.part(j + 1).wait_send())


def greet_blocks():
    barrier = pltpu.get_barrier_semaphore()
    count, place = lax.axis_size("blk"), lax.axis_index("blk")

    def greet(j):
        pl.semaphore_signal(
            barrier, inc=1, device_id={"blk": lax.rem(place + j + 1, count)}, device_id_type=MESH
        )

    loop(count - 1, greet)
    return count - 1


def front_kernel(x, gain, w, whole, qkv, send, recv):
    ring = Ring(send, recv)
    pl.semaphore_wait(pltpu.get_barrier_semaphore(), ring.greet())
    gathers = []
    for m in range(2):
        rows = x[m].astype(F32)
        whole[m, 0] = (rows * inverse_rms(rows) * gain[...]).astype(BF)
        gathers.append(Gather(ring, whole.at[m]))
        gathers[m].start()
    for m in range(2):
        gathers[m].relay()
    for m in range(2):
        gathers[m].finish()

        def columns(n, m=m):
            cols = tile_of(n, 256)
            part = nn(whole[m].reshape(512, 1024), w[:, cols]).astype(BF)
            for k in range(4):
                qkv[m, ring.row_chunk(k), cols] = part[k * TILE : (k + 1) * TILE]

        loop(3, columns)
    for m in range(2):
        gathers[m].close()


def closed_row(closed, qi):
    column = lax.broadcasted_iota(jnp.int32, closed.shape, 1) + qi * TILE
    return jnp.where(column < 512, closed, 0.0)


def head(h, size=TILE, base=0):
    return slice(base + h * size, base + (h + 1) * size)


def memory_kernel(
    qkv, state_query, state_proj, bias, slope, own_keep, closed, rel, g,
    prior, across, keeps, update, update_lse, state_after, kv_all, state_kv, attended, lse, table, whole_grad,
    unit_low, held, send, recv, s0, r0, s1, r1, s2, r2, s3, r3, local,
):
    scale = TILE**-0.5
    ring = Ring(send, recv)
    place, count = lax.axis_index("blk"), lax.axis_size("blk")
    pl.semaphore_wait(pltpu.get_barrier_semaphore(), ring.greet() + greet_blocks())
    gathers = []
    for m in range(2):
        whole_grad[m, 0] = g[m]
        gathers.append(Gather(ring, whole_grad.at[m]))
        gathers[m].start()
    after = {"blk": lax.rem(place + 1, count)}
    shifts = [
        remote(qkv.at[m, :, 256:768], kv_all.at[m, 0:512], s0.at[m], r0.at[m], after)
        for m in range(2)
    ]
    for copy in shifts:
        copy.start()

    def tell(j):
        return remote(
            own_keep, keeps.at[place], s3.at[j], r3.at[j], {"blk": lax.rem(place + j, count)}
        )

    loop(count - 1, lambda j: tell(j + 1).start())
    keeps[place] = own_keep[...]

    def update_tile(m):
        def step(t):
            rows = tile_of(t)
            for h in range(2):
                scores = nt(state_query[rows, head(h)], qkv[m, :, head(h, base=256)]) * scale
                top = jnp.max(scores, axis=-1, keepdims=True)
                raised = jnp.exp(scores - top)
                total = jnp.sum(raised, axis=-1, keepdims=True)
                update_lse[m, h, rows] = top + jnp.log(total)
                u = nn((raised / total).astype(BF), qkv[m, :, head(h, base=512)])
                update[m, rows, head(h)] = u
                unit_low[m, rows, head(h)] = (u * inverse_rms(u)).astype(BF)

        return step

    there = [
        Exchange(unit_low.at[m], across.at[m], s1.at[m], r1.at[m], local.at[m]) for m in range(2)
    ]
    back = [
        Exchange(held.at[m], prior.at[m], s2.at[m], r2.at[m], local.at[2 + m]) for m in range(2)
    ]
    for m in range(2):
        loop(4, update_tile(m))
        there[m].start()
    for m in range(2):
        gathers[m].relay()

    row = lax.broadcasted_iota(jnp.int32, (TILE, TILE), 0)
    col = lax.broadcasted_iota(jnp.int32, (TILE, TILE), 1)
    for h in range(2):
        far = jnp.full((TILE, TILE), rel[BUCKETS - 1, h], F32)
        table[h, :, 0:128] = jnp.where(row < col, far, MASKED)
        table[h, :, 128:256] = far
        table[h, :, 256:384] = far
        for shift, at in ((TILE, 384), (0, 512)):
            distance = row - col + shift
            total = jnp.full((TILE, TILE), rel[0, h], F32)
            for t in range(1, BUCKETS):
                total = jnp.where(distance >= STARTS[t], rel[t, h], total)
            table[h, :, at : at + TILE] = jnp.where(distance >= 0, total, MASKED)

    for m in range(2):
        kv_all[m, 512:1024] = qkv[m, :, 256:768]
    loop(count - 1, lambda j: tell(j + 1).wait_recv())
    for m in range(2):
        there[m].finish()

        def scan(b, state, m=m):
            rows = tile_of(b, 16)
            u = across[m, rows].astype(F32)
            forget = jax.nn.sigmoid(bias[...] + slope[...] * u)
            before = keeps[b, m : m + 1] * state
            held[m, rows] = before.astype(BF)
            return forget * before + (1.0 - forget) * u

        lax.fori_loop(0, count, scan, jnp.zeros((16, 256), F32))
        back[m].start()
    for m in range(2):
        back[m].finish()

        def state(t, m=m):
            rows = tile_of(t)
            before = prior[m, rows]
            for h in range(2):
                state_kv[m, rows, head(h, 256)] = nn(before[:, head(h)], state_proj[h]).astype(BF)
                u = update[m, rows, head(h)]
                u = u * inverse_rms(u)
                forget = jax.nn.sigmoid(bias[:, head(h)] + slope[:, head(h)] * u)
                state_after[m, rows, head(h)] = (
                    forget * before[:, head(h)].astype(F32) + (1.0 - forget) * u
                )

        loop(4, state)
        shifts[m].wait_recv()

        def attend(qi, m=m):
            rows = tile_of(qi)
            window = pl.ds(pl.multiple_of(qi * TILE, TILE), 5 * TILE)
            shut = closed_row(closed[m, 0:1], qi)
            for h in range(2):
                q = qkv[m, rows, head(h)]
                token = nt(q, kv_all[m, window, head(h)]) * scale + (table[h] + shut)
                from_state = nt(q, state_kv[m, :, h * 256 : h * 256 + TILE]) * scale
                top = jnp.maximum(
                    jnp.max(token, axis=-1, keepdims=True),
                    jnp.max(from_state, axis=-1, keepdims=True),
                )
                token = jnp.exp(token - top)
                from_state = jnp.exp(from_state - top)
                total = jnp.sum(token, axis=-1, keepdims=True) + jnp.sum(
                    from_state, axis=-1, keepdims=True
                )
                lse[m, h, rows] = top + jnp.log(total)
                out = nn(token.astype(BF), kv_all[m, window, head(h, base=256)]) + nn(
                    from_state.astype(BF), state_kv[m, :, h * 256 + TILE : (h + 1) * 256]
                )
                attended[m, rows, head(h)] = (out / total).astype(BF)

        loop(4, attend)
    for m in range(2):
        gathers[m].finish()
        gathers[m].close()
        shifts[m].wait_send()
        there[m].close()
        back[m].close()
    loop(count - 1, lambda j: tell(j + 1).wait_send())


def mlp_kernel(
    attended, x, g, whole_grad, w_out, w_up, w_down, gain,
    att_rel, middle, grad_middle, whole_gm, branch, g_up, g_down, g_gain,
    terms, whole_mlp, active, grad_hidden, grad_terms, mid, into, send, recv,
):
    ring = Ring(send, recv)
    pl.semaphore_wait(pltpu.get_barrier_semaphore(), ring.greet())
    first = [Reduce(ring, terms.at[m], mid.at[m], into.at[m]) for m in range(2)]
    for m in range(2):
        for k in range(4):
            att_rel[m, k] = attended[m, ring.row_chunk(k)]

        def columns(n, m=m):
            cols = tile_of(n, 256)
            part = nn(att_rel[m].reshape(512, 256), w_out[:, cols]).astype(BF)
            for k in range(4):
                terms[m, k, :, cols] = part[k * TILE : (k + 1) * TILE]

        loop(4, columns)
        first[m].start()
    for m in range(2):
        first[m].relay()
    second = [Gather(ring, whole_mlp.at[m]) for m in range(2)]
    for m in range(2):
        rows = x[m].astype(F32) + first[m].finish()
        middle[m] = rows
        whole_mlp[m, 0] = (rows * inverse_rms(rows) * gain[...]).astype(BF)
        second[m].start()
    for m in range(2):
        second[m].relay()
    third = [Reduce(ring, grad_terms.at[m], mid.at[2 + m], into.at[2 + m]) for m in range(2)]
    for m in range(2):
        second[m].finish()

        def hidden_columns(n, m=m):
            cols = tile_of(n, 256)
            hidden = nn(whole_mlp[m].reshape(512, 1024), w_up[:, cols])
            grad_active = nt(whole_grad[m].reshape(512, 1024), w_down[cols])
            square = hidden * hidden
            bent = jnp.tanh(ROOT * hidden * (1.0 + CUBIC * square))
            active[m, :, cols] = (0.5 * hidden * (1.0 + bent)).astype(BF)
            rise = 0.5 * (1.0 + bent) + 0.5 * hidden * (1.0 - bent * bent) * ROOT * (
                1.0 + 3.0 * CUBIC * square
            )
            grad_hidden[m, :, cols] = (grad_active * rise).astype(BF)

        loop(4, hidden_columns)

        def grad_columns(n, m=m):
            cols = tile_of(n, 256)
            part = nt(grad_hidden[m], w_up[cols]).astype(BF)
            for k in range(4):
                grad_terms[m, k, :, cols] = part[k * TILE : (k + 1) * TILE]

        loop(4, grad_columns)
        third[m].start()
    for m in range(2):
        third[m].relay()

        def branch_columns(n, m=m):
            cols = tile_of(n, 256)
            part = nn(active[m], w_down[:, cols]).astype(BF)
            for k in range(4):
                branch[m, k, :, cols] = part[k * TILE : (k + 1) * TILE]

        loop(4, branch_columns)

    fourth = [Gather(ring, whole_gm.at[m]) for m in range(2)]
    for m in range(2):
        grad_normed = third[m].finish()
        rows = middle[m]
        inverse = inverse_rms(rows)
        unit = rows * inverse
        part = jnp.sum(grad_normed * unit, axis=0, keepdims=True)
        g_gain[...] = part if m == 0 else g_gain[...] + part
        scaled = grad_normed * gain[...]
        inner = jnp.mean(scaled * unit, axis=-1, keepdims=True)
        total = g[m].astype(F32) + inverse * (scaled - unit * inner)
        grad_middle[m] = total
        whole_gm[m, 0] = total.astype(BF)
        fourth[m].start()

    def up_rows(n):
        rows = tile_of(n, 256)
        total = tn(whole_mlp[0, :, :, rows].reshape(512, 256), grad_hidden[0])
        total = total + tn(whole_mlp[1, :, :, rows].reshape(512, 256), grad_hidden[1])
        g_up[rows] = total.astype(BF)

    loop(2, up_rows)
    fourth[0].relay()
    fourth[1].relay()
    loop(2, lambda n: up_rows(n + 2))

    def down_rows(n):
        rows = tile_of(n, 256)
        total = tn(active[0, :, rows], whole_grad[0].reshape(512, 1024))
        total = total + tn(active[1, :, rows], whole_grad[1].reshape(512, 1024))
        g_down[rows] = total.astype(BF)

    loop(4, down_rows)
    for m in range(2):
        fourth[m].finish()
    for m in range(2):
        for step in (first, second, third, fourth):
            step[m].close()


def back_kernel(
    whole_gm, w_out, qkv, kv_all, state_kv, lse, table, closed, prior, update, update_lse, state_query, state_proj,
    bias, slope, across, keeps, branch, middle,
    dqkv, g_query, g_proj, g_rel, g_bias, g_scale, out,
    grad_att, grad_kv, grad_state, early, later, grad_prior, moved, held, grad_after, near, sums,
    mid, into, send, recv, s0, r0, s1, r1, s2, r2, local,
):
    scale = TILE**-0.5
    ring = Ring(send, recv)
    place, count = lax.axis_index("blk"), lax.axis_size("blk")
    pl.semaphore_wait(pltpu.get_barrier_semaphore(), ring.greet() + greet_blocks())
    outs = [Reduce(ring, branch.at[m], mid.at[m], into.at[m]) for m in range(2)]
    for m in range(2):
        outs[m].start()
    before = {"blk": lax.rem(place + count - 1, count)}
    shifts = [remote(early.at[m], later.at[m], s0.at[m], r0.at[m], before) for m in range(2)]
    there = [
        Exchange(grad_prior.at[m], moved.at[m], s1.at[m], r1.at[m], local.at[m]) for m in range(2)
    ]
    back = [
        Exchange(held.at[m], grad_after.at[m], s2.at[m], r2.at[m], local.at[2 + m])
        for m in range(2)
    ]
    near[...] = jnp.zeros(near.shape, F32)
    g_query[...] = jnp.zeros(g_query.shape, F32)
    g_bias[...] = jnp.zeros(g_bias.shape, F32)
    g_scale[...] = jnp.zeros(g_scale.shape, F32)
    grad_kv[...] = jnp.zeros(grad_kv.shape, F32)
    grad_state[...] = jnp.zeros(grad_state.shape, F32)

    def own_chunk(qi):
        return lax.rem(qi + 4 - ring.me, 4)

    for m in range(2):
        part = nt(whole_gm[m].reshape(512, 1024), w_out[...]).astype(BF)
        for k in range(4):
            grad_att[m, ring.row_chunk(k)] = part[k * TILE : (k + 1) * TILE]

        def attend(qi, m=m):
            rows = tile_of(qi)
            window = pl.ds(pl.multiple_of(qi * TILE, TILE), 5 * TILE)
            shut = closed_row(closed[m, 0:1], qi)
            for h in range(2):
                k_cols, v_cols = head(h), head(h, base=256)
                sk_cols = slice(h * 256, h * 256 + TILE)
                sv_cols = slice(h * 256 + TILE, (h + 1) * 256)
                q = qkv[m, rows, head(h)]
                d = grad_att[m, rows, head(h)]
                level = lse[m, h, rows]
                token = jnp.exp(
                    nt(q, kv_all[m, window, k_cols]) * scale + (table[h] + shut) - level
                )
                from_state = jnp.exp(nt(q, state_kv[m, :, sk_cols]) * scale - level)
                grad_token = nt(d, kv_all[m, window, v_cols])
                grad_from = nt(d, state_kv[m, :, sv_cols])
                delta = jnp.sum(token * grad_token, axis=-1, keepdims=True) + jnp.sum(
                    from_state * grad_from, axis=-1, keepdims=True
                )
                grad_token = token * (grad_token - delta)
                grad_from = from_state * (grad_from - delta)
                near[h, :, 0:128] += (
                    grad_token[:, 0:128] + grad_token[:, 128:256] + grad_token[:, 256:384]
                )
                near[h, :, 128:384] += grad_token[:, 384:640]
                token_low = grad_token.astype(BF)
                from_low = grad_from.astype(BF)
                grad_q = scale * (
                    nn(token_low, kv_all[m, window, k_cols]) + nn(from_low, state_kv[m, :, sk_cols])
                )
                dqkv[m, own_chunk(qi), :, head(h)] = grad_q.astype(BF)
                grad_kv[m, window, k_cols] += tn(token_low, q)
                grad_kv[m, window, v_cols] += tn(token.astype(BF), d)
                grad_state[m, :, sk_cols] += tn(from_low, q)
                grad_state[m, :, sv_cols] += tn(from_state.astype(BF), d)

        loop(4, attend)
        early[m, :, 0:256] = (scale * grad_kv[m, 0:512, 0:256]).astype(BF)
        early[m, :, 256:512] = grad_kv[m, 0:512, 256:512].astype(BF)
        shifts[m].start()
        for h in range(2):
            low = jnp.concatenate(
                [
                    (scale * grad_state[m, :, h * 256 : h * 256 + TILE]).astype(BF),
                    grad_state[m, :, h * 256 + TILE : (h + 1) * 256].astype(BF),
                ],
                1,
            )
            grad_prior[m, :, head(h)] = nt(low, state_proj[h]).astype(BF)
            part = tn(prior[m, :, head(h)], low)
            g_proj[h] = part if m == 0 else g_proj[h] + part
        there[m].start()
        outs[m].relay()

    for m in range(2):
        there[m].finish()

        def scan(t, grad, m=m):
            b = count - 1 - t
            rows = tile_of(b, 16)
            held[m, rows] = grad.astype(BF)
            forget = jax.nn.sigmoid(bias[...] + slope[...] * across[m, rows].astype(F32))
            return keeps[b, m : m + 1] * (moved[m, rows].astype(F32) + forget * grad)

        lax.fori_loop(0, count, scan, jnp.zeros((16, 256), F32))
        back[m].start()

    row = lax.broadcasted_iota(jnp.int32, (TILE, TILE), 0)
    col = lax.broadcasted_iota(jnp.int32, (TILE, TILE), 1)
    distance = [row - col + TILE, row - col]
    for h in range(2):
        for t in range(BUCKETS):
            total = jnp.zeros((1, TILE), F32)
            for part in range(2):
                d = distance[part]
                inside = d >= STARTS[t]
                if t + 1 < BUCKETS:
                    inside = inside & (d < STARTS[t + 1])
                values = near[h, :, TILE * (part + 1) : TILE * (part + 2)]
                total = total + jnp.sum(jnp.where(inside, values, 0.0), axis=0, keepdims=True)
            if t + 1 == BUCKETS:
                total = total + jnp.sum(near[h, :, 0:TILE], axis=0, keepdims=True)
            sums[t : t + 1] = total
        g_rel[h] = jnp.sum(sums[...], axis=1, keepdims=True)

    for m in range(2):
        out[m] = middle[m] + outs[m].finish()
    for m in range(2):
        back[m].finish()

        def update_tile(t, m=m):
            rows = tile_of(t)
            for h in range(2):
                cols, k_cols, v_cols = head(h), head(h, base=256), head(h, base=512)
                grad = grad_after[m, rows, cols].astype(F32)
                u = update[m, rows, cols]
                inverse = inverse_rms(u)
                unit = u * inverse
                forget = jax.nn.sigmoid(bias[:, cols] + slope[:, cols] * unit)
                gate = grad * (prior[m, rows, cols].astype(F32) - unit) * forget * (1.0 - forget)
                g_bias[:, cols] += jnp.sum(gate, axis=0, keepdims=True)
                g_scale[:, cols] += jnp.sum(gate * unit, axis=0, keepdims=True)
                grad_unit = grad * (1.0 - forget) + gate * slope[:, cols]
                inner = jnp.mean(grad_unit * unit, axis=-1, keepdims=True)
                low = (inverse * (grad_unit - unit * inner)).astype(BF)
                q = state_query[rows, cols]
                probs = jnp.exp(nt(q, qkv[m, :, k_cols]) * scale - update_lse[m, h, rows])
                grad_probs = nt(low, qkv[m, :, v_cols])
                delta = jnp.sum(probs * grad_probs, axis=-1, keepdims=True)
                grad_scores = (probs * (grad_probs - delta)).astype(BF)
                g_query[rows, cols] += scale * nn(grad_scores, qkv[m, :, k_cols])
                grad_kv[m, 512:1024, cols] += tn(grad_scores, q)
                grad_kv[m, 512:1024, head(h, base=256)] += tn(probs.astype(BF), low)

        loop(4, update_tile)
        shifts[m].wait_recv()

        def finish_rows(t, m=m):
            rows = tile_of(t)
            full = grad_kv[m, pl.ds(pl.multiple_of(512 + t * TILE, TILE), TILE)]
            extra = later[m, rows].astype(F32)
            dqkv[m, own_chunk(t), :, 256:512] = (scale * full[:, 0:256] + extra[:, 0:256]).astype(BF)
            dqkv[m, own_chunk(t), :, 512:768] = (full[:, 256:512] + extra[:, 256:512]).astype(BF)

        loop(4, finish_rows)
    for m in range(2):
        outs[m].close()
        shifts[m].wait_send()
        there[m].close()
        back[m].close()


def end_kernel(
    dqkv, w, x, gain, grad_middle, whole, att_rel, whole_gm,
    grad_x, g_qkv, g_out, g_gain,
    terms, mid, into, send, recv,
):
    ring = Ring(send, recv)
    pl.semaphore_wait(pltpu.get_barrier_semaphore(), ring.greet())
    sums = [Reduce(ring, terms.at[m], mid.at[m], into.at[m]) for m in range(2)]
    for m in range(2):

        def columns(n, m=m):
            cols = tile_of(n, 256)
            part = nt(dqkv[m].reshape(512, 768), w[cols]).astype(BF)
            for k in range(4):
                terms[m, k, :, cols] = part[k * TILE : (k + 1) * TILE]

        loop(4, columns)
        sums[m].start()

    def out_rows():
        total = tn(att_rel[0].reshape(512, 256), whole_gm[0].reshape(512, 1024))
        total = total + tn(att_rel[1].reshape(512, 256), whole_gm[1].reshape(512, 1024))
        g_out[...] = total.astype(BF)

    def qkv_rows(n):
        rows = tile_of(n, 256)
        total = tn(whole[0, :, :, rows].reshape(512, 256), dqkv[0].reshape(512, 768))
        total = total + tn(whole[1, :, :, rows].reshape(512, 256), dqkv[1].reshape(512, 768))
        g_qkv[rows] = total.astype(BF)

    out_rows()
    for m in range(2):
        sums[m].relay()
    loop(4, qkv_rows)
    for m in range(2):
        grad_normed = sums[m].finish()
        rows = x[m].astype(F32)
        inverse = inverse_rms(rows)
        unit = rows * inverse
        part = jnp.sum(grad_normed * unit, axis=0, keepdims=True)
        g_gain[...] = part if m == 0 else g_gain[...] + part
        scaled = grad_normed * gain[...]
        inner = jnp.mean(scaled * unit, axis=-1, keepdims=True)
        grad_x[m] = grad_middle[m] + inverse * (scaled - unit * inner)
    for m in range(2):
        sums[m].close()


def call(kernel, name, number, outs, scratch, *args):
    return pl.pallas_call(
        kernel,
        out_shape=tuple(jax.ShapeDtypeStruct(shape, kind) for shape, kind in outs),
        in_specs=[SMEM if a.shape == (BUCKETS, 2) else VMEM for a in args],
        out_specs=tuple(VMEM for _ in outs),
        scratch_shapes=scratch,
        compiler_params=pltpu.CompilerParams(
            collective_id=number, has_side_effects=True, vmem_limit_bytes=LIMIT
        ),
        name=name,
    )(*args)


def sems(*shape):
    return pltpu.SemaphoreType.DMA(shape)


def body(
    tokens_in,
    grad_out,
    flags,
    attn_gain,
    mlp_gain,
    w_qkv,
    w_out,
    rel_bias,
    state_query,
    state_proj,
    forget_bias,
    forget_scale,
    w_up,
    w_down,
):
    micros, rows, width = tokens_in.shape
    block = rows * 4
    local_width = w_qkv.shape[2]
    heads = rel_bias.shape[1]
    states = state_query.shape[0]
    buckets = rel_bias.shape[0]
    count = lax.axis_size("blk")
    w = w_qkv.reshape(width, 3 * local_width)
    attn_row, mlp_row = attn_gain[None], mlp_gain[None]
    bias_row, scale_row = forget_bias[None], forget_scale[None]
    keep_own = (1 - flags[:, 0]).astype(F32)
    keep_rows = jnp.zeros((8, local_width), F32).at[:micros].set(keep_own[:, None])
    closed = jnp.broadcast_to(
        jnp.where(flags == 0, 0.0, MASKED).astype(F32)[:, :, None], (micros, 8, 5 * TILE)
    )
    whole_shape = (micros, 4, rows, width)

    whole, qkv = call(
        front_kernel,
        "front",
        1,
        [(whole_shape, BF), ((micros, block, 3 * local_width), BF)],
        [sems(12), sems(12)],
        tokens_in,
        attn_row,
        w,
    )
    (
        prior,
        across,
        keeps,
        update,
        update_lse,
        state_after,
        kv_all,
        state_kv,
        attended,
        lse,
        table,
        whole_grad,
    ) = call(
        memory_kernel,
        "memory",
        2,
        [
            ((micros, states, local_width), BF),
            ((micros, states, local_width), BF),
            ((count, 8, local_width), F32),
            ((micros, states, local_width), F32),
            ((micros, heads, states, 1), F32),
            ((micros, states, local_width), F32),
            ((micros, 2 * block, 2 * local_width), BF),
            ((micros, states, 2 * local_width), BF),
            ((micros, block, local_width), BF),
            ((micros, heads, block, 1), F32),
            ((heads, TILE, 5 * TILE), F32),
            (whole_shape, BF),
        ],
        [pltpu.VMEM((micros, states, local_width), BF)] * 2
        + [sems(12), sems(12), sems(2), sems(2)]
        + [sems(2, count)] * 4
        + [sems(count)] * 2
        + [sems(4)],
        qkv,
        state_query,
        state_proj,
        bias_row,
        scale_row,
        keep_rows,
        closed,
        rel_bias,
        grad_out,
    )
    att_rel, middle, grad_middle, whole_gm, branch, g_up, g_down, g_mlp_gain = call(
        mlp_kernel,
        "mlp",
        3,
        [
            ((micros, 4, rows, local_width), BF),
            ((micros, rows, width), F32),
            ((micros, rows, width), F32),
            (whole_shape, BF),
            (whole_shape, BF),
            (w_up.shape, BF),
            (w_down.shape, BF),
            ((1, width), F32),
        ],
        [
            pltpu.VMEM(whole_shape, BF),
            pltpu.VMEM(whole_shape, BF),
            pltpu.VMEM((micros, block, w_up.shape[1]), BF),
            pltpu.VMEM((micros, block, w_up.shape[1]), BF),
            pltpu.VMEM(whole_shape, BF),
            pltpu.VMEM((4, 4, rows // 2, width), BF),
            pltpu.VMEM((4, 2, rows, width), BF),
            sems(48),
            sems(48),
        ],
        attended,
        tokens_in,
        grad_out,
        whole_grad,
        w_out,
        w_up,
        w_down,
        mlp_row,
    )

    def summed(values):
        return lax.psum(values.astype(BF), "blk").astype(F32)

    g_up, g_down = summed(g_up), summed(g_down)

    state_shape = (micros, states, local_width)
    dqkv, g_query, g_proj, g_rel, g_bias, g_scale, out = call(
        back_kernel,
        "back",
        4,
        [
            ((micros, 4, rows, 3 * local_width), BF),
            ((states, local_width), F32),
            (state_proj.shape, F32),
            ((heads, buckets, 1), F32),
            ((1, local_width), F32),
            ((1, local_width), F32),
            ((micros, rows, width), F32),
        ],
        [
            pltpu.VMEM((micros, block, local_width), BF),
            pltpu.VMEM((micros, 2 * block, 2 * local_width), F32),
            pltpu.VMEM((micros, states, 2 * local_width), F32),
            pltpu.VMEM((micros, block, 2 * local_width), BF),
            pltpu.VMEM((micros, block, 2 * local_width), BF),
            pltpu.VMEM(state_shape, BF),
            pltpu.VMEM(state_shape, BF),
            pltpu.VMEM(state_shape, BF),
            pltpu.VMEM(state_shape, BF),
            pltpu.VMEM((heads, TILE, 3 * TILE), F32),
            pltpu.VMEM((buckets, TILE), F32),
            pltpu.VMEM((2, 4, rows // 2, width), BF),
            pltpu.VMEM((2, 2, rows, width), BF),
            sems(12),
            sems(12),
            sems(2),
            sems(2),
        ]
        + [sems(2, count)] * 4
        + [sems(4)],
        whole_gm,
        w_out,
        qkv,
        kv_all,
        state_kv,
        lse,
        table,
        closed,
        prior,
        update,
        update_lse,
        state_query,
        state_proj,
        bias_row,
        scale_row,
        across,
        keeps,
        branch,
        middle,
    )
    grad_x, g_qkv, g_out, g_attn_gain = call(
        end_kernel,
        "end",
        5,
        [
            ((micros, rows, width), F32),
            ((width, 3 * local_width), BF),
            (w_out.shape, BF),
            ((1, width), F32),
        ],
        [
            pltpu.VMEM(whole_shape, BF),
            pltpu.VMEM((2, 4, rows // 2, width), BF),
            pltpu.VMEM((2, 2, rows, width), BF),
            sems(12),
            sems(12),
        ],
        dqkv,
        w,
        tokens_in,
        attn_row,
        grad_middle,
        whole,
        att_rel,
        whole_gm,
    )

    def over_head(values):
        for step in (1, 2):
            values = values + lax.ppermute(values, "head", [(i, i ^ step) for i in range(4)])
        return values

    gains = over_head(jnp.concatenate([g_attn_gain, g_mlp_gain], 0).reshape(8, local_width))
    g_rel = jnp.transpose(g_rel[:, :, 0])
    small = jnp.concatenate(
        [g_rel.reshape(1, buckets * heads), jnp.zeros((1, local_width - buckets * heads), F32)], 1
    )
    packed = jnp.concatenate(
        [g_query, gains, g_bias, g_scale, small, jnp.zeros((5, local_width), F32)], 0
    )
    g_qkv, g_out, packed, g_proj = (summed(part) for part in (g_qkv, g_out, packed, g_proj))
    gains = packed[states : states + 8].reshape(2, width)
    return (
        out,
        grad_x,
        state_after[:, None],
        gains[0],
        gains[1],
        g_qkv.reshape(width, 3, local_width),
        g_out,
        packed[states + 10, : buckets * heads].reshape(buckets, heads),
        packed[:states],
        g_proj,
        packed[states + 8],
        packed[states + 9],
        g_up,
        g_down,
    )


def solution(mesh):
    return jax.shard_map(
        body,
        mesh=mesh,
        in_specs=(
            P(None, ("blk", "head"), None),
            P(None, ("blk", "head"), None),
            P(None, "blk"),
            P(),
            P(),
            P(None, None, "head"),
            P("head", None),
            P(None, "head"),
            P(None, "head"),
            P("head", None, None),
            P("head"),
            P("head"),
            P(None, "head"),
            P("head", None),
        ),
        out_specs=(
            P(None, ("blk", "head"), None),
            P(None, ("blk", "head"), None),
            P(None, "blk", None, "head"),
            P(),
            P(),
            P(None, None, "head"),
            P("head", None),
            P(None, "head"),
            P(None, "head"),
            P("head", None, None),
            P("head"),
            P("head"),
            P(None, "head"),
            P("head", None),
        ),
        check_vma=False,
    )
```

time: 1520 us -> 424 us (0.28)
  waiting for transfers between devices: 732 us -> 122 us
  other arithmetic: 357 us -> 12.3 us
  Pallas kernels: 0 us -> 254 us
  matrix products: 139 us -> 0 us
  blocking collectives: 130 us -> 0 us
  local copies, waits for them, and re-layouts: 102 us -> 20.2 us
  starting transfers between devices: 17.2 us -> 1.31 us
    all_gather x16 -> x0, waiting for transfers between devices: 580 us -> none  [the longest x4 254 us: carried_in(): everything = jax.tree.map(lambda part: lax.all_gather(part, axis), shard)]
    pallas_call x0 -> x5, Pallas kernels: none -> 254 us  [call(): pl.pallas_call(kernel, out_shape=tuple((jax.ShapeDtypeStruct(shape, kind)...]
    reduce_scatter x8 -> x0, waiting for transfers between devices: 145 us -> none  [the longest x4 99.7 us: reduce_rows(): lax.psum_scatter(term(jnp.int32(0), rows * lax.axis_size('head')), 'head'...]
    dot_general x72 -> x0, matrix products: 139 us -> none  [the longest x4 18.4 us: scores_of(): jnp.einsum('ihd,jhd->hij', queries, all_keys, preferred_element_type=jnp....]
    psum x2 -> x0, blocking collectives: 130 us -> none  [the longest x1 66 us: body(): lax.psum((g_attn_gain, g_mlp_gain), ('blk', 'head'))]
    psum x1, waiting for transfers between devices: 0.01 us -> 119 us  [summed(): return lax.psum(values.astype(BF), 'blk').astype(F32)]
    select_n x64 -> x0, other arithmetic: 106 us -> none  [turn(): return jax.tree.map(lambda a, b: jnp.where(reached, a, b), new, before)]
    add x76 -> x1, other arithmetic: 105 us -> 0.01 us  [over_head(): values + lax.ppermute(values, 'head', [(i, i ^ step) for i in range(4)])]
  transfers between devices with their start and end apart: 29 -> 3, of which waited for: 27 -> 2; matrix products, arithmetic and copies ran while one was open for 12% -> 1% of each run, Pallas kernels for 0% -> 0%
where the time goes in v2:
time: 424 us
  Pallas kernels  254 us (60%)
  waiting for transfers between devices  122 us (29%)
  local copies, waits for them, and re-layouts  20.2 us (5%)
  between operations  14.3 us (3%)
  other arithmetic  12.3 us (3%)
    pallas_call x5, Pallas kernels, call(): pl.pallas_call(kernel, out_shape=tuple((jax.ShapeDtypeStruct(shape, kind)...  254 us
    psum x1, waiting for transfers between devices, summed(): return lax.psum(values.astype(BF), 'blk').astype(F32)  119 us
    convert_element_type x6, other arithmetic, summed(): return lax.psum(values.astype(BF), 'blk').astype(F32)  10.2 us
    unnamed x38, local copies, waits for them, and re-layouts  9.26 us
  transfers between devices with their start and end apart: 3, of which 2 were waited for; matrix products, arithmetic and copies ran while one was open for 1% of the time, Pallas kernels for 0%

profile of v2, /device:TPU:1, one launch (start us, length us, event | category | flops | bytes accessed | tf_op | source)
XLA Modules:
  0.0 423.9 jit_solution(14852703965096161196)
XLA Ops:
  7.2 0.7 fusion
  7.9 0.7 convert_bitcast_fusion
  8.5 1.7 copy.34
  10.3 1.6 copy.35.w
  11.8 0.7 copy.36.rel
  12.5 26.1 %front.1 = (bf16[2,4,128,1024]{3,2,1,0:T(8,128)(2,1)}, bf16[2,512,768]{2,1,0:T(8,128)(2,1)}) custom-call(bf16[2,128,1024]{2,1,0:T(8,128)(2,1)} %x.9, f32[1,1024]{1,0:T(1,128)} %bitcast.25, bf16[1024,768]{1,0:T(8,128)(2,1)} %copy.35.w), custom_call_target="tpu_custom_call" | custom-call | tf_op jit(solution)/shard_map/front/pallas_call | solution.py:709
  38.6 0.7 broadcast_in_dim.49.closed
  39.3 0.7 scatter.8.own_keep
  40.0 57.0 %memory.1 = (bf16[2,512,256]{2,1,0:T(8,128)(2,1)}, bf16[2,512,256]{2,1,0:T(8,128)(2,1)}, f32[32,8,256]{2,1,0:T(8,128)}, f32[2,512,256]{2,1,0:T(8,128)}, f32[2,2,...) custom-call(bf16[2,512,768]{2,1,0:T(8,128)(2,1)} %get-tuple-element., ...), custom_call_target="tpu_custom_call" | custom-call | tf_op jit(solution)/shard_map/memory/pallas_call | solution.py:709
  97.0 83.9 %mlp.1 = (bf16[2,4,128,256]{3,2,1,0:T(8,128)(2,1)}, f32[2,128,1024]{2,1,0:T(8,128)}, f32[2,128,1024]{2,1,0:T(8,128)}, bf16[2,4,128,1024]{3,2,1,0:T(8,128)(2,1)},...) custom-call(bf16[2,512,256]{2,1,0:T(8,128)(2,1)} %get-tuple-element., ...), custom_call_target="tpu_custom_call" | custom-call | tf_op jit(solution)/shard_map/mlp/pallas_call | solution.py:709
  180.9 59.5 %back.1 = (bf16[2,4,128,768]{3,2,1,0:T(8,128)(2,1)}, f32[512,256]{1,0:T(8,128)}, f32[2,128,256]{2,1,0:T(8,128)}, f32[2,32,1]{2,1,0:T(8,128)}, f32[1,256]{1,0:T(1...) custom-call(bf16[2,4,128,1024]{3,2,1,0:T(8,128)(2,1)} %get-tuple-element.62.whole_gm, bf16[256,1024]{1,0:T(8,128)(2,1)} %w_out.3, ...), custom_call_target="tpu_custom_call" | custom-call | tf_op jit(solution)/shard_map/back/pallas_call | solution.py:709
  240.5 27.6 %end.1 = (f32[2,128,1024]{2,1,0:T(8,128)}, bf16[1024,768]{1,0:T(8,128)(2,1)}, bf16[256,1024]{1,0:T(8,128)(2,1)}, f32[1,1024]{1,0:T(1,128)}) custom-call(bf16[2,4,128,768]{3,2,1,0:T(8,128)(2,1)} %get-tuple-element.75.dqkv, bf16[1024,768]{1,0:T(8,128)(2,1)} %copy.35.w, bf16[2,128,1024]{2,1,0:T(8,128)(2,1)} %x.9, f32[1,1024]{1,0:T(1,128)} %bitcast.26, ...), custom_call_target="tpu_custom_call" | custom-call | tf_op jit(solution)/shard_map/end/pallas_call | solution.py:709
  268.1 0.7 pad_maximum_fusion
  269.0 2.5 collective-permute-done
  271.5 1.2 collective-permute-start.1
  273.0 2.6 copy.39
  275.6 0.7 convert_element_type.27
  276.3 2.0 concatenate.14
  278.3 119.2 %all-reduce.5.cloned.1.call-done = (bf16[1024,3,256]{0,2,1:T(8,128)(2,1)}, bf16[528,256]{1,0:T(8,128)(2,1)}, bf16[256,1024]{1,0:T(8,128)(2,1)}, bf16[2,128,256]{...) async-done(((bf16[1024,3,256]{0,2,1:T(8,128)(2,1)}, bf16[528,256]{1,0:T(8,128)(2,1)}, bf16[256,1024]{1,0:T(8,128)(2,1)}, ...) | async-done | bytes 6692880 | tf_op jit(solution)/shard_map/psum | solution.py:851
  397.5 1.0 convert_element_type.25
  398.5 1.8 slice.48
  400.3 1.3 fusion.1
  401.6 4.2 convert_element_type.29
  405.9 2.5 convert_element_type.30
  408.3 2.1 copy.41
  410.4 1.1 convert_element_type.26
  411.6 0.6 copy.42
  412.2 0.6 copy.43
  413.4 0.7 convert_element_type.28
  414.2 1.0 copy.54
  415.1 1.0 copy.55
  416.1 1.0 copy.56
  (48 shorter events, 1.3 us)
Async XLA Ops:
  7.2 390.3 %all-reduce.5.cloned.1.call-start = ((), (), s32[]{:S(2)}) async-start(), calls=%async_computation | async-start | bytes 13385728 | tf_op jit(solution)/shard_map/psum | solution.py:851
  10.3 1.6 copy-start.11
  240.4 27.7 %copy-start.10 = (f32[1,1024]{1,0:T(1,128)S(1)}, f32[1,1024]{1,0:T(1,128)}, u32[]{:S(2)}) copy-start(f32[1,1024]{1,0:T(1,128)} %get-tuple-element.83) | copy-start | bytes 12292
  240.4 32.2 %copy-start.9 = (f32[2,32,1]{2,1,0:T(8,128)S(1)}, f32[2,32,1]{2,1,0:T(8,128)}, u32[]{:S(2)}) copy-start(f32[2,32,1]{2,1,0:T(8,128)} %get-tuple-element.86) | copy-start | bytes 772
  240.4 32.3 %copy-start.6 = (f32[512,256]{1,0:T(8,128)S(1)}, f32[512,256]{1,0:T(8,128)}, u32[]{:S(2)}) copy-start(f32[512,256]{1,0:T(8,128)} %get-tuple-element.81) | copy-start | bytes 1572868
  240.5 32.5 %copy-start.13 = (f32[1,256]{1,0:T(1,128)S(1)}, f32[1,256]{1,0:T(1,128)}, u32[]{:S(2)}) copy-start(f32[1,256]{1,0:T(1,128)} %get-tuple-element.84) | copy-start | bytes 3076
  240.5 32.6 %copy-start.12 = (f32[1,256]{1,0:T(1,128)S(1)}, f32[1,256]{1,0:T(1,128)}, u32[]{:S(2)}) copy-start(f32[1,256]{1,0:T(1,128)} %get-tuple-element.85) | copy-start | bytes 3076
  268.1 7.5 %copy-start.7 = (f32[2,128,256]{2,1,0:T(8,128)S(1)}, f32[2,128,256]{2,1,0:T(8,128)}, u32[]{:S(2)}) copy-start(f32[2,128,256]{2,1,0:T(8,128)} %get-tuple-element.89) | copy-start | bytes 786436
  268.9 2.6 collective-permute-start
  271.5 4.8 %collective-permute-start.1 = (f32[8,256]{1,0:T(8,128)S(1)}, f32[8,256]{1,0:T(8,128)S(1)}, u32[]{:S(2)}, u32[]{:S(2)}) collective-permute-start(f32[8,256]{1,0:T(8,128)S(1)} %add.24), channel_id=1, source_target_pairs={{0,2},{1,3},{2,0},{3,1},{4,6},{5,7},{6,4},{7,5},{8,10},{9,11},{10,... | collective-permute-start | bytes 24584 | tf_op jit(solution)/shard_map/ppermute | solution.py:939
  401.6 4.2 copy-start
  405.9 2.5 copy-start.1
  408.3 2.1 copy-start.5
  408.3 5.1 %copy-start.8 = (bf16[2,128,256]{2,1,0:T(8,128)(2,1)S(1)}, bf16[2,128,256]{2,1,0:T(8,128)(2,1)}, u32[]{:S(2)}) copy-start(bf16[2,128,256]{2,1,0:T(8,128)(2,1)} %get-tuple-element.123) | copy-start | bytes 393220
  410.4 3.8 copy-start.3
  410.4 4.7 %copy-start.4 = (f32[2,128,1024]{2,1,0:T(8,128)S(1)}, f32[2,128,1024]{2,1,0:T(8,128)}, u32[]{:S(2)}) copy-start(f32[2,128,1024]{2,1,0:T(8,128)} %get-tuple-element.145) | copy-start | bytes 3145732
  414.2 1.9 copy-start.2
Sparse Core Ops, SparseCore 0:
  278.4 118.9 all-reduce.4

commit v3 on v2

v3 whole, which is shorter than its diff:
```python
import math
import types

import jax
import jax.numpy as jnp
from jax import lax
from jax.experimental import pallas as pl
from jax.experimental.pallas import tpu as pltpu
from jax.sharding import PartitionSpec as P

BUCKETS = 32
MAXDIST = 128
EPSILON = 1e-06
MASKED = -1e30
TILE = 128
MESH = pl.DeviceIdType.MESH
BF = jnp.bfloat16
F32 = jnp.float32
VMEM = pl.BlockSpec(memory_space=pltpu.VMEM)
SMEM = pl.BlockSpec(memory_space=pltpu.SMEM)
LIMIT = 60 * 2**20
ROOT = math.sqrt(2.0 / math.pi)
CUBIC = 0.044715


def bucket_starts():
    exact = BUCKETS // 2
    levels = [
        int(math.ceil(exact * (MAXDIST / exact) ** (t / (BUCKETS - exact))))
        for t in range(1, BUCKETS - exact)
    ]
    return list(range(exact + 1)) + levels


STARTS = bucket_starts()


def nn(a, b):
    return lax.dot_general(a, b, (((1,), (0,)), ((), ())), preferred_element_type=F32)


def nt(a, b):
    return lax.dot_general(a, b, (((1,), (1,)), ((), ())), preferred_element_type=F32)


def tn(a, b):
    return lax.dot_general(a, b, (((0,), (0,)), ((), ())), preferred_element_type=F32)


def inverse_rms(values):
    return lax.rsqrt(jnp.mean(values * values, axis=-1, keepdims=True) + EPSILON)


def tile_of(index, size=TILE):
    return pl.ds(pl.multiple_of(index * size, size), size)


def loop(count, step):
    def run(i, c):
        step(i)
        return c

    lax.fori_loop(0, count, run, 0)


def remote(src, dst, send_sem, recv_sem, device):
    return pltpu.make_async_remote_copy(
        src_ref=src,
        dst_ref=dst,
        send_sem=send_sem,
        recv_sem=recv_sem,
        device_id=device,
        device_id_type=MESH,
    )


class Links:
    def __init__(self, send, recv):
        self.send, self.recv, self.used = send, recv, 0

    def go(self, src, dst, device):
        copy = remote(src, dst, self.send.at[self.used], self.recv.at[self.used], device)
        self.used += 1
        copy.start()
        return copy


class Ring:
    def __init__(self, links, me, device):
        self.links, self.me = links, me
        self.right = device(lax.rem(me + 1, 4))
        self.left = device(lax.rem(me + 3, 4))

    def go(self, src, dst, peer):
        return self.links.go(src, dst, peer)

    def greet(self):
        barrier = pltpu.get_barrier_semaphore()
        for peer in (self.right, self.left):
            pl.semaphore_signal(barrier, inc=1, device_id=peer, device_id_type=MESH)
        return 2

    def chunk(self, k):
        return lax.rem(self.me + k, 4)

    def row_chunk(self, k):
        return tile_of(self.chunk(k))


def head_ring(links):
    return Ring(links, lax.axis_index("head"), lambda i: {"head": i})


def by_rows(buf):
    half = buf.shape[1] // 2

    def piece(k, part=None, offset=0):
        return buf.at[k] if part is None else buf.at[k, part * half : (part + 1) * half]

    return piece


def by_columns(buf, base, rows, chunk):
    half = buf.shape[1] // 2

    def piece(k, part=None, offset=0):
        at = pl.ds(pl.multiple_of(base + chunk(k + offset) * rows, rows), rows)
        return buf.at[at] if part is None else buf.at[at, part * half : (part + 1) * half]

    return piece


class Gather:
    def __init__(self, ring, piece):
        self.ring, self.piece = ring, piece

    def start(self):
        r, p = self.ring, self.piece
        self.a0 = r.go(p(0, 0), p(3, 0, 1), r.right)
        self.b0 = r.go(p(0, 1), p(1, 1, 3), r.left)
        self.a1 = r.go(p(0, 1), p(3, 1, 1), r.right)
        self.b1 = r.go(p(0, 0), p(1, 0, 3), r.left)

    def relay(self):
        r, p = self.ring, self.piece
        self.a0.wait_recv()
        self.a2 = r.go(p(3, 0), p(2, 0, 1), r.right)
        self.b0.wait_recv()
        self.b2 = r.go(p(1, 1), p(2, 1, 3), r.left)

    def finish(self):
        for copy in (self.a1, self.b1, self.a2, self.b2):
            copy.wait_recv()

    def close(self):
        for copy in (self.a0, self.b0, self.a1, self.b1, self.a2, self.b2):
            copy.wait_send()


class Reduce:
    def __init__(self, ring, terms, mid, into):
        self.ring, self.terms, self.mid, self.into = ring, terms, mid, into
        if mid.shape[1] == into.shape[1]:
            half = into.shape[2] // 2
            self.place = lambda i, part: into.at[i, :, part * half : (part + 1) * half]
        else:
            half = into.shape[1] // 2
            self.place = lambda i, part: into.at[i, part * half : (part + 1) * half]

    def start(self):
        r, t = self.ring, self.terms
        self.a0 = r.go(t(2, 0), self.mid.at[0], r.right)
        self.b0 = r.go(t(2, 1), self.mid.at[1], r.left)
        self.a1 = r.go(t(1, 1), self.place(0, 1), r.right)
        self.b1 = r.go(t(3, 0), self.place(1, 0), r.left)

    def relay(self):
        r, t, mid = self.ring, self.terms, self.mid
        self.a0.wait_recv()
        mid[2] = (mid[0].astype(F32) + t(1, 0)[...].astype(F32)).astype(BF)
        self.a2 = r.go(mid.at[2], self.place(0, 0), r.right)
        self.b0.wait_recv()
        mid[3] = (mid[1].astype(F32) + t(3, 1)[...].astype(F32)).astype(BF)
        self.b2 = r.go(mid.at[3], self.place(1, 1), r.left)

    def finish(self):
        for copy in (self.a1, self.b1, self.a2, self.b2):
            copy.wait_recv()
        return (
            self.terms(0)[...].astype(F32)
            + self.into[0].astype(F32)
            + self.into[1].astype(F32)
        )

    def close(self):
        for copy in (self.a0, self.b0, self.a1, self.b1, self.a2, self.b2):
            copy.wait_send()


def block_device(x, z, c):
    return {"blk": (x * 4 + z) * 2 + c}


def block_place():
    place = lax.axis_index("blk")
    return place % 2, (place // 2) % 4, place // 8


class Plane:
    def __init__(self, links):
        c, z, x = block_place()
        self.links = links
        self.peer = block_device(x, z, 1 - c)
        rx = Ring(links, x, lambda i: block_device(i, z, c))
        rz = Ring(links, z, lambda i: block_device(x, i, c))
        self.rings = [rx, rz]
        self.first, self.second = (rx, rz), (rz, rx)
        self.base = c * 512
        self.own = pl.ds(pl.multiple_of(c * 512, 512), 512)
        self.away = pl.ds(pl.multiple_of((1 - c) * 512, 512), 512)
        self.top = [c * 512 + x * 64, c * 512 + 256 + z * 64]
        self.last = [
            pl.ds(pl.multiple_of(self.top[0] + z * 16, 16), 16),
            pl.ds(pl.multiple_of(self.top[1] + x * 16, 16), 16),
        ]

    def greet(self):
        barrier = pltpu.get_barrier_semaphore()
        pl.semaphore_signal(barrier, inc=1, device_id=self.peer, device_id_type=MESH)
        return 1 + sum(ring.greet() for ring in self.rings)


class Steps:
    def advance(self, steps=1):
        for _ in range(steps):
            if self.steps:
                self.steps.pop(0)()


class PlaneReduce(Steps):
    def __init__(self, plane, parts, result, half, mid, into, quarter, small_mid, small_into):
        self.plane, self.parts, self.result, self.half = plane, parts, result, half
        self.quarter = quarter
        first, second = plane.first, plane.second
        self.reduce1 = [
            Reduce(first[i], by_columns(half, i * 256, 64, first[i].chunk), mid.at[i], into.at[i])
            for i in range(2)
        ]
        self.reduce2 = [
            Reduce(
                second[i],
                by_columns(quarter.at[i], 0, 16, second[i].chunk),
                small_mid.at[i],
                small_into.at[i],
            )
            for i in range(2)
        ]
        self.steps = [
            self.cores,
            self.start1,
            lambda: [r.relay() for r in self.reduce1],
            self.start2,
            lambda: [r.relay() for r in self.reduce2],
            self.finish,
        ]

    def cores(self):
        plane = self.plane
        self.swap = plane.links.go(self.parts.at[plane.away], self.half, plane.peer)

    def start1(self):
        self.swap.wait_recv()

        def add(t):
            rows = tile_of(t, 64)
            own = pl.ds(pl.multiple_of(self.plane.base + t * 64, 64), 64)
            self.half[rows] = (
                self.parts[own].astype(F32) + self.half[rows].astype(F32)
            ).astype(BF)

        loop(8, add)
        for r in self.reduce1:
            r.start()

    def start2(self):
        for i, r in enumerate(self.reduce1):
            self.quarter[i] = r.finish().astype(BF)
            self.reduce2[i].start()

    def finish(self):
        for i, r in enumerate(self.reduce2):
            self.result(i, r.finish().astype(BF))

    def close(self):
        self.swap.wait_send()
        for r in self.reduce1 + self.reduce2:
            r.close()


class PlaneGather(Steps):
    def __init__(self, plane, total):
        self.plane, self.total = plane, total
        first, second = plane.first, plane.second
        self.gather1 = [
            Gather(second[i], by_columns(total, plane.top[i], 16, second[i].chunk))
            for i in range(2)
        ]
        self.gather2 = [
            Gather(first[i], by_columns(total, plane.base + i * 256, 64, first[i].chunk))
            for i in range(2)
        ]
        self.steps = [
            lambda: [g.start() for g in self.gather1],
            lambda: [g.relay() for g in self.gather1],
            self.start2,
            lambda: [g.relay() for g in self.gather2],
            self.cores,
            lambda: self.swap.wait_recv(),
        ]

    def start2(self):
        for i, g in enumerate(self.gather1):
            g.finish()
            self.gather2[i].start()

    def cores(self):
        for g in self.gather2:
            g.finish()
        rows = self.total.at[self.plane.own]
        self.swap = self.plane.links.go(rows, rows, self.plane.peer)

    def close(self):
        self.swap.wait_send()
        for g in self.gather1 + self.gather2:
            g.close()


def reduce_scratch(width):
    return dict(
        half=((512, width), BF),
        mid=((2, 4, 64, width // 2), BF),
        into=((2, 2, 64, width), BF),
        quarter=((2, 64, width), BF),
        small_mid=((2, 4, 16, width // 2), BF),
        small_into=((2, 2, 16, width), BF),
    )


class Exchange:
    def __init__(self, source, target, send, recv, local):
        self.count = lax.axis_size("blk")
        self.place = lax.axis_index("blk")
        self.size = source.shape[0] // self.count
        self.source, self.target = source, target
        self.send, self.recv, self.local = send, recv, local

    def part(self, j):
        peer = lax.rem(self.place + j, self.count)
        return remote(
            self.source.at[tile_of(peer, self.size)],
            self.target.at[tile_of(self.place, self.size)],
            self.send.at[j],
            self.recv.at[j],
            {"blk": peer},
        )

    def own(self):
        rows = tile_of(self.place, self.size)
        return pltpu.make_async_copy(self.source.at[rows], self.target.at[rows], self.local)

    def start(self):
        loop(self.count - 1, lambda j: self.part(j + 1).start())
        self.own().start()

    def finish(self):
        self.own().wait()
        loop(self.count - 1, lambda j: self.part(j + 1).wait_recv())

    def close(self):
        loop(self.count - 1, lambda j: self.part(j + 1).wait_send())


def greet_blocks():
    barrier = pltpu.get_barrier_semaphore()
    count, place = lax.axis_size("blk"), lax.axis_index("blk")

    def greet(j):
        pl.semaphore_signal(
            barrier, inc=1, device_id={"blk": lax.rem(place + j + 1, count)}, device_id_type=MESH
        )

    loop(count - 1, greet)
    return count - 1


def closed_row(closed, qi):
    column = lax.broadcasted_iota(jnp.int32, closed.shape, 1) + qi * TILE
    return jnp.where(column < 512, closed, 0.0)


def head(h, size=TILE, base=0):
    return slice(base + h * size, base + (h + 1) * size)


def window_of(qi):
    return pl.ds(pl.multiple_of(qi * TILE, TILE), 5 * TILE)


def split_rows(target, m, cols, part):
    for k in range(4):
        target[m, k, :, cols] = part[k * TILE : (k + 1) * TILE]


def write_table(table, rel):
    row = lax.broadcasted_iota(jnp.int32, (TILE, TILE), 0)
    col = lax.broadcasted_iota(jnp.int32, (TILE, TILE), 1)
    for h in range(2):
        far = jnp.full((TILE, TILE), rel[BUCKETS - 1, h], F32)
        table[h, :, 0:128] = jnp.where(row < col, far, MASKED)
        table[h, :, 128:256] = far
        table[h, :, 256:384] = far
        for shift, at in ((TILE, 384), (0, 512)):
            distance = row - col + shift
            total = jnp.full((TILE, TILE), rel[0, h], F32)
            for t in range(1, BUCKETS):
                total = jnp.where(distance >= STARTS[t], rel[t, h], total)
            table[h, :, at : at + TILE] = jnp.where(distance >= 0, total, MASKED)


def forward_kernel(r):
    scale = TILE**-0.5
    links = Links(r.send, r.recv)
    ring = head_ring(links)
    plane = Plane(links)
    place, count = lax.axis_index("blk"), lax.axis_size("blk")
    both = range(2)
    for m in both:
        rows = r.x[m].astype(F32)
        r.whole.ref[m, 0] = (rows * inverse_rms(rows) * r.attn_gain[...]).astype(BF)
        r.whole_grad[m, 0] = r.g[m]
    pl.semaphore_wait(pltpu.get_barrier_semaphore(), ring.greet() + greet_blocks())
    whole, qkv, kv_all = r.whole.ref, r.qkv.ref, r.kv_all.ref
    prior, across, keeps = r.prior.ref, r.across.ref, r.keeps.ref
    update, stats, state_kv = r.update.ref, r.stats.ref, r.state_kv.ref
    table, att_rel, middle, branch = r.table.ref, r.att_rel.ref, r.middle.ref, r.branch.ref
    gather_x = [Gather(ring, by_rows(whole.at[m])) for m in both]
    gather_g = [Gather(ring, by_rows(r.whole_grad.at[m])) for m in both]
    for m in both:
        gather_x[m].start()

    def tell(j):
        peer = {"blk": lax.rem(place + j, count)}
        return remote(r.own_keep, keeps.at[place], r.s3.at[j], r.r3.at[j], peer)

    loop(count - 1, lambda j: tell(j + 1).start())
    keeps[place] = r.own_keep[...]
    write_table(table, r.rel)
    r.table.put()
    after = {"blk": lax.rem(place + 1, count)}
    shifts = [
        remote(qkv.at[m, :, 256:768], kv_all.at[m, 0:512], r.s0.at[m], r.r0.at[m], after)
        for m in both
    ]
    there = [
        Exchange(r.unit_low.at[m], across.at[m], r.s1.at[m], r.r1.at[m], r.local.at[m])
        for m in both
    ]
    back = [
        Exchange(r.held.at[m], prior.at[m], r.s2.at[m], r.r2.at[m], r.local.at[2 + m])
        for m in both
    ]

    def project(m):
        def columns(n):
            cols = tile_of(n, 256)
            part = nn(whole[m].reshape(512, 1024), r.w[:, cols]).astype(BF)
            for k in range(4):
                qkv[m, ring.row_chunk(k), cols] = part[k * TILE : (k + 1) * TILE]

        loop(3, columns)
        shifts[m].start()
        kv_all[m, 512:1024] = qkv[m, :, 256:768]

    def update_tile(m):
        def step(t):
            rows = tile_of(t)
            for h in range(2):
                scores = nt(r.state_query[rows, head(h)], qkv[m, :, head(h, base=256)]) * scale
                top = jnp.max(scores, axis=-1, keepdims=True)
                raised = jnp.exp(scores - top)
                total = jnp.sum(raised, axis=-1, keepdims=True)
                stats[m, rows, h : h + 1] = top + jnp.log(total)
                u = nn((raised / total).astype(BF), qkv[m, :, head(h, base=512)])
                update[m, rows, head(h)] = u
                r.unit_low[m, rows, head(h)] = (u * inverse_rms(u)).astype(BF)

        return step

    def scan(m):
        def step(b, state):
            rows = tile_of(b, 16)
            u = across[m, rows].astype(F32)
            forget = jax.nn.sigmoid(r.bias[...] + r.slope[...] * u)
            before = keeps[b, m : m + 1] * state
            r.held[m, rows] = before.astype(BF)
            return forget * before + (1.0 - forget) * u

        lax.fori_loop(0, count, step, jnp.zeros((16, 256), F32))

    def state(m):
        def step(t):
            rows = tile_of(t)
            before = prior[m, rows]
            for h in range(2):
                state_kv[m, rows, head(h, 256)] = nn(before[:, head(h)], r.state_proj[h]).astype(BF)
                u = update[m, rows, head(h)]
                u = u * inverse_rms(u)
                forget = jax.nn.sigmoid(r.bias[:, head(h)] + r.slope[:, head(h)] * u)
                r.state_after.ref[m, rows, head(h)] = (
                    forget * before[:, head(h)].astype(F32) + (1.0 - forget) * u
                )

        return step

    def attend(m):
        def step(qi):
            rows, window = tile_of(qi), window_of(qi)
            shut = closed_row(r.closed[m, 0:1], qi)
            for h in range(2):
                q = qkv[m, rows, head(h)]
                token = nt(q, kv_all[m, window, head(h)]) * scale + (table[h] + shut)
                from_state = nt(q, state_kv[m, :, h * 256 : h * 256 + TILE]) * scale
                top = jnp.maximum(
                    jnp.max(token, axis=-1, keepdims=True),
                    jnp.max(from_state, axis=-1, keepdims=True),
                )
                token = jnp.exp(token - top)
                from_state = jnp.exp(from_state - top)
                total = jnp.sum(token, axis=-1, keepdims=True) + jnp.sum(
                    from_state, axis=-1, keepdims=True
                )
                stats[m, rows, 2 + h : 3 + h] = top + jnp.log(total)
                out = nn(token.astype(BF), kv_all[m, window, head(h, base=256)]) + nn(
                    from_state.astype(BF), state_kv[m, :, h * 256 + TILE : (h + 1) * 256]
                )
                att_rel[m, lax.rem(qi + 4 - ring.me, 4), :, head(h)] = (out / total).astype(BF)

        return step

    first = [
        Reduce(ring, by_rows(r.terms.at[m]), r.mids.at[m], r.intos.at[m]) for m in both
    ]
    second = [Gather(ring, by_rows(r.whole_mlp.at[m])) for m in both]
    third = [
        Reduce(ring, by_rows(r.terms.at[m]), r.mids.at[2 + m], r.intos.at[2 + m]) for m in both
    ]
    fourth = [Gather(ring, by_rows(r.whole_gm.at[m])) for m in both]

    def out_terms(m):
        def columns(n):
            cols = tile_of(n, 256)
            part = nn(att_rel[m].reshape(512, 256), r.w_out.ref[:, cols]).astype(BF)
            split_rows(r.terms, m, cols, part)

        loop(4, columns)

    def normalise(m):
        rows = r.x[m].astype(F32) + first[m].finish()
        middle[m] = rows
        r.whole_mlp[m, 0] = (rows * inverse_rms(rows) * r.mlp_gain[...]).astype(BF)

    def hidden(m):
        def columns(n):
            cols = tile_of(n, 256)
            value = nn(r.whole_mlp[m].reshape(512, 1024), r.w_up.ref[:, cols])
            grad_active = nt(r.whole_grad[m].reshape(512, 1024), r.w_down.ref[cols])
            square = value * value
            bent = jnp.tanh(ROOT * value * (1.0 + CUBIC * square))
            r.active[m, :, cols] = (0.5 * value * (1.0 + bent)).astype(BF)
            rise = 0.5 * (1.0 + bent) + 0.5 * value * (1.0 - bent * bent) * ROOT * (
                1.0 + 3.0 * CUBIC * square
            )
            r.grad_hidden[m, :, cols] = (grad_active * rise).astype(BF)

        loop(4, columns)

    def grad_terms(m):
        def columns(n):
            cols = tile_of(n, 256)
            part = nt(r.grad_hidden[m], r.w_up.ref[cols]).astype(BF)
            split_rows(r.terms, m, cols, part)

        loop(4, columns)

    def branch_terms(m):
        def columns(n):
            cols = tile_of(n, 256)
            part = nn(r.active[m], r.w_down.ref[:, cols]).astype(BF)
            split_rows(branch, m, cols, part)

        loop(4, columns)

    def grad_rows(m):
        grad_normed = third[m].finish()
        rows = middle[m]
        inverse = inverse_rms(rows)
        unit = rows * inverse
        part = jnp.sum(grad_normed * unit, axis=0, keepdims=True)
        r.g_gain[...] = part if m == 0 else r.g_gain[...] + part
        scaled = grad_normed * r.mlp_gain[...]
        inner = jnp.mean(scaled * unit, axis=-1, keepdims=True)
        total = r.g[m].astype(F32) + inverse * (scaled - unit * inner)
        r.grad_middle[m] = total
        r.whole_gm[m, 0] = total.astype(BF)

    def up_rows(n):
        rows = tile_of(n, 256)
        total = tn(r.whole_mlp[0, :, :, rows].reshape(512, 256), r.grad_hidden[0])
        total = total + tn(r.whole_mlp[1, :, :, rows].reshape(512, 256), r.grad_hidden[1])
        r.parts[rows, 0:1024] = total.astype(BF)

    def down_rows(n):
        rows = tile_of(n, 256)
        total = tn(r.active[0, :, rows], r.whole_grad[0].reshape(512, 1024))
        total = total + tn(r.active[1, :, rows], r.whole_grad[1].reshape(512, 1024))
        r.parts[rows, 1024:2048] = total.astype(BF)

    def keep_seed(i, rows):
        r.seeds[i] = rows

    weights = PlaneReduce(
        plane, r.parts, keep_seed, r.half, r.mid, r.into, r.quarter, r.small_mid, r.small_into
    )

    gather_x[0].relay()
    gather_x[1].relay()
    gather_x[0].finish()
    project(0)
    loop(4, update_tile(0))
    there[0].start()
    gather_x[1].finish()
    gather_g[0].start()
    gather_g[1].start()
    project(1)
    r.whole.put()
    r.qkv.put()
    loop(4, update_tile(1))
    there[1].start()
    r.update.put()
    gather_g[0].relay()
    loop(count - 1, lambda j: tell(j + 1).wait_recv())
    there[0].finish()
    scan(0)
    back[0].start()
    gather_g[1].relay()
    there[1].finish()
    scan(1)
    back[1].start()
    r.across.put()
    r.keeps.put()
    shifts[0].wait_recv()
    shifts[1].wait_recv()
    r.kv_all.put()
    back[0].finish()
    loop(4, state(0))
    loop(4, attend(0))
    r.w_out.get()
    out_terms(0)
    first[0].start()
    back[1].finish()
    r.prior.put()
    loop(4, state(1))
    r.state_kv.put()
    r.state_after.put()
    loop(2, attend(1))
    first[0].relay()
    loop(2, lambda qi: attend(1)(qi + 2))
    r.stats.put()
    out_terms(1)
    r.att_rel.put()
    first[1].start()
    normalise(0)
    second[0].start()
    first[1].relay()
    second[0].relay()
    normalise(1)
    second[1].start()
    r.middle.put()
    r.w_up.get()
    r.w_down.get()
    gather_g[0].finish()
    second[0].finish()
    hidden(0)
    second[1].relay()
    first[0].close()
    grad_terms(0)
    third[0].start()
    branch_terms(0)
    third[0].relay()
    gather_g[1].finish()
    second[1].finish()
    hidden(1)
    first[1].close()
    grad_terms(1)
    third[1].start()
    grad_rows(0)
    fourth[0].start()
    loop(1, up_rows)
    third[1].relay()
    fourth[0].relay()
    loop(3, lambda n: up_rows(n + 1))
    grad_rows(1)
    fourth[1].start()
    loop(2, down_rows)
    fourth[1].relay()
    loop(2, lambda n: down_rows(n + 2))
    weights.advance()
    branch_terms(1)
    r.branch.put()
    weights.advance(5)
    for m in both:
        fourth[m].finish()
    weights.close()
    for m in both:
        for step in (gather_x, gather_g, second, third, fourth):
            step[m].close()
        shifts[m].wait_send()
        there[m].close()
        back[m].close()
    loop(count - 1, lambda j: tell(j + 1).wait_send())


def backward_kernel(r):
    scale = TILE**-0.5
    links = Links(r.send, r.recv)
    ring = head_ring(links)
    plane = Plane(links)
    opposite = {"head": ring.chunk(2)}
    place, count = lax.axis_index("blk"), lax.axis_size("blk")
    both = range(2)
    r.total_mlp[plane.last[0]] = r.seeds[0]
    r.total_mlp[plane.last[1]] = r.seeds[1]
    barrier = pltpu.get_barrier_semaphore()
    pl.semaphore_signal(barrier, inc=1, device_id=opposite, device_id_type=MESH)
    pl.semaphore_wait(barrier, 1 + ring.greet() + greet_blocks())
    mlp_sum = PlaneGather(plane, r.total_mlp)
    mlp_sum.advance()
    qkv, kv_all, state_kv, stats = r.qkv, r.kv_all, r.state_kv, r.stats
    r.branch.get()
    branch = r.branch.ref
    outs = [Reduce(ring, by_rows(branch.at[m]), r.mids.at[m], r.intos.at[m]) for m in both]
    ends = [
        Reduce(ring, by_rows(branch.at[m]), r.mids.at[2 + m], r.intos.at[2 + m]) for m in both
    ]
    for m in both:
        outs[m].start()
    before = {"blk": lax.rem(place + count - 1, count)}
    shifts = [
        remote(r.early.at[m], r.later.at[m], r.s0.at[m], r.r0.at[m], before) for m in both
    ]
    there = [
        Exchange(r.grad_prior.at[m], r.moved.at[m], r.s1.at[m], r.r1.at[m], r.local.at[m])
        for m in both
    ]
    back = [
        Exchange(r.held.at[m], r.grad_after.at[m], r.s2.at[m], r.r2.at[m], r.local.at[2 + m])
        for m in both
    ]
    for ref in (r.near, r.sums, r.g_query, r.g_bias, r.g_scale, r.grad_kv, r.grad_state):
        ref[...] = jnp.zeros(ref.shape, F32)

    def own_chunk(qi):
        return lax.rem(qi + 4 - ring.me, 4)

    def attention_rows(m):
        part = nt(r.whole_gm[m].reshape(512, 1024), r.w_out[...]).astype(BF)
        for k in range(4):
            r.grad_att[m, ring.row_chunk(k)] = part[k * TILE : (k + 1) * TILE]

    def attend(m):
        def step(qi):
            rows, window = tile_of(qi), window_of(qi)
            shut = closed_row(r.closed[m, 0:1], qi)
            for h in range(2):
                k_cols, v_cols = head(h), head(h, base=256)
                sk_cols = slice(h * 256, h * 256 + TILE)
                sv_cols = slice(h * 256 + TILE, (h + 1) * 256)
                q = qkv[m, rows, head(h)]
                d = r.grad_att[m, rows, head(h)]
                level = stats[m, rows, 2 + h : 3 + h]
                token = jnp.exp(
                    nt(q, kv_all[m, window, k_cols]) * scale + (r.table[h] + shut) - level
                )
                from_state = jnp.exp(nt(q, state_kv[m, :, sk_cols]) * scale - level)
                grad_token = nt(d, kv_all[m, window, v_cols])
                grad_from = nt(d, state_kv[m, :, sv_cols])
                delta = jnp.sum(token * grad_token, axis=-1, keepdims=True) + jnp.sum(
                    from_state * grad_from, axis=-1, keepdims=True
                )
                grad_token = token * (grad_token - delta)
                grad_from = from_state * (grad_from - delta)
                r.near[h, :, 0:128] += (
                    grad_token[:, 0:128] + grad_token[:, 128:256] + grad_token[:, 256:384]
                )
                r.near[h, :, 128:384] += grad_token[:, 384:640]
                token_low = grad_token.astype(BF)
                from_low = grad_from.astype(BF)
                grad_q = scale * (
                    nn(token_low, kv_all[m, window, k_cols]) + nn(from_low, state_kv[m, :, sk_cols])
                )
                r.dqkv[m, own_chunk(qi), :, head(h)] = grad_q.astype(BF)
                r.grad_kv[m, window, k_cols] += tn(token_low, q)
                r.grad_kv[m, window, v_cols] += tn(token.astype(BF), d)
                r.grad_state[m, :, sk_cols] += tn(from_low, q)
                r.grad_state[m, :, sv_cols] += tn(from_state.astype(BF), d)

        return step

    def pass_on(m):
        r.early[m, :, 0:256] = (scale * r.grad_kv[m, 0:512, 0:256]).astype(BF)
        r.early[m, :, 256:512] = r.grad_kv[m, 0:512, 256:512].astype(BF)
        for h in range(2):
            low = jnp.concatenate(
                [
                    (scale * r.grad_state[m, :, h * 256 : h * 256 + TILE]).astype(BF),
                    r.grad_state[m, :, h * 256 + TILE : (h + 1) * 256].astype(BF),
                ],
                1,
            )
            r.grad_prior[m, :, head(h)] = nt(low, r.state_proj.ref[h]).astype(BF)
            part = tn(r.prior.ref[m, :, head(h)], low)
            r.g_proj[h] = part if m == 0 else r.g_proj[h] + part
        there[m].start()
        shifts[m].start()

    def scan(m):
        def step(t, grad):
            b = count - 1 - t
            rows = tile_of(b, 16)
            r.held[m, rows] = grad.astype(BF)
            u = r.across.ref[m, rows].astype(F32)
            forget = jax.nn.sigmoid(r.bias[...] + r.slope[...] * u)
            moved = r.moved[m, rows].astype(F32)
            return r.keeps.ref[b, m : m + 1] * (moved + forget * grad)

        lax.fori_loop(0, count, step, jnp.zeros((16, 256), F32))

    def bucket_sums():
        row = lax.broadcasted_iota(jnp.int32, (TILE, TILE), 0)
        col = lax.broadcasted_iota(jnp.int32, (TILE, TILE), 1)
        distance = [row - col + TILE, row - col]
        for h in range(2):
            for t in range(BUCKETS):
                total = jnp.zeros((1, TILE), F32)
                for part in range(2):
                    d = distance[part]
                    inside = d >= STARTS[t]
                    if t + 1 < BUCKETS:
                        inside = inside & (d < STARTS[t + 1])
                    values = r.near[h, :, TILE * (part + 1) : TILE * (part + 2)]
                    total = total + jnp.sum(
                        jnp.where(inside, values, 0.0), axis=0, keepdims=True
                    )
                if t + 1 == BUCKETS:
                    total = total + jnp.sum(r.near[h, :, 0:TILE], axis=0, keepdims=True)
                r.sums[t : t + 1] = total
            r.g_rel[h] = lax.dot_general(
                jnp.ones((8, TILE), F32),
                r.sums[...],
                (((1,), (1,)), ((), ())),
                precision=lax.Precision.HIGHEST,
                preferred_element_type=F32,
            )

    def update_tile(m):
        def step(t):
            rows = tile_of(t)
            for h in range(2):
                cols, k_cols, v_cols = head(h), head(h, base=256), head(h, base=512)
                grad = r.grad_after[m, rows, cols].astype(F32)
                u = r.update.ref[m, rows, cols]
                inverse = inverse_rms(u)
                unit = u * inverse
                forget = jax.nn.sigmoid(r.bias[:, cols] + r.slope[:, cols] * unit)
                gate = grad * (r.prior.ref[m, rows, cols].astype(F32) - unit)
                gate = gate * forget * (1.0 - forget)
                r.g_bias[:, cols] += jnp.sum(gate, axis=0, keepdims=True)
                r.g_scale[:, cols] += jnp.sum(gate * unit, axis=0, keepdims=True)
                grad_unit = grad * (1.0 - forget) + gate * r.slope[:, cols]
                inner = jnp.mean(grad_unit * unit, axis=-1, keepdims=True)
                low = (inverse * (grad_unit - unit * inner)).astype(BF)
                q = r.state_query.ref[rows, cols]
                probs = jnp.exp(nt(q, qkv[m, :, k_cols]) * scale - stats[m, rows, h : h + 1])
                grad_probs = nt(low, qkv[m, :, v_cols])
                delta = jnp.sum(probs * grad_probs, axis=-1, keepdims=True)
                grad_scores = (probs * (grad_probs - delta)).astype(BF)
                r.g_query[rows, cols] += scale * nn(grad_scores, qkv[m, :, k_cols])
                r.grad_kv[m, 512:1024, cols] += tn(grad_scores, q)
                r.grad_kv[m, 512:1024, head(h, base=256)] += tn(probs.astype(BF), low)

        return step

    def finish_rows(m):
        def step(t):
            rows = tile_of(t)
            full = r.grad_kv[m, pl.ds(pl.multiple_of(512 + t * TILE, TILE), TILE)]
            extra = r.later[m, rows].astype(F32)
            at = own_chunk(t)
            r.dqkv[m, at, :, 256:512] = (scale * full[:, 0:256] + extra[:, 0:256]).astype(BF)
            r.dqkv[m, at, :, 512:768] = (full[:, 256:512] + extra[:, 256:512]).astype(BF)

        return step

    def out_weights(n):
        rows = tile_of(n, 256)
        part = tn(r.att_rel.ref[0].reshape(512, 256), r.whole_gm[0, :, :, rows].reshape(512, 256))
        part = part + tn(
            r.att_rel.ref[1].reshape(512, 256), r.whole_gm[1, :, :, rows].reshape(512, 256)
        )
        r.parts[rows, 768:1024] = part.astype(BF)

    def end_terms(m):
        def columns(n):
            cols = tile_of(n, 256)
            part = nt(r.dqkv[m].reshape(512, 768), r.w.ref[cols]).astype(BF)
            split_rows(branch, m, cols, part)

        loop(4, columns)

    def weight_rows(n):
        rows = slice(n * 256, (n + 1) * 256)
        whole = r.whole.ref
        part = tn(whole[0, :, :, rows].reshape(512, 256), r.dqkv[0].reshape(512, 768))
        part = part + tn(whole[1, :, :, rows].reshape(512, 256), r.dqkv[1].reshape(512, 768))
        r.parts[rows, 0:768] = part.astype(BF)
        product = part * r.w.ref[rows].astype(F32)
        high = product.astype(BF)
        low = (product - high.astype(F32)).astype(BF)
        ones = jnp.ones((8, 768), BF)
        return (nt(ones, high) + nt(ones, low))[0:1] / r.attn_gain[:, rows]

    def end_rows(m):
        grad_normed = ends[m].finish()
        rows = r.x.ref[m].astype(F32)
        inverse = inverse_rms(rows)
        unit = rows * inverse
        scaled = grad_normed * r.attn_gain[...]
        inner = jnp.mean(scaled * unit, axis=-1, keepdims=True)
        r.grad_x.ref[m] = r.grad_middle.ref[m] + inverse * (scaled - unit * inner)

    def give_seed(i, rows):
        r.total[plane.last[i]] = rows

    attention_rows(0)
    loop(2, attend(0))
    mlp_sum.advance()
    outs[0].relay()
    outs[1].relay()
    loop(2, lambda qi: attend(0)(qi + 2))
    mlp_sum.advance()
    r.prior.get()
    r.state_proj.get()
    pass_on(0)
    attention_rows(1)
    loop(2, attend(1))
    mlp_sum.advance()
    loop(2, lambda qi: attend(1)(qi + 2))
    mlp_sum.advance()
    pass_on(1)
    r.across.get()
    r.keeps.get()
    there[0].finish()
    scan(0)
    back[0].start()
    r.att_rel.get()
    loop(4, out_weights)
    mlp_sum.advance()
    there[1].finish()
    scan(1)
    back[1].start()
    bucket_sums()
    r.middle.get()
    for m in both:
        r.out.ref[m] = r.middle.ref[m] + outs[m].finish()
    r.out.put()
    r.update.get()
    r.state_query.get()
    for m in both:
        outs[m].close()
    r.w.get()
    r.whole.get()
    back[0].finish()
    loop(4, update_tile(0))
    shifts[0].wait_recv()
    loop(4, finish_rows(0))
    end_terms(0)
    ends[0].start()
    back[1].finish()
    loop(4, update_tile(1))
    shifts[1].wait_recv()
    loop(4, finish_rows(1))
    ends[0].relay()
    small = [weight_rows(n) for n in range(4)]
    small = small + [r.g_mlp_gain[:, n * 256 : (n + 1) * 256] for n in range(4)]
    small = small + [r.g_bias[...], r.g_scale[...], r.g_rel[0, 0:1], r.g_rel[1, 0:1]]
    r.parts[0:512, 1024:1280] = r.g_query[...].astype(BF)
    r.parts[512:768, 1024:1280] = r.g_proj[...].reshape(256, 256).astype(BF)
    r.parts[768:784, 1024:1280] = jnp.concatenate(small + [jnp.zeros((4, 256), F32)], 0).astype(BF)
    r.parts[784:1024, 1024:1280] = jnp.zeros((240, 256), BF)
    weights = PlaneReduce(
        plane, r.parts, give_seed, r.half, r.mid, r.into, r.quarter, r.small_mid, r.small_into
    )
    spread = PlaneGather(plane, r.total)
    weights.advance()
    end_terms(1)
    ends[1].start()
    weights.advance()
    r.x.get()
    r.grad_middle.get()
    end_rows(0)
    weights.advance()
    ends[1].relay()
    weights.advance(3)
    spread.advance()
    end_rows(1)
    r.grad_x.put()
    spread.advance(5)
    own = r.total.at[768:784, 1024:1280]
    swaps = [
        links.go(own, r.others.at[i], peer)
        for i, peer in enumerate((ring.right, opposite, ring.left))
    ]
    mlp_sum.advance(6)
    mlp_sum.close()
    weights.close()
    spread.close()
    for m in both:
        ends[m].close()
        shifts[m].wait_send()
        there[m].close()
        back[m].close()
    for swap in swaps:
        swap.wait_recv()
    r.gains[...] = r.total[768:784, 1024:1280].astype(F32) + (
        r.others[0].astype(F32) + r.others[1].astype(F32) + r.others[2].astype(F32)
    )
    for swap in swaps:
        swap.wait_send()


class Late:
    def __init__(self, source, ref, sem):
        self.ref = ref
        self.copy = pltpu.make_async_copy(source, ref, sem)
        self.copy.start()
        self.open = True

    def get(self):
        if self.open:
            self.copy.wait()
            self.open = False


class Early:
    def __init__(self, target, ref, sem):
        self.ref = ref
        self.copy = pltpu.make_async_copy(ref, target, sem)
        self.sent = False

    def put(self):
        self.copy.start()
        self.sent = True


def call(kernel, name, number, now, late, small, outs, early, scratch, semaphores):
    anywhere = pl.BlockSpec(memory_space=pl.ANY)
    in_names = list(now) + list(small) + list(late)
    out_names = list(outs) + list(early)
    own = [a.shape for a in late.values()], [a.dtype for a in late.values()]
    buffers = list(zip(*own)) + list(early.values()) + list(scratch.values())

    def run(*refs):
        n, o = len(in_names), len(out_names)
        r = types.SimpleNamespace()
        held = refs[n + o : n + o + len(buffers)]
        rest = refs[n + o + len(buffers) :]
        fetch, store = rest[0], rest[1]
        for key, ref in zip(in_names[: len(now) + len(small)], refs):
            setattr(r, key, ref)
        for i, key in enumerate(late):
            setattr(r, key, Late(refs[len(now) + len(small) + i], held[i], fetch.at[i]))
        for key, ref in zip(outs, refs[n:]):
            setattr(r, key, ref)
        stores = []
        for i, key in enumerate(early):
            result = Early(refs[n + len(outs) + i], held[len(late) + i], store.at[i])
            setattr(r, key, result)
            stores.append(result)
        for key, ref in zip(scratch, held[len(late) + len(early) :]):
            setattr(r, key, ref)
        for key, ref in zip(semaphores, rest[2:]):
            setattr(r, key, ref)
        kernel(r)
        for result in stores:
            if not result.sent:
                result.put()
            result.copy.wait()

    shapes = list(outs.values()) + list(early.values())
    results = pl.pallas_call(
        run,
        out_shape=tuple(jax.ShapeDtypeStruct(shape, kind) for shape, kind in shapes),
        in_specs=[VMEM] * len(now) + [SMEM] * len(small) + [anywhere] * len(late),
        out_specs=tuple([VMEM] * len(outs) + [anywhere] * len(early)),
        scratch_shapes=[pltpu.VMEM(shape, kind) for shape, kind in buffers]
        + [sems(max(1, len(late))), sems(max(1, len(early)))]
        + list(semaphores.values()),
        compiler_params=pltpu.CompilerParams(
            collective_id=number, has_side_effects=True, vmem_limit_bytes=LIMIT
        ),
        name=name,
    )(*now.values(), *small.values(), *late.values())
    return dict(zip(out_names, results))


def sems(*shape):
    return pltpu.SemaphoreType.DMA(shape)


def body(
    tokens_in,
    grad_out,
    flags,
    attn_gain,
    mlp_gain,
    w_qkv,
    w_out,
    rel_bias,
    state_query,
    state_proj,
    forget_bias,
    forget_scale,
    w_up,
    w_down,
):
    micros, rows, width = tokens_in.shape
    block = rows * 4
    local = w_qkv.shape[2]
    heads = rel_bias.shape[1]
    states = state_query.shape[0]
    buckets = rel_bias.shape[0]
    count = lax.axis_size("blk")
    w = w_qkv.reshape(width, 3 * local)
    keep_own = (1 - flags[:, 0]).astype(F32)
    closed = jnp.broadcast_to(
        jnp.where(flags == 0, 0.0, MASKED).astype(F32)[:, :, None], (micros, 8, 5 * TILE)
    )
    own_keep = jnp.broadcast_to(
        jnp.concatenate([keep_own, jnp.zeros((8 - micros,), F32)])[:, None], (8, local)
    )
    whole_shape = ((micros, 4, rows, width), BF)
    state_low = ((micros, states, local), BF)
    state_wide = ((micros, states, local), F32)
    rows_wide = ((micros, rows, width), F32)
    mlp_width = w_up.shape[1] + w_down.shape[1]
    exchange = dict(
        s0=sems(2),
        r0=sems(2),
        s1=sems(2, count),
        r1=sems(2, count),
        s2=sems(2, count),
        r2=sems(2, count),
        local=sems(4),
    )
    gates = dict(bias=forget_bias[None], slope=forget_scale[None])
    f = call(
        forward_kernel,
        "forward",
        1,
        dict(
            x=tokens_in,
            g=grad_out,
            attn_gain=attn_gain[None],
            mlp_gain=mlp_gain[None],
            w=w,
            state_query=state_query,
            state_proj=state_proj,
            own_keep=own_keep,
            closed=closed,
            **gates,
        ),
        dict(w_out=w_out, w_up=w_up, w_down=w_down),
        dict(rel=rel_bias),
        dict(
            grad_middle=rows_wide,
            whole_gm=whole_shape,
            seeds=((2, 16, mlp_width), BF),
            g_gain=((1, width), F32),
        ),
        dict(
            whole=whole_shape,
            qkv=((micros, block, 3 * local), BF),
            kv_all=((micros, 2 * block, 2 * local), BF),
            state_kv=((micros, states, 2 * local), BF),
            prior=state_low,
            across=state_low,
            keeps=((count, 8, local), F32),
            update=state_wide,
            stats=((micros, block, TILE), F32),
            table=((heads, TILE, 5 * TILE), F32),
            state_after=state_wide,
            att_rel=((micros, 4, rows, local), BF),
            middle=rows_wide,
            branch=whole_shape,
        ),
        dict(
            whole_grad=whole_shape,
            unit_low=state_low,
            held=state_low,
            terms=whole_shape,
            whole_mlp=whole_shape,
            active=((micros, block, w_up.shape[1]), BF),
            grad_hidden=((micros, block, w_up.shape[1]), BF),
            mids=((4, 4, rows // 2, width), BF),
            intos=((4, 2, rows, width), BF),
            parts=((width, mlp_width), BF),
            **reduce_scratch(mlp_width),
        ),
        dict(send=sems(104), recv=sems(104), s3=sems(count), r3=sems(count), **exchange),
    )
    b = call(
        backward_kernel,
        "backward",
        2,
        dict(
            whole_gm=f["whole_gm"],
            w_out=w_out,
            qkv=f["qkv"],
            kv_all=f["kv_all"],
            state_kv=f["state_kv"],
            stats=f["stats"],
            table=f["table"],
            closed=closed,
            seeds=f["seeds"],
            attn_gain=attn_gain[None],
            g_mlp_gain=f["g_gain"],
            **gates,
        ),
        dict(
            branch=f["branch"],
            prior=f["prior"],
            state_proj=state_proj,
            across=f["across"],
            keeps=f["keeps"],
            att_rel=f["att_rel"],
            middle=f["middle"],
            update=f["update"],
            state_query=state_query,
            w=w,
            whole=f["whole"],
            x=tokens_in,
            grad_middle=f["grad_middle"],
        ),
        {},
        dict(
            total_mlp=((width, mlp_width), BF),
            total=((width, 1280), BF),
            gains=((16, local), F32),
        ),
        dict(out=rows_wide, grad_x=rows_wide),
        dict(
            dqkv=((micros, 4, rows, 3 * local), BF),
            g_query=((states, local), F32),
            g_proj=(state_proj.shape, F32),
            g_rel=((heads, 8, local), F32),
            g_bias=((1, local), F32),
            g_scale=((1, local), F32),
            grad_att=((micros, block, local), BF),
            grad_kv=((micros, 2 * block, 2 * local), F32),
            grad_state=((micros, states, 2 * local), F32),
            early=((micros, block, 2 * local), BF),
            later=((micros, block, 2 * local), BF),
            grad_prior=state_low,
            moved=state_low,
            held=state_low,
            grad_after=state_low,
            near=((heads, TILE, 3 * TILE), F32),
            sums=((local, TILE), F32),
            mids=((4, 4, rows // 2, width), BF),
            intos=((4, 2, rows, width), BF),
            others=((3, 16, local), BF),
            parts=((width, 1280), BF),
            **reduce_scratch(1280),
        ),
        dict(send=sems(104), recv=sems(104), **exchange),
    )
    total, g_mlp, gains = b["total"], b["total_mlp"], b["gains"]
    g_out = jnp.concatenate(
        [total[n * 256 : (n + 1) * 256, 768:1024] for n in range(4)], 1
    ).astype(F32)
    side = total[:784, 1024:1280].astype(F32)
    return (
        b["out"],
        b["grad_x"],
        f["state_after"][:, None],
        gains[0:4].reshape(width),
        gains[4:8].reshape(width),
        total[:, 0:768].astype(F32).reshape(width, 3, local),
        g_out,
        jnp.transpose(side[778:780, :buckets]),
        side[:512],
        side[512:768].reshape(state_proj.shape),
        side[776],
        side[777],
        g_mlp[:, :1024].astype(F32),
        g_mlp[:, 1024:].astype(F32),
    )


def solution(mesh):
    return jax.shard_map(
        body,
        mesh=mesh,
        in_specs=(
            P(None, ("blk", "head"), None),
            P(None, ("blk", "head"), None),
            P(None, "blk"),
            P(),
            P(),
            P(None, None, "head"),
            P("head", None),
            P(None, "head"),
            P(None, "head"),
            P("head", None, None),
            P("head"),
            P("head"),
            P(None, "head"),
            P("head", None),
        ),
        out_specs=(
            P(None, ("blk", "head"), None),
            P(None, ("blk", "head"), None),
            P(None, "blk", None, "head"),
            P(),
            P(),
            P(None, None, "head"),
            P("head", None),
            P(None, "head"),
            P(None, "head"),
            P("head", None, None),
            P("head"),
            P("head"),
            P(None, "head"),
            P("head", None),
        ),
        check_vma=False,
    )
```

time: 424 us -> 309 us (0.73)
  waiting for transfers between devices: 122 us -> 0 us
  Pallas kernels: 254 us -> 277 us
  between operations: 14.3 us -> 0.71 us
    psum x1 -> x0, waiting for transfers between devices: 119 us -> none  [summed(): return lax.psum(values.astype(BF), 'blk').astype(F32)]
    pallas_call x5 -> x2, Pallas kernels: 254 us -> 277 us  [call(): pl.pallas_call(run, out_shape=tuple((jax.ShapeDtypeStruct(shape, kind) fo...]
    unnamed x38 -> x17, local copies, waits for them, and re-layouts: 9.26 us -> 12.2 us
    convert_element_type x6 -> x4, other arithmetic: 10.2 us -> 8.55 us  [the longest x1 6.75 us: body(): g_mlp[:, 1024:].astype(F32)]
  transfers between devices with their start and end apart: 3 -> 0, of which waited for: 2 -> 0; matrix products, arithmetic and copies ran while one was open for 1% -> 0% of each run, Pallas kernels for 0% -> 0%
where the time goes in v3:
time: 309 us
  Pallas kernels  277 us (90%)
  local copies, waits for them, and re-layouts  21.3 us (7%)
  other arithmetic  9.44 us (3%)
    pallas_call x2, Pallas kernels, call(): pl.pallas_call(run, out_shape=tuple((jax.ShapeDtypeStruct(shape, kind) fo...  277 us
    unnamed x17, local copies, waits for them, and re-layouts  12.2 us
    convert_element_type x1, other arithmetic, body(): g_mlp[:, 1024:].astype(F32)  6.75 us

profile of v3, /device:TPU:1, one launch (start us, length us, event | category | flops | bytes accessed | tf_op | source)
XLA Modules:
  0.0 309.0 jit_solution(17144559751480616552)
XLA Ops:
  0.6 0.7 fusion
  1.3 0.7 convert_bitcast_fusion
  2.0 0.7 broadcast_in_dim.40.refs_7_
  2.6 1.4 copy.34.refs_11_
  4.0 0.7 broadcast_in_dim.44.refs_8_.refs_7_
  4.7 1.7 copy.32
  6.4 1.6 copy.33.refs_4_.refs_22_
  8.0 156.9 %forward.1 = (f32[2,128,1024]{2,1,0:T(8,128)}, bf16[2,4,128,1024]{3,2,1,0:T(8,128)(2,1)}, bf16[2,16,2048]{2,1,0:T(8,128)(2,1)}, f32[1,1024]{1,0:T(1,128)}, bf16[...) custom-call(bf16[2,128,1024]{2,1,0:T(8,128)(2,1)} %refs_24_.1, ...), custom_call_target="tpu_custom_call" | custom-call | tf_op jit(solution)/shard_map/forward/pallas_call | solution.py:1110
  164.9 120.6 %backward.1 = (bf16[1024,2048]{1,0:T(8,128)(2,1)}, bf16[1024,1280]{1,0:T(8,128)(2,1)}, f32[16,256]{1,0:T(8,128)}, f32[2,128,1024]{2,1,0:T(8,128)}, f32[2,128,1024]{2,1,0:T(8,128)}) custom-call(bf16[2,4,128,1024]{3,2,1,0:T(8,128)(2,1)} %get-tuple-element.37.refs_0_, bf16[256,1024]{1,0:T(8,128)(2,1)} %refs_1_.3, ...), custom_call_target="tpu_custom_call" | custom-call | tf_op jit(solution)/shard_map/backward/pallas_call | solution.py:1110
  285.5 0.0 copy-start
  285.5 0.9 slice_bitcast_fusion
  286.4 0.6 copy.40
  287.0 0.6 copy.39
  287.6 1.1 fusion.1
  288.7 1.1 maximum_convert_fusion
  289.8 0.0 copy-done
  289.8 0.1 slice_convert_fusion.3
  289.9 0.6 slice_bitcast_fusion.2
  290.4 0.6 fusion.2
  291.0 0.7 slice.62
  291.7 0.8 slice.61
  292.5 0.2 slice_convert_fusion.2
  292.8 2.4 copy.36
  295.1 3.5 %copy.38 = f32[1024,3,256]{2,0,1:T(8,128)} copy(f32[1024,3,256]{0,2,1:T(8,128)} %bitcast.24) | data formatting | bytes 6291456
  298.7 0.0 copy-start.3
  298.7 6.8 %slice_convert_fusion = (f32[1024,1024]{1,0:T(8,128)}, f32[1024,1024]{1,0:T(8,128)}) fusion(bf16[1024,2048]{1,0:T(8,128)(2,1)} %get-tuple-element.59), kind=kLoop, calls=%fused_computation | loop fusion | flops 2097152 | bytes 12582912 | tf_op jit(solution)/shard_map/convert_element_type | solution.py:1316
  305.4 0.0 copy-done.3
  305.4 1.0 copy.44
  306.4 0.6 copy-done.2
  307.0 1.0 copy.45
  308.0 0.0 copy-done.1
  308.0 1.0 copy.46
  (3 shorter events, 0.0 us)
Async XLA Ops:
  285.5 4.3 %copy-start = (bf16[1024,1280]{1,0:T(8,128)(2,1)S(1)}, bf16[1024,1280]{1,0:T(8,128)(2,1)}, u32[]{:S(2)}) copy-start(bf16[1024,1280]{1,0:T(8,128)(2,1)} %get-tuple-element.58) | copy-start | bytes 7864324
  298.7 6.8 %copy-start.3 = (f32[2,128,1024]{2,1,0:T(8,128)S(1)}, f32[2,128,1024]{2,1,0:T(8,128)}, u32[]{:S(2)}) copy-start(f32[2,128,1024]{2,1,0:T(8,128)} %get-tuple-element.112) | copy-start | bytes 3145732
  305.4 1.6 copy-start.2
  305.4 2.6 copy-start.1

commit v4 on v3

--- a/solution.py
+++ b/solution.py
@@ -90,6 +90,7 @@
         self.links, self.me = links, me
         self.right = device(lax.rem(me + 1, 4))
         self.left = device(lax.rem(me + 3, 4))
+        self.opposite = device(lax.rem(me + 2, 4))
 
     def go(self, src, dst, peer):
         return self.links.go(src, dst, peer)
@@ -238,20 +239,17 @@
 
 
 class PlaneReduce(Steps):
-    def __init__(self, plane, parts, result, half, mid, into, quarter, small_mid, small_into):
+    def __init__(self, plane, parts, result, extra, half, mid, into, quarter, small_into):
         self.plane, self.parts, self.result, self.half = plane, parts, result, half
-        self.quarter = quarter
+        self.quarter, self.extra = quarter, extra
         first, second = plane.first, plane.second
         self.reduce1 = [
             Reduce(first[i], by_columns(half, i * 256, 64, first[i].chunk), mid.at[i], into.at[i])
             for i in range(2)
         ]
         self.reduce2 = [
-            Reduce(
-                second[i],
-                by_columns(quarter.at[i], 0, 16, second[i].chunk),
-                small_mid.at[i],
-                small_into.at[i],
+            ReduceDirect(
+                second[i], by_columns(quarter.at[i], 0, 16, second[i].chunk), small_into.at[i]
             )
             for i in range(2)
         ]
@@ -260,7 +258,6 @@
             self.start1,
             lambda: [r.relay() for r in self.reduce1],
             self.start2,
-            lambda: [r.relay() for r in self.reduce2],
             self.finish,
         ]
 
@@ -279,6 +276,7 @@
             ).astype(BF)
 
         loop(8, add)
+        self.extra()
         for r in self.reduce1:
             r.start()
 
@@ -302,7 +300,7 @@
         self.plane, self.total = plane, total
         first, second = plane.first, plane.second
         self.gather1 = [
-            Gather(second[i], by_columns(total, plane.top[i], 16, second[i].chunk))
+            GatherDirect(second[i], by_columns(total, plane.top[i], 16, second[i].chunk))
             for i in range(2)
         ]
         self.gather2 = [
@@ -311,7 +309,6 @@
         ]
         self.steps = [
             lambda: [g.start() for g in self.gather1],
-            lambda: [g.relay() for g in self.gather1],
             self.start2,
             lambda: [g.relay() for g in self.gather2],
             self.cores,
@@ -341,9 +338,52 @@
         mid=((2, 4, 64, width // 2), BF),
         into=((2, 2, 64, width), BF),
         quarter=((2, 64, width), BF),
-        small_mid=((2, 4, 16, width // 2), BF),
-        small_into=((2, 2, 16, width), BF),
+        small_into=((2, 3, 16, width), BF),
     )
+
+
+class GatherDirect:
+    def __init__(self, ring, piece):
+        self.ring, self.piece = ring, piece
+
+    def start(self):
+        r, p = self.ring, self.piece
+        self.copies = [
+            r.go(p(0), p(4 - k, None, k), peer)
+            for k, peer in ((1, r.right), (3, r.left), (2, r.opposite))
+        ]
+
+    def finish(self):
+        for copy in self.copies:
+            copy.wait_recv()
+
+    def close(self):
+        for copy in self.copies:
+            copy.wait_send()
+
+
+class ReduceDirect:
+    def __init__(self, ring, terms, into):
+        self.ring, self.terms, self.into = ring, terms, into
+
+    def start(self):
+        r, t = self.ring, self.terms
+        self.copies = [
+            r.go(t(k), self.into.at[k - 1], peer)
+            for k, peer in ((1, r.right), (3, r.left), (2, r.opposite))
+        ]
+
+    def finish(self):
+        for copy in self.copies:
+            copy.wait_recv()
+        total = self.terms(0)[...].astype(F32)
+        for k in range(3):
+            total = total + self.into[k].astype(F32)
+        return total
+
+    def close(self):
+        for copy in self.copies:
+            copy.wait_send()
 
 
 class Exchange:
@@ -393,9 +433,9 @@
     return count - 1
 
 
-def closed_row(closed, qi):
-    column = lax.broadcasted_iota(jnp.int32, closed.shape, 1) + qi * TILE
-    return jnp.where(column < 512, closed, 0.0)
+def closed_row(flag, qi):
+    column = lax.broadcasted_iota(jnp.int32, (1, 5 * TILE), 1) + qi * TILE
+    return jnp.where(column < 512, MASKED * flag.astype(F32), 0.0)
 
 
 def head(h, size=TILE, base=0):
@@ -415,15 +455,15 @@
     row = lax.broadcasted_iota(jnp.int32, (TILE, TILE), 0)
     col = lax.broadcasted_iota(jnp.int32, (TILE, TILE), 1)
     for h in range(2):
-        far = jnp.full((TILE, TILE), rel[BUCKETS - 1, h], F32)
+        far = jnp.full((TILE, TILE), rel[h, BUCKETS - 1], F32)
         table[h, :, 0:128] = jnp.where(row < col, far, MASKED)
         table[h, :, 128:256] = far
         table[h, :, 256:384] = far
         for shift, at in ((TILE, 384), (0, 512)):
             distance = row - col + shift
-            total = jnp.full((TILE, TILE), rel[0, h], F32)
+            total = jnp.full((TILE, TILE), rel[h, 0], F32)
             for t in range(1, BUCKETS):
-                total = jnp.where(distance >= STARTS[t], rel[t, h], total)
+                total = jnp.where(distance >= STARTS[t], rel[h, t], total)
             table[h, :, at : at + TILE] = jnp.where(distance >= 0, total, MASKED)
 
 
@@ -434,10 +474,17 @@
     plane = Plane(links)
     place, count = lax.axis_index("blk"), lax.axis_size("blk")
     both = range(2)
-    for m in both:
+
+    def norm_rows(m):
         rows = r.x[m].astype(F32)
         r.whole.ref[m, 0] = (rows * inverse_rms(rows) * r.attn_gain[...]).astype(BF)
+
+    norm_rows(0)
+    for m in both:
         r.whole_grad[m, 0] = r.g[m]
+        keep = 1.0 - r.flags[0, m].astype(F32)
+        r.own_keep[m : m + 1] = jnp.full((1, 256), keep, F32)
+    r.own_keep[2:8] = jnp.zeros((6, 256), F32)
     pl.semaphore_wait(pltpu.get_barrier_semaphore(), ring.greet() + greet_blocks())
     whole, qkv, kv_all = r.whole.ref, r.qkv.ref, r.kv_all.ref
     prior, across, keeps = r.prior.ref, r.across.ref, r.keeps.ref
@@ -445,8 +492,8 @@
     table, att_rel, middle, branch = r.table.ref, r.att_rel.ref, r.middle.ref, r.branch.ref
     gather_x = [Gather(ring, by_rows(whole.at[m])) for m in both]
     gather_g = [Gather(ring, by_rows(r.whole_grad.at[m])) for m in both]
-    for m in both:
-        gather_x[m].start()
+    gather_x[0].start()
+    norm_rows(1)
 
     def tell(j):
         peer = {"blk": lax.rem(place + j, count)}
@@ -473,7 +520,7 @@
     def project(m):
         def columns(n):
             cols = tile_of(n, 256)
-            part = nn(whole[m].reshape(512, 1024), r.w[:, cols]).astype(BF)
+            part = nn(whole[m].reshape(512, 1024), r.w[n]).astype(BF)
             for k in range(4):
                 qkv[m, ring.row_chunk(k), cols] = part[k * TILE : (k + 1) * TILE]
 
@@ -525,7 +572,7 @@
     def attend(m):
         def step(qi):
             rows, window = tile_of(qi), window_of(qi)
-            shut = closed_row(r.closed[m, 0:1], qi)
+            shut = closed_row(r.flags[0, m], qi)
             for h in range(2):
                 q = qkv[m, rows, head(h)]
                 token = nt(q, kv_all[m, window, head(h)]) * scale + (table[h] + shut)
@@ -554,7 +601,7 @@
     third = [
         Reduce(ring, by_rows(r.terms.at[m]), r.mids.at[2 + m], r.intos.at[2 + m]) for m in both
     ]
-    fourth = [Gather(ring, by_rows(r.whole_gm.at[m])) for m in both]
+    fourth = Gather(ring, by_rows(r.gm0))
 
     def out_terms(m):
         def columns(n):
@@ -582,7 +629,7 @@
             )
             r.grad_hidden[m, :, cols] = (grad_active * rise).astype(BF)
 
-        loop(4, columns)
+        return columns
 
     def grad_terms(m):
         def columns(n):
@@ -611,7 +658,8 @@
         inner = jnp.mean(scaled * unit, axis=-1, keepdims=True)
         total = r.g[m].astype(F32) + inverse * (scaled - unit * inner)
         r.grad_middle[m] = total
-        r.whole_gm[m, 0] = total.astype(BF)
+        if m == 0:
+            r.gm0[0] = total.astype(BF)
 
     def up_rows(n):
         rows = tile_of(n, 256)
@@ -629,18 +677,18 @@
         r.seeds[i] = rows
 
     weights = PlaneReduce(
-        plane, r.parts, keep_seed, r.half, r.mid, r.into, r.quarter, r.small_mid, r.small_into
+        plane, r.parts, keep_seed, lambda: None, r.half, r.mid, r.into, r.quarter, r.small_into
     )
 
     gather_x[0].relay()
-    gather_x[1].relay()
+    gather_x[1].start()
     gather_x[0].finish()
     project(0)
+    gather_x[1].relay()
     loop(4, update_tile(0))
     there[0].start()
     gather_x[1].finish()
     gather_g[0].start()
-    gather_g[1].start()
     project(1)
     r.whole.put()
     r.qkv.put()
@@ -648,14 +696,15 @@
     there[1].start()
     r.update.put()
     gather_g[0].relay()
+    gather_g[1].start()
     loop(count - 1, lambda j: tell(j + 1).wait_recv())
     there[0].finish()
     scan(0)
     back[0].start()
-    gather_g[1].relay()
     there[1].finish()
     scan(1)
     back[1].start()
+    gather_g[1].relay()
     r.across.put()
     r.keeps.put()
     shifts[0].wait_recv()
@@ -672,9 +721,9 @@
     loop(4, state(1))
     r.state_kv.put()
     r.state_after.put()
-    loop(2, attend(1))
+    loop(1, attend(1))
     first[0].relay()
-    loop(2, lambda qi: attend(1)(qi + 2))
+    loop(3, lambda qi: attend(1)(qi + 1))
     r.stats.put()
     out_terms(1)
     r.att_rel.put()
@@ -683,46 +732,46 @@
     second[0].start()
     first[1].relay()
     second[0].relay()
+    r.w_up.get()
+    r.w_down.get()
+    gather_g[0].finish()
+    gather_g[1].finish()
     normalise(1)
     second[1].start()
     r.middle.put()
-    r.w_up.get()
-    r.w_down.get()
-    gather_g[0].finish()
     second[0].finish()
-    hidden(0)
+    loop(2, hidden(0))
     second[1].relay()
+    loop(2, lambda n: hidden(0)(n + 2))
     first[0].close()
     grad_terms(0)
     third[0].start()
-    branch_terms(0)
+    second[1].finish()
+    loop(2, hidden(1))
     third[0].relay()
-    gather_g[1].finish()
-    second[1].finish()
-    hidden(1)
+    loop(2, lambda n: hidden(1)(n + 2))
     first[1].close()
     grad_terms(1)
     third[1].start()
+    loop(4, up_rows)
     grad_rows(0)
-    fourth[0].start()
-    loop(1, up_rows)
+    fourth.start()
     third[1].relay()
-    fourth[0].relay()
-    loop(3, lambda n: up_rows(n + 1))
-    grad_rows(1)
-    fourth[1].start()
-    loop(2, down_rows)
-    fourth[1].relay()
-    loop(2, lambda n: down_rows(n + 2))
+    loop(4, down_rows)
+    weights.advance()
+    fourth.relay()
+    branch_terms(0)
     weights.advance()
     branch_terms(1)
     r.branch.put()
-    weights.advance(5)
+    weights.advance()
+    grad_rows(1)
+    weights.advance(2)
+    fourth.finish()
+    weights.close()
+    fourth.close()
     for m in both:
-        fourth[m].finish()
-    weights.close()
-    for m in both:
-        for step in (gather_x, gather_g, second, third, fourth):
+        for step in (gather_x, gather_g, second, third):
             step[m].close()
         shifts[m].wait_send()
         there[m].close()
@@ -735,14 +784,22 @@
     links = Links(r.send, r.recv)
     ring = head_ring(links)
     plane = Plane(links)
-    opposite = {"head": ring.chunk(2)}
     place, count = lax.axis_index("blk"), lax.axis_size("blk")
     both = range(2)
     r.total_mlp[plane.last[0]] = r.seeds[0]
     r.total_mlp[plane.last[1]] = r.seeds[1]
+    gm = [r.gm0, r.gm1]
+    r.gm1[0] = r.grad_middle[1].astype(BF)
+    core = place % 2
+    others = [
+        {"head": ring.chunk(k), "blk": place - core + c} for k in range(1, 4) for c in range(2)
+    ]
     barrier = pltpu.get_barrier_semaphore()
-    pl.semaphore_signal(barrier, inc=1, device_id=opposite, device_id_type=MESH)
-    pl.semaphore_wait(barrier, 1 + ring.greet() + greet_blocks())
+    for device in others:
+        pl.semaphore_signal(barrier, inc=1, device_id=device, device_id_type=MESH)
+    pl.semaphore_wait(barrier, len(others) + greet_blocks())
+    fourth = Gather(ring, by_rows(r.gm1))
+    fourth.start()
     mlp_sum = PlaneGather(plane, r.total_mlp)
     mlp_sum.advance()
     qkv, kv_all, state_kv, stats = r.qkv, r.kv_all, r.state_kv, r.stats
@@ -752,8 +809,6 @@
     ends = [
         Reduce(ring, by_rows(branch.at[m]), r.mids.at[2 + m], r.intos.at[2 + m]) for m in both
     ]
-    for m in both:
-        outs[m].start()
     before = {"blk": lax.rem(place + count - 1, count)}
     shifts = [
         remote(r.early.at[m], r.later.at[m], r.s0.at[m], r.r0.at[m], before) for m in both
@@ -773,14 +828,14 @@
         return lax.rem(qi + 4 - ring.me, 4)
 
     def attention_rows(m):
-        part = nt(r.whole_gm[m].reshape(512, 1024), r.w_out[...]).astype(BF)
+        part = nt(gm[m][...].reshape(512, 1024), r.w_out[...]).astype(BF)
         for k in range(4):
             r.grad_att[m, ring.row_chunk(k)] = part[k * TILE : (k + 1) * TILE]
 
     def attend(m):
         def step(qi):
             rows, window = tile_of(qi), window_of(qi)
-            shut = closed_row(r.closed[m, 0:1], qi)
+            shut = closed_row(r.flags[0, m], qi)
             for h in range(2):
                 k_cols, v_cols = head(h), head(h, base=256)
                 sk_cols = slice(h * 256, h * 256 + TILE)
@@ -913,16 +968,20 @@
 
     def out_weights(n):
         rows = tile_of(n, 256)
-        part = tn(r.att_rel.ref[0].reshape(512, 256), r.whole_gm[0, :, :, rows].reshape(512, 256))
+        part = tn(r.att_rel.ref[0].reshape(512, 256), gm[0][:, :, rows].reshape(512, 256))
         part = part + tn(
-            r.att_rel.ref[1].reshape(512, 256), r.whole_gm[1, :, :, rows].reshape(512, 256)
+            r.att_rel.ref[1].reshape(512, 256), gm[1][:, :, rows].reshape(512, 256)
         )
         r.parts[rows, 768:1024] = part.astype(BF)
 
     def end_terms(m):
         def columns(n):
             cols = tile_of(n, 256)
-            part = nt(r.dqkv[m].reshape(512, 768), r.w.ref[cols]).astype(BF)
+            part = nt(r.dqkv[m, :, :, 0:256].reshape(512, 256), r.w.ref[0, cols])
+            for p in (1, 2):
+                some = r.dqkv[m, :, :, p * 256 : (p + 1) * 256].reshape(512, 256)
+                part = part + nt(some, r.w.ref[p, cols])
+            part = part.astype(BF)
             split_rows(branch, m, cols, part)
 
         loop(4, columns)
@@ -933,7 +992,7 @@
         part = tn(whole[0, :, :, rows].reshape(512, 256), r.dqkv[0].reshape(512, 768))
         part = part + tn(whole[1, :, :, rows].reshape(512, 256), r.dqkv[1].reshape(512, 768))
         r.parts[rows, 0:768] = part.astype(BF)
-        product = part * r.w.ref[rows].astype(F32)
+        product = part * jnp.concatenate([r.w.ref[p, rows] for p in range(3)], 1).astype(F32)
         high = product.astype(BF)
         low = (product - high.astype(F32)).astype(BF)
         ones = jnp.ones((8, 768), BF)
@@ -946,27 +1005,58 @@
         unit = rows * inverse
         scaled = grad_normed * r.attn_gain[...]
         inner = jnp.mean(scaled * unit, axis=-1, keepdims=True)
-        r.grad_x.ref[m] = r.grad_middle.ref[m] + inverse * (scaled - unit * inner)
+        r.grad_x.ref[m] = r.grad_middle[m] + inverse * (scaled - unit * inner)
 
     def give_seed(i, rows):
         r.total[plane.last[i]] = rows
 
+    def share(i):
+        k, c = i // 2 + 1, i % 2
+        slot = (3 - k) * 2 + core
+        return remote(
+            r.parts.at[768:784, 1024:1280],
+            r.others.at[slot],
+            r.s3.at[i],
+            r.r3.at[slot],
+            others[i],
+        )
+
+    def got(i):
+        return remote(
+            r.parts.at[768:784, 1024:1280], r.others.at[i], r.s3.at[i], r.r3.at[i], others[i]
+        )
+
+    def add_gains():
+        for i in range(6):
+            got(i).wait_recv()
+        total = r.others[0].astype(F32)
+        for i in range(1, 6):
+            total = total + r.others[i].astype(F32)
+        row = lax.broadcasted_iota(jnp.int32, (16, 256), 0)
+        total = jnp.where(row < 8, total, 0.0) * core.astype(F32)
+        at = slice(256, 272), slice(1024, 1280)
+        r.half[at] = (r.half[at].astype(F32) + total).astype(BF)
+
     attention_rows(0)
-    loop(2, attend(0))
+    fourth.relay()
+    loop(1, attend(0))
     mlp_sum.advance()
-    outs[0].relay()
-    outs[1].relay()
-    loop(2, lambda qi: attend(0)(qi + 2))
+    loop(2, lambda qi: attend(0)(qi + 1))
     mlp_sum.advance()
+    loop(1, lambda qi: attend(0)(qi + 3))
     r.prior.get()
     r.state_proj.get()
     pass_on(0)
+    fourth.finish()
     attention_rows(1)
+    outs[0].start()
     loop(2, attend(1))
     mlp_sum.advance()
+    outs[0].relay()
+    outs[1].start()
     loop(2, lambda qi: attend(1)(qi + 2))
-    mlp_sum.advance()
     pass_on(1)
+    outs[1].relay()
     r.across.get()
     r.keeps.get()
     there[0].finish()
@@ -974,11 +1064,11 @@
     back[0].start()
     r.att_rel.get()
     loop(4, out_weights)
-    mlp_sum.advance()
+    bucket_sums()
     there[1].finish()
     scan(1)
     back[1].start()
-    bucket_sums()
+    mlp_sum.advance()
     r.middle.get()
     for m in both:
         r.out.ref[m] = r.middle.ref[m] + outs[m].finish()
@@ -1008,44 +1098,35 @@
     r.parts[768:784, 1024:1280] = jnp.concatenate(small + [jnp.zeros((4, 256), F32)], 0).astype(BF)
     r.parts[784:1024, 1024:1280] = jnp.zeros((240, 256), BF)
     weights = PlaneReduce(
-        plane, r.parts, give_seed, r.half, r.mid, r.into, r.quarter, r.small_mid, r.small_into
+        plane, r.parts, give_seed, add_gains, r.half, r.mid, r.into, r.quarter, r.small_into
     )
     spread = PlaneGather(plane, r.total)
     weights.advance()
+    for i in range(6):
+        share(i).start()
     end_terms(1)
     ends[1].start()
     weights.advance()
     r.x.get()
-    r.grad_middle.get()
     end_rows(0)
     weights.advance()
     ends[1].relay()
-    weights.advance(3)
-    spread.advance()
+    weights.advance(2)
+    spread.advance(2)
     end_rows(1)
     r.grad_x.put()
-    spread.advance(5)
-    own = r.total.at[768:784, 1024:1280]
-    swaps = [
-        links.go(own, r.others.at[i], peer)
-        for i, peer in enumerate((ring.right, opposite, ring.left))
-    ]
-    mlp_sum.advance(6)
+    spread.advance(3)
     mlp_sum.close()
     weights.close()
     spread.close()
+    fourth.close()
+    for i in range(6):
+        share(i).wait_send()
     for m in both:
         ends[m].close()
         shifts[m].wait_send()
         there[m].close()
         back[m].close()
-    for swap in swaps:
-        swap.wait_recv()
-    r.gains[...] = r.total[768:784, 1024:1280].astype(F32) + (
-        r.others[0].astype(F32) + r.others[1].astype(F32) + r.others[2].astype(F32)
-    )
-    for swap in swaps:
-        swap.wait_send()
 
 
 class Late:
@@ -1123,6 +1204,55 @@
     return dict(zip(out_names, results))
 
 
+def finish_kernel(total, g_mlp, out, grad_x, state, *refs):
+    results, (wide, low, pieces, rows_in, states_in, fetch, store) = refs[:11], refs[11:]
+    places = [rows_in.at[0], rows_in.at[1], states_in]
+    taken = [
+        pltpu.make_async_copy(a, b, fetch.at[8 + i])
+        for i, (a, b) in enumerate(zip((out, grad_x, state), places))
+    ]
+    passed = [
+        pltpu.make_async_copy(a, b, store.at[i])
+        for i, (a, b) in enumerate(zip(places, results[:3]))
+    ]
+    g_up, g_down, g_qkv, g_out, g_query, g_proj, gains, others = results[3:]
+    loads = []
+    for n in range(4):
+        rows = slice(n * 256, (n + 1) * 256)
+        loads.append(pltpu.make_async_copy(g_mlp.at[rows], low.at[rows], fetch.at[n]))
+        loads.append(pltpu.make_async_copy(total.at[rows], pieces.at[rows], fetch.at[4 + n]))
+    for copy in loads + taken:
+        copy.start()
+    stores = []
+
+    def put(value, at, target):
+        wide[at] = value.astype(F32)
+        copy = pltpu.make_async_copy(wide.at[at], target, store.at[3 + len(stores)])
+        copy.start()
+        stores.append(copy)
+
+    for n in range(4):
+        rows = slice(n * 256, (n + 1) * 256)
+        loads[2 * n].wait()
+        put(low[rows, 0:1024], (rows, slice(0, 1024)), g_up.at[rows])
+        put(low[rows, 1024:2048], (rows, slice(1024, 2048)), g_down.at[rows])
+        loads[2 * n + 1].wait()
+        for p in range(3):
+            cols = slice(p * 256, (p + 1) * 256)
+            put(pieces[rows, cols], (rows, slice(2048 + p * 256, 2304 + p * 256)), g_qkv.at[p, rows])
+        put(pieces[rows, 768:1024], (rows, slice(2816, 3072)), g_out.at[:, rows])
+    put(pieces[0:512, 1024:1280], (slice(0, 512), slice(3072, 3328)), g_query)
+    put(pieces[512:768, 1024:1280], (slice(512, 768), slice(3072, 3328)), g_proj)
+    for into, copy in zip(taken, passed):
+        into.wait()
+        copy.start()
+    small = pieces[768:784, 1024:1280].astype(F32)
+    gains[...] = small[0:8]
+    others[...] = small[8:16]
+    for copy in stores + passed:
+        copy.wait()
+
+
 def sems(*shape):
     return pltpu.SemaphoreType.DMA(shape)
 
@@ -1150,14 +1280,8 @@
     states = state_query.shape[0]
     buckets = rel_bias.shape[0]
     count = lax.axis_size("blk")
-    w = w_qkv.reshape(width, 3 * local)
-    keep_own = (1 - flags[:, 0]).astype(F32)
-    closed = jnp.broadcast_to(
-        jnp.where(flags == 0, 0.0, MASKED).astype(F32)[:, :, None], (micros, 8, 5 * TILE)
-    )
-    own_keep = jnp.broadcast_to(
-        jnp.concatenate([keep_own, jnp.zeros((8 - micros,), F32)])[:, None], (8, local)
-    )
+    w = jnp.transpose(w_qkv, (1, 0, 2))
+    small = dict(flags=jnp.transpose(flags))
     whole_shape = ((micros, 4, rows, width), BF)
     state_low = ((micros, states, local), BF)
     state_wide = ((micros, states, local), F32)
@@ -1185,15 +1309,13 @@
             w=w,
             state_query=state_query,
             state_proj=state_proj,
-            own_keep=own_keep,
-            closed=closed,
             **gates,
         ),
         dict(w_out=w_out, w_up=w_up, w_down=w_down),
-        dict(rel=rel_bias),
+        dict(rel=jnp.transpose(rel_bias), **small),
         dict(
             grad_middle=rows_wide,
-            whole_gm=whole_shape,
+            gm0=((4, rows, width), BF),
             seeds=((2, 16, mlp_width), BF),
             g_gain=((1, width), F32),
         ),
@@ -1215,6 +1337,7 @@
         ),
         dict(
             whole_grad=whole_shape,
+            own_keep=((8, local), F32),
             unit_low=state_low,
             held=state_low,
             terms=whole_shape,
@@ -1233,14 +1356,14 @@
         "backward",
         2,
         dict(
-            whole_gm=f["whole_gm"],
+            gm0=f["gm0"],
+            grad_middle=f["grad_middle"],
             w_out=w_out,
             qkv=f["qkv"],
             kv_all=f["kv_all"],
             state_kv=f["state_kv"],
             stats=f["stats"],
             table=f["table"],
-            closed=closed,
             seeds=f["seeds"],
             attn_gain=attn_gain[None],
             g_mlp_gain=f["g_gain"],
@@ -1259,13 +1382,11 @@
             w=w,
             whole=f["whole"],
             x=tokens_in,
-            grad_middle=f["grad_middle"],
         ),
-        {},
+        small,
         dict(
             total_mlp=((width, mlp_width), BF),
             total=((width, 1280), BF),
-            gains=((16, local), F32),
         ),
         dict(out=rows_wide, grad_x=rows_wide),
         dict(
@@ -1288,32 +1409,61 @@
             sums=((local, TILE), F32),
             mids=((4, 4, rows // 2, width), BF),
             intos=((4, 2, rows, width), BF),
-            others=((3, 16, local), BF),
+            others=((6, 16, local), BF),
+            gm1=((4, rows, width), BF),
             parts=((width, 1280), BF),
             **reduce_scratch(1280),
         ),
-        dict(send=sems(104), recv=sems(104), **exchange),
+        dict(send=sems(104), recv=sems(104), s3=sems(6), r3=sems(6), **exchange),
     )
-    total, g_mlp, gains = b["total"], b["total_mlp"], b["gains"]
-    g_out = jnp.concatenate(
-        [total[n * 256 : (n + 1) * 256, 768:1024] for n in range(4)], 1
-    ).astype(F32)
-    side = total[:784, 1024:1280].astype(F32)
+    results = [
+        rows_wide[0],
+        rows_wide[0],
+        state_wide[0],
+        w_up.shape,
+        w_down.shape,
+        w.shape,
+        w_out.shape,
+        state_query.shape,
+        (heads * state_proj.shape[1], local),
+        (8, local),
+        (8, local),
+    ]
+    anywhere = pl.BlockSpec(memory_space=pl.ANY)
+    out, grad_x, state_after, g_up, g_down, g_qkv, g_out, g_query, g_proj, gains, others = (
+        pl.pallas_call(
+            finish_kernel,
+            out_shape=tuple(jax.ShapeDtypeStruct(shape, F32) for shape in results),
+            in_specs=[anywhere] * 5,
+            out_specs=tuple([anywhere] * 9 + [VMEM] * 2),
+            scratch_shapes=[
+                pltpu.VMEM((width, 3328), F32),
+                pltpu.VMEM((width, mlp_width), BF),
+                pltpu.VMEM((width, 1280), BF),
+                pltpu.VMEM((2,) + rows_wide[0], F32),
+                pltpu.VMEM(state_wide[0], F32),
+                sems(11),
+                sems(32),
+            ],
+            compiler_params=pltpu.CompilerParams(vmem_limit_bytes=LIMIT),
+            name="finish",
+        )(b["total"], b["total_mlp"], b["out"], b["grad_x"], f["state_after"])
+    )
     return (
-        b["out"],
-        b["grad_x"],
-        f["state_after"][:, None],
+        out,
+        grad_x,
+        state_after[:, None],
         gains[0:4].reshape(width),
         gains[4:8].reshape(width),
-        total[:, 0:768].astype(F32).reshape(width, 3, local),
+        jnp.transpose(g_qkv, (1, 0, 2)),
         g_out,
-        jnp.transpose(side[778:780, :buckets]),
-        side[:512],
-        side[512:768].reshape(state_proj.shape),
-        side[776],
-        side[777],
-        g_mlp[:, :1024].astype(F32),
-        g_mlp[:, 1024:].astype(F32),
+        jnp.transpose(others[2:4, :buckets]),
+        g_query,
+        g_proj.reshape(state_proj.shape),
+        others[0],
+        others[1],
+        g_up,
+        g_down,
     )
 
 

time: 309 us -> 259 us (0.84)
  Pallas kernels: 277 us -> 254 us
  local copies, waits for them, and re-layouts: 21.3 us -> 4.55 us
  other arithmetic: 9.44 us -> 0 us
    pallas_call x2, Pallas kernels: 277 us -> 244 us  [call(): pl.pallas_call(run, out_shape=tuple((jax.ShapeDtypeStruct(shape, kind) fo...]
    unnamed x17 -> x3, local copies, waits for them, and re-layouts: 12.2 us -> 1.97 us
    pallas_call x0 -> x1, Pallas kernels: none -> 9.67 us  [body(): pl.pallas_call(finish_kernel, out_shape=tuple((jax.ShapeDtypeStruct(shape...]
    convert_element_type x4 -> x0, other arithmetic: 8.55 us -> none  [the longest x1 6.75 us: body(): g_mlp[:, 1024:].astype(F32)]
    reshape x2 -> x0, local copies, waits for them, and re-layouts: 3.93 us -> none  [the longest x1 2.36 us: body(): total[:, 0:768].astype(F32).reshape(width, 3, local)]
where the time goes in v4:
time: 259 us
  Pallas kernels  254 us (98%)
  local copies, waits for them, and re-layouts  4.55 us (2%)
    pallas_call x2, Pallas kernels, call(): pl.pallas_call(run, out_shape=tuple((jax.ShapeDtypeStruct(shape, kind) fo...  244 us
    pallas_call x1, Pallas kernels, body(): pl.pallas_call(finish_kernel, out_shape=tuple((jax.ShapeDtypeStruct(shape...  9.67 us

profile of v4, /device:TPU:1, one launch (start us, length us, event | category | flops | bytes accessed | tf_op | source)
XLA Modules:
  0.0 259.2 jit_solution(2782199136328732545)
XLA Ops:
  0.6 136.2 %forward.1 = (f32[2,128,1024]{2,1,0:T(8,128)}, bf16[4,128,1024]{2,1,0:T(8,128)(2,1)}, bf16[2,16,2048]{2,1,0:T(8,128)(2,1)}, f32[1,1024]{1,0:T(1,128)}, bf16[2,4,...) custom-call(bf16[2,128,1024]{2,1,0:T(8,128)(2,1)} %refs_25_.1, ...), custom_call_target="tpu_custom_call" | custom-call | tf_op jit(solution)/shard_map/forward/pallas_call | solution.py:1191
  136.9 108.1 %backward.1 = (bf16[1024,2048]{1,0:T(8,128)(2,1)}, bf16[1024,1280]{1,0:T(8,128)(2,1)}, f32[2,128,1024]{2,1,0:T(8,128)}, f32[2,128,1024]{2,1,0:T(8,128)}) custom-call(bf16[4,128,1024]{2,1,0:T(8,128)(2,1)} %get-tuple-element.47.refs_0_, f32[2,128,1024]{2,1,0:T(8,128)} %get-tuple-element.48.refs_1_, bf16[256,1024]{1,0:T(8,128)(2,1)} %refs_2_.1, ...), custom_call_target="tpu_custom_call" | custom-call | tf_op jit(solution)/shard_map/backward/pallas_call | solution.py:1191
  245.0 9.7 %finish.1 = (f32[2,128,1024]{2,1,0:T(8,128)}, f32[2,128,1024]{2,1,0:T(8,128)}, f32[2,512,256]{2,1,0:T(8,128)}, f32[1024,1024]{1,0:T(8,128)}, f32[1024,1024]{1,0:...) custom-call(bf16[1024,1280]{1,0:T(8,128)(2,1)} %get-tuple-element.64, ...), custom_call_target="tpu_custom_call" | custom-call | tf_op jit(solution)/shard_map/finish/pallas_call | solution.py:1434
  254.7 1.2 slice_bitcast_fusion.2
  255.9 1.3 fusion
  257.2 0.8 slice_bitcast_fusion
  258.0 0.6 copy.30
  258.6 0.6 copy.29
